TPU v7x, 256 devices: a whole 4x4x8 slice. The times are simulated.
256 devices in a mesh: ep: 128 (over z, y, x), tp: 2 (over core).
Axes of the slice: x: 4, y: 4, z: 8, core: 2. Of those that a mesh axis runs over, the one named last changes fastest.
Arguments:
- tokens: bfloat16 [16384, 4096], P('ep', 'tp'), may hold values from -6 to 6
- expert_ids: int32 [16384, 8], P('ep'), may hold values from 0 to 127, all different within a row; in each aligned block of 128 rows (0 to 127, 128 to 255, ...) at most 12 rows name the same one
- gate_levels: int32 [16384, 8], P('ep'), may hold values from 32 to 255
- gate_weight: bfloat16 [128, 4096, 768], P('ep', None, 'tp'), may hold values from -0.09375 to 0.09375
- up_weight: bfloat16 [128, 4096, 768], P('ep', None, 'tp'), may hold values from -0.09375 to 0.09375
- down_weight: bfloat16 [128, 768, 4096], P('ep', 'tp'), may hold values from -0.21875 to 0.21875
Outputs:
- mixed: bfloat16 [16384, 4096], P('ep', 'tp')
Inputs may be any that keep to these rules, and one draw needn't show every extreme that they name: `expert_ids`: each token names 8 different experts. Among the 128 tokens of one aligned block, no expert is named by more than 12 tokens, and in some blocks one expert is named by exactly 12.
All inputs are finite; a program needn't handle non-finite values.
Results may differ from a plain program's by a relative error of at most 0.011.
Values may be sent and summed in bfloat16 or wider, within the bound.
No kernel may reach another device: no remote copies, remote signals or barrier semaphores. Data moves between devices by JAX's collectives and lax.ppermute only.
A program may use at most 128 MiB of HBM per device.

v0:
```python
import jax
import jax.numpy as jnp
from jax import lax
from jax.sharding import PartitionSpec as P


def hidden_units(row_block, w_gate, w_up):
    gate_values = jnp.dot(row_block, w_gate, preferred_element_type=jnp.float32)
    up_values = jnp.dot(row_block, w_up, preferred_element_type=jnp.float32)
    return (jax.nn.silu(gate_values) * up_values).astype(jnp.bfloat16)


def on_device(tokens, expert_ids, gate_levels, gate_weight, up_weight, down_weight):
    n_ep = lax.axis_size("ep")
    tok_count, top_count = expert_ids.shape
    half_width = tokens.shape[1]
    experts_all = gate_weight.shape[0] * n_ep
    capacity = 3 * tok_count * top_count // (2 * experts_all)
    route_ids = expert_ids.reshape(-1)
    routes = route_ids.shape[0]
    onehot = (route_ids[:, None] == jnp.arange(experts_all, dtype=jnp.int32)[None, :]).astype(
        jnp.int32
    )
    earlier = jnp.cumsum(onehot, axis=0) - onehot
    slot_rank = jnp.sum(earlier * onehot, axis=1)
    target = route_ids * capacity + slot_rank
    source_route = (
        jnp.full((experts_all * capacity,), routes, jnp.int32)
        .at[target]
        .set(jnp.arange(routes, dtype=jnp.int32))
    )
    padded_tokens = jnp.concatenate([tokens, jnp.zeros((1, half_width), tokens.dtype)], axis=0)
    outgoing = padded_tokens[source_route // top_count].reshape(n_ep, -1, half_width)
    filled = (source_route < routes).astype(jnp.int32)
    arrived, arrived_live = (
        lax.all_to_all(outgoing, "ep", split_axis=0, concat_axis=0, tiled=True),
        lax.all_to_all(filled.reshape(n_ep, -1), "ep", split_axis=0, concat_axis=0, tiled=True),
    )
    slots_all = arrived.shape[0] * arrived.shape[1]
    incoming = arrived.reshape(slots_all, half_width)
    w_gate = gate_weight[0]
    w_up = up_weight[0]
    w_down = down_weight[0]
    gathered = lax.all_gather(incoming, "tp", axis=1, tiled=True)
    hidden = hidden_units(gathered, w_gate, w_up)
    partial_sum = jnp.dot(hidden, w_down, preferred_element_type=jnp.float32)
    expert_out = lax.psum_scatter(
        partial_sum.astype(jnp.bfloat16), "tp", scatter_dimension=1, tiled=True
    )
    returned = lax.all_to_all(
        expert_out.reshape(n_ep, -1, half_width), "ep", split_axis=0, concat_axis=0, tiled=True
    )
    returned = returned.reshape(-1, half_width)
    levels = gate_levels.astype(jnp.float32)
    weights = levels / jnp.sum(levels, axis=1, keepdims=True)
    picked = returned[target].reshape(tok_count, top_count, half_width)
    mixed = jnp.einsum("tk,tkd->td", weights, picked.astype(jnp.float32))
    return mixed.astype(jnp.bfloat16)


def solution(mesh):
    in_specs = (
        P("ep", "tp"),
        P("ep", None),
        P("ep", None),
        P("ep", None, "tp"),
        P("ep", None, "tp"),
        P("ep", "tp", None),
    )
    out_specs = P("ep", "tp")
    return jax.shard_map(
        on_device, mesh=mesh, in_specs=in_specs, out_specs=out_specs, check_vma=False
    )
```

profile of v0, /device:TPU:1, one launch (start us, length us, event | category | flops | bytes accessed | tf_op | source)
XLA Modules:
  0.0 590.5 jit_solution(7452896200611473311)
XLA Ops:
  6.5 0.9 copy.8
  7.7 0.7 broadcast_multiply_fusion
  8.7 0.8 copy-done.2
  9.5 1.1 broadcast_add_fusion
  10.6 0.9 copy.11
  11.7 1.4 fusion.13
  13.1 4.3 scatter_custom_fusion
  17.4 1.9 concatenate.3
  19.3 13.8 %gather_fusion = bf16[1536,2048]{1,0:T(8,128)(2,1)} fusion(bf16[129,2048]{1,0:T(8,128)(2,1)} %concatenate.3, s32[2048]{0:T(1024)S(1)} %pad_clamp_fusion), kind=kCustom, calls=%fused_computation | custom fusion | bytes 12589056 | tf_op jit(solution)/shard_map/gather | solution.py:33
  33.1 10.6 %reshape.63 = bf16[128,12,2048]{2,1,0:T(8,128)(2,1)} reshape(bf16[1536,2048]{1,0:T(8,128)(2,1)} %gather_fusion) | data formatting | bytes 12582912 | tf_op jit(solution)/shard_map/reshape | solution.py:33
  43.7 200.0 %all_to_all.10 = bf16[128,12,2048]{2,1,0:T(8,128)(2,1)} all-to-all(bf16[128,12,2048]{2,1,0:T(8,128)(2,1)} %reshape.63), channel_id=1, replica_groups=mesh['ep'=128,'tp'=2] {'ep'}, dimensions={0} | all-to-all | bytes 12582912 | tf_op jit(solution)/shard_map/all_to_all | solution.py:36
  243.7 10.7 %reshape.64 = bf16[1536,2048]{1,0:T(8,128)(2,1)} reshape(bf16[128,12,2048]{2,1,0:T(8,128)(2,1)} %all_to_all.10) | data formatting | bytes 12582912 | tf_op jit(solution)/shard_map/reshape | solution.py:40
  254.5 0.2 reduce-scatter.2.cloned.1.call-start
  254.7 29.4 %all-gather.2.cloned.1.call-done = bf16[1536,4096]{1,0:T(8,128)(2,1)} async-done(((bf16[1536,2048]{1,0:T(8,128)(2,1)}), bf16[1536,4096]{1,0:T(8,128)(2,1)}) %all-gather.2.cloned.1.call-update) | async-done | bytes 12582928 | tf_op jit(solution)/shard_map/all_gather | solution.py:44
  284.1 11.5 %fusion.4 = f32[1536,384]{1,0:T(8,128)} fusion(bf16[1536,4096]{1,0:T(8,128)(2,1)} %all-gather.2.cloned.1.call-done, bf16[1,4096,384]{2,1,0:T(8,128)(2,1)} %param.9), kind=kOutput, calls=%fused_computation.9 | convolution fusion | flops 4831838208 | bytes 18087936 | tf_op jit(solution)/shard_map/dot_general | solution.py:8
  295.6 20.0 %convolution_convert_fusion = bf16[1536,4096]{1,0:T(8,128)(2,1)} fusion(bf16[1,384,4096]{2,1,0:T(8,128)(2,1)S(1)} %copy-done, bf16[1536,4096]{1,0:T(8,128)(2,1)} %all-gather.2.cloned.1.call-done, bf16[1,4096,384]{2,1,0:T(8,128)(2,1)} %param.10, f32[1536,384]{1,0:T(8,128)} %fusion.4), kind=kOutput, calls=%fused_computation.3 | convolution fusion | flops 9673506816 | bytes 33816576 | tf_op jit(solution)/shard_map/dot_general | solution.py:46
  315.7 28.1 %reduce-scatter.2.cloned.1.call-done = bf16[1536,2048]{1,0:T(8,128)(2,1)} async-done(((bf16[1536,4096]{1,0:T(8,128)(2,1)}), bf16[1536,2048]{1,0:T(8,128)(2,1)}) %reduce-scatter.2.cloned.1.call-update) | async-done | bytes 6291472 | tf_op jit(solution)/shard_map/reduce_scatter | solution.py:47
  343.7 10.6 %reshape.65 = bf16[128,12,2048]{2,1,0:T(8,128)(2,1)} reshape(bf16[1536,2048]{1,0:T(8,128)(2,1)} %reduce-scatter.2.cloned.1.call-done) | data formatting | bytes 12582912 | tf_op jit(solution)/shard_map/reshape | solution.py:51
  354.3 14.5 %all-to-all-start.1 = ((bf16[128,12,2048]{2,1,0:T(8,128)(2,1)}), bf16[128,12,2048]{2,1,0:T(8,128)(2,1)}, u32[]{:S(2)}, u32[]{:S(2)}) async-start(bf16[128,12,2048]{2,1,0:T(8,128)(2,1)} %reshape.65), calls=%async_computation.2 | async-start | bytes 16777216 | tf_op jit(solution)/shard_map/all_to_all | solution.py:50
  368.9 186.9 %all-to-all-done.1 = bf16[128,12,2048]{2,1,0:T(8,128)(2,1)} async-done(((bf16[128,12,2048]{2,1,0:T(8,128)(2,1)}), bf16[128,12,2048]{2,1,0:T(8,128)(2,1)}, u32[]{:S(2)}, u32[]{:S(2)}) %all-to-all-start.1) | async-done | bytes 6291488 | tf_op jit(solution)/shard_map/all_to_all | solution.py:50
  555.9 10.7 %reshape.66 = bf16[1536,2048]{1,0:T(8,128)(2,1)} reshape(bf16[128,12,2048]{2,1,0:T(8,128)(2,1)} %all-to-all-done.1) | data formatting | bytes 12582912 | tf_op jit(solution)/shard_map/reshape | solution.py:53
  566.6 12.6 %gather_fusion.1 = bf16[1024,2048]{1,0:T(8,128)(2,1)} fusion(bf16[1536,2048]{1,0:T(8,128)(2,1)} %reshape.66, s32[1024]{0:T(1024)S(1)} %broadcast_clamp_fusion), kind=kCustom, calls=%fused_computation.1 | custom fusion | bytes 8392704 | tf_op jit(solution)/shard_map/gather | solution.py:56
  579.1 3.4 fusion
  582.6 1.1 copy.15
  (27 shorter events, 1.0 us)
Async XLA Ops:
  6.5 289.1 %copy-start = (bf16[1,384,4096]{2,1,0:T(8,128)(2,1)S(1)}, bf16[1,384,4096]{2,1,0:T(8,128)(2,1)}, u32[]{:S(2)}) copy-start(bf16[1,384,4096]{2,1,0:T(8,128)(2,1)} %param.11) | copy-start | bytes 9437188
  6.5 277.6 %all-gather.2.cloned.1.call-start = ((), (), s32[]{:S(2)}) async-start(), calls=%async_computation.3 | async-start | bytes 18874368 | tf_op jit(solution)/shard_map/all_gather | solution.py:44
  8.7 0.8 copy-start.2
  254.5 89.3 %reduce-scatter.2.cloned.1.call-start = ((), (), s32[]{:S(2)}) async-start(), calls=%async_computation.4 | async-start | bytes 18874368 | tf_op jit(solution)/shard_map/reduce_scatter | solution.py:47
  354.3 14.5 %copy-start.3 = (s32[128,8]{0,1:T(8,128)S(1)}, s32[128,8]{0,1:T(8,128)}, u32[]{:S(2)}) copy-start(s32[128,8]{0,1:T(8,128)} %param.8) | copy-start | bytes 12292
  354.3 201.6 %all-to-all-start.1 = ((bf16[128,12,2048]{2,1,0:T(8,128)(2,1)}), bf16[128,12,2048]{2,1,0:T(8,128)(2,1)}, u32[]{:S(2)}, u32[]{:S(2)}) async-start(bf16[128,12,2048]{2,1,0:T(8,128)(2,1)} %reshape.65), calls=%async_computation.2 | async-start | bytes 16777216 | tf_op jit(solution)/shard_map/all_to_all | solution.py:50
  566.6 17.1 %copy-start.1 = (bf16[1,384,4096]{2,1,0:T(8,128)(2,1)S(1)}, bf16[1,384,4096]{2,1,0:T(8,128)(2,1)}, u32[]{:S(2)}) copy-start(bf16[1,384,4096]{2,1,0:T(8,128)(2,1)} %param.11) | copy-start | bytes 9437188
Sparse Core Ops, SparseCore 0:
  254.6 29.4 all-gather.1
  315.8 27.8 reduce-scatter.1
where the time goes:
time: 592 us; the launch traced here: 591 us
  waiting for transfers between devices  244 us (41%)
  blocking collectives  200 us (34%)
  local copies, waits for them, and re-layouts  79.5 us (13%)
  matrix products  35 us (6%)
  starting transfers between devices  14.7 us (2%)
  between operations  13.5 us (2%)
    all_to_all x1, blocking collectives, on_device(): lax.all_to_all(outgoing, 'ep', split_axis=0, concat_axis=0, tiled=True)  200 us
    all_to_all x1, waiting for transfers between devices, on_device(): lax.all_to_all(expert_out.reshape(n_ep, -1, half_width), 'ep', split_axis...  187 us
    all_gather x1, waiting for transfers between devices, on_device(): gathered = lax.all_gather(incoming, 'tp', axis=1, tiled=True)  29.4 us
    reduce_scatter x1, waiting for transfers between devices, on_device(): lax.psum_scatter(partial_sum.astype(jnp.bfloat16), 'tp', scatter_dimensio...  28.1 us
    dot_general x1, matrix products, on_device(): partial_sum = jnp.dot(hidden, w_down, preferred_element_type=jnp.float32)  20 us
    all_to_all x1, starting transfers between devices, on_device(): lax.all_to_all(expert_out.reshape(n_ep, -1, half_width), 'ep', split_axis...  14.5 us
    gather x1, local copies, waits for them, and re-layouts, on_device(): padded_tokens[source_route // top_count].reshape(n_ep, -1, half_width)  13.8 us
    gather x1, local copies, waits for them, and re-layouts, on_device(): picked = returned[target].reshape(tok_count, top_count, half_width)  12.6 us
  transfers between devices with their start and end apart: 3, of which 3 were waited for; matrix products, arithmetic and copies ran while one was open for 0% of the time, Pallas kernels for 0%

commit v1 on v0

v1 whole, which is shorter than its diff:
```python
import jax
import jax.numpy as jnp
from jax import lax
from jax.sharding import Mesh, PartitionSpec as P

PLANE = (4, 4)
CHUNKS = 2
SWAP = [(0, 1), (1, 0)]


def swap(array):
    return lax.ppermute(array, "tp", SWAP)


def on_device(tokens, expert_ids, gate_levels, gate_weight, up_weight, down_weight):
    planes = lax.axis_size("z")
    plane_experts = lax.axis_size("y") * lax.axis_size("x")
    core = lax.axis_index("tp")
    tok_count, top_count = expert_ids.shape
    half_width = tokens.shape[1]
    experts_all = planes * plane_experts
    capacity = 3 * tok_count * top_count // (2 * experts_all)
    blocks = planes // 2
    my_tokens = blocks * tok_count
    my_slots = blocks * capacity
    width = half_width // CHUNKS

    meta = lax.all_gather(
        jnp.concatenate([expert_ids, gate_levels], axis=1), "z", axis=0, tiled=True
    )
    mine = lax.dynamic_slice_in_dim(meta, core * my_tokens, my_tokens, 0)
    ids, levels = mine[:, :top_count], mine[:, top_count:].astype(jnp.float32)
    weights = levels / jnp.sum(levels, axis=1, keepdims=True)
    first = lax.axis_index("z") * plane_experts
    plane_ids = first + jnp.arange(plane_experts, dtype=jnp.int32)
    hits = ids[None, :, :] == plane_ids[:, None, None]
    named = jnp.any(hits, axis=2)
    scale = jnp.sum(jnp.where(hits, weights[None, :, :], 0.0), axis=2)
    order = jnp.arange(tok_count)
    before = (order[:, None] < order[None, :]).astype(jnp.bfloat16)
    rank = jnp.einsum(
        "ebt,ts->ebs",
        named.reshape(plane_experts, blocks, tok_count).astype(jnp.bfloat16),
        before,
        preferred_element_type=jnp.float32,
    ).astype(jnp.int32)
    place = rank + capacity * jnp.arange(blocks, dtype=jnp.int32)[None, :, None]
    place = jnp.where(named, place.reshape(plane_experts, my_tokens), -1)
    fits = place[:, None, :] == jnp.arange(my_slots, dtype=jnp.int32)[None, :, None]
    rows = plane_experts * my_slots
    select = fits.astype(jnp.bfloat16).reshape(rows, my_tokens)
    mix = jnp.where(fits, scale[:, None, :], 0.0).astype(jnp.bfloat16).reshape(rows, my_tokens)

    w_gate = jnp.concatenate([gate_weight[0], swap(gate_weight[0])], axis=1)
    w_up = jnp.concatenate([up_weight[0], swap(up_weight[0])], axis=1)
    w_down = jnp.concatenate([down_weight[0], swap(down_weight[0])], axis=0)

    def both(array, index, axis):
        own = core * half_width + index * width
        other = (1 - core) * half_width + index * width
        return jnp.concatenate(
            [
                lax.dynamic_slice_in_dim(array, own, width, axis),
                lax.dynamic_slice_in_dim(array, other, width, axis),
            ],
            axis=axis,
        )

    gate_values = up_values = 0.0
    for index in range(CHUNKS):
        piece = tokens[:, index * width : (index + 1) * width]
        column = lax.all_gather(piece, "z", axis=0, tiled=True)
        keep = lax.dynamic_slice_in_dim(column, core * my_tokens, my_tokens, 0)
        give = lax.dynamic_slice_in_dim(column, (1 - core) * my_tokens, my_tokens, 0)
        features = jnp.concatenate([keep, swap(give)], axis=1)
        outgoing = jnp.dot(select, features, preferred_element_type=jnp.float32)
        outgoing = outgoing.astype(jnp.bfloat16).reshape(plane_experts, my_slots, 2 * width)
        arrived = lax.all_to_all(outgoing, ("y", "x"), split_axis=0, concat_axis=0, tiled=True)
        arrived = arrived.reshape(rows, 2 * width)
        gate_values += jnp.dot(
            arrived, both(w_gate, index, 0), preferred_element_type=jnp.float32
        )
        up_values += jnp.dot(arrived, both(w_up, index, 0), preferred_element_type=jnp.float32)
    hidden = (jax.nn.silu(gate_values) * up_values).astype(jnp.bfloat16)

    outputs = []
    for index in range(CHUNKS):
        produced = jnp.dot(hidden, both(w_down, index, 1), preferred_element_type=jnp.float32)
        produced = produced.astype(jnp.bfloat16).reshape(plane_experts, my_slots, 2 * width)
        returned = lax.all_to_all(produced, ("y", "x"), split_axis=0, concat_axis=0, tiled=True)
        returned = returned.reshape(rows, 2 * width)
        partial = lax.dot_general(
            mix, returned, (((0,), (0,)), ((), ())), preferred_element_type=jnp.float32
        ).astype(jnp.bfloat16)
        own, other = partial[:, :width], swap(partial[:, width:])
        column = jnp.concatenate(
            [jnp.where(core == 0, own, other), jnp.where(core == 0, other, own)], axis=0
        )
        outputs.append(lax.psum_scatter(column, "z", scatter_dimension=0, tiled=True))
    return jnp.concatenate(outputs, axis=1)


def solution(mesh):
    n_ep, n_tp = mesh.shape["ep"], mesh.shape["tp"]
    n_y, n_x = PLANE
    torus = Mesh(
        mesh.devices.reshape(n_ep // (n_y * n_x), n_y, n_x, n_tp), ("z", "y", "x", "tp")
    )
    ep = ("z", "y", "x")
    in_specs = (
        P(ep, "tp"),
        P(ep, None),
        P(ep, None),
        P(ep, None, "tp"),
        P(ep, None, "tp"),
        P(ep, "tp", None),
    )
    return jax.shard_map(
        on_device, mesh=torus, in_specs=in_specs, out_specs=P(ep, "tp"), check_vma=False
    )
```

time: 592 us -> 358 us (0.60)
  blocking collectives: 200 us -> 19 us
  local copies, waits for them, and re-layouts: 79.5 us -> 8.72 us
  waiting for transfers between devices: 244 us -> 210 us
  starting transfers between devices: 14.7 us -> 44.4 us
  other arithmetic: 3.46 us -> 19.3 us
    all_to_all x1 -> x0, blocking collectives: 200 us -> none  [on_device(): lax.all_to_all(outgoing, 'ep', split_axis=0, concat_axis=0, tiled=True)]
    all_to_all x1 -> x4, waiting for transfers between devices: 187 us -> 127 us  [the longest x2 91.2 us: on_device(): lax.all_to_all(produced, ('y', 'x'), split_axis=0, concat_axis=0, tiled=T...]
    reshape x4 -> x0, local copies, waits for them, and re-layouts: 42.6 us -> none  [the longest x1 10.7 us: on_device(): returned = returned.reshape(-1, half_width)]
    gather x2 -> x0, local copies, waits for them, and re-layouts: 26.4 us -> none  [the longest x1 13.8 us: on_device(): padded_tokens[source_route // top_count].reshape(n_ep, -1, half_width)]
    all_gather x0 -> x1, blocking collectives: none -> 19 us  [on_device(): lax.all_gather(jnp.concatenate([expert_ids, gate_levels], axis=1), 'z', a...]
    concatenate x0 -> x7, other arithmetic: none -> 16.8 us  [the longest x1 4.36 us: on_device(): w_gate = jnp.concatenate([gate_weight[0], swap(gate_weight[0])], axis=1)]
    ppermute x0 -> x7, starting transfers between devices: none -> 16.2 us  [swap(): return lax.ppermute(array, 'tp', SWAP)]
    all_to_all x1 -> x4, starting transfers between devices: 14.5 us -> 28.1 us  [the longest x2 15.7 us: on_device(): lax.all_to_all(outgoing, ('y', 'x'), split_axis=0, concat_axis=0, tiled=T...]
  transfers between devices with their start and end apart: 3 -> 15, of which waited for: 3 -> 8; matrix products, arithmetic and copies ran while one was open for 0% -> 12% of each run, Pallas kernels for 0% -> 0%
where the time goes in v1:
time: 358 us; the launch traced here: 354 us
  waiting for transfers between devices  210 us (59%)
  starting transfers between devices  44.4 us (12%)
  matrix products  38.9 us (11%)
  other arithmetic  19.3 us (5%)
  blocking collectives  19 us (5%)
  between operations  13.5 us (4%)
  local copies, waits for them, and re-layouts  8.72 us (2%)
    all_to_all x2, waiting for transfers between devices, on_device(): lax.all_to_all(produced, ('y', 'x'), split_axis=0, concat_axis=0, tiled=T...  91.2 us
    all_gather x2, waiting for transfers between devices, on_device(): column = lax.all_gather(piece, 'z', axis=0, tiled=True)  41.2 us
    all_to_all x2, waiting for transfers between devices, on_device(): lax.all_to_all(outgoing, ('y', 'x'), split_axis=0, concat_axis=0, tiled=T...  35.8 us
    reduce_scatter x2, waiting for transfers between devices, on_device(): lax.psum_scatter(column, 'z', scatter_dimension=0, tiled=True)  35.1 us
    all_gather x1, blocking collectives, on_device(): lax.all_gather(jnp.concatenate([expert_ids, gate_levels], axis=1), 'z', a...  19 us
    ppermute x7, starting transfers between devices, swap(): return lax.ppermute(array, 'tp', SWAP)  16.2 us
    all_to_all x2, starting transfers between devices, on_device(): lax.all_to_all(outgoing, ('y', 'x'), split_axis=0, concat_axis=0, tiled=T...  15.7 us
    all_to_all x2, starting transfers between devices, on_device(): lax.all_to_all(produced, ('y', 'x'), split_axis=0, concat_axis=0, tiled=T...  12.4 us
  transfers between devices with their start and end apart: 15, of which 8 were waited for; matrix products, arithmetic and copies ran while one was open for 12% of the time, Pallas kernels for 0%

profile of v1, /device:TPU:1, one launch (start us, length us, event | category | flops | bytes accessed | tf_op | source)
XLA Modules:
  0.0 354.0 jit_solution(6902406094971089305)
XLA Ops:
  9.2 41.2 %all-gather.5.cloned.1.call-done = bf16[1024,1024]{1,0:T(8,128)(2,1)} async-done(((bf16[128,1024]{1,0:T(8,128)(2,1)}), bf16[1024,1024]{1,0:T(8,128)(2,1)}) %all-gather.5.cloned.1.call-update) | async-done | bytes 2097168 | tf_op jit(solution)/shard_map/all_gather | solution.py:72
  52.1 4.5 %collective-permute-start.2 = (bf16[512,1024]{1,0:T(8,128)(2,1)S(1)}, bf16[512,1024]{1,0:T(8,128)(2,1)}, u32[]{:S(2)}, u32[]{:S(2)}) collective-permute-start(bf16[512,1024]{1,0:T(8,128)(2,1)S(1)} %get-tuple-element.24), channel_id=1, source_target_pairs={{0,1},{1,0},{2,3},{3,2},{4,5},{5,4},{6,7},{7,6},{8,9},{9,8},{10,11... | collective-permute-start | bytes 3145736 | tf_op jit(solution)/shard_map/ppermute | solution.py:12
  56.7 19.0 %all_gather.9 = s32[1024,16]{0,1:T(8,128)S(1)} all-gather(s32[128,16]{0,1:T(8,128)S(1)} %pad_add_fusion), channel_id=1, replica_groups=mesh['z'=8,'y'=4,'x'=4,'tp'=2] {'z'}, dimensions={0}, use_global_device_ids=true | all-gather | bytes 73728 | tf_op jit(solution)/shard_map/all_gather | solution.py:28
  76.7 4.7 %convolution_convert_fusion.2 = bf16[768,2048]{1,0:T(8,128)(2,1)} fusion(pred[768,512]{1,0:T(32,128)(4,1)S(1)} %bitcast_compare_fusion, bf16[512,1024]{1,0:T(8,128)(2,1)} %collective-permute-done.2, bf16[512,1024]{1,0:T(8,128)(2,1)S(1)} %get-tuple-element.23), kind=kOutput, calls=%fused_computation.28 | convolution fusion | flops 1616379904 | bytes 5636096 | tf_op jit(solution)/shard_map/dot_general | solution.py:76
  81.4 6.5 %all-to-all-start.1 = ((bf16[16,48,2048]{2,1,0:T(8,128)(2,1)}), bf16[16,48,2048]{2,1,0:T(8,128)(2,1)S(1)}, u32[]{:S(2)}, u32[]{:S(2)}) async-start(bf16[16,48,2048]{2,1,0:T(8,128)(2,1)} %bitcast.42), calls=%async_computation.1 | async-start | bytes 6291456 | tf_op jit(solution)/shard_map/all_to_all | solution.py:78
  87.9 5.9 %collective-permute-start.1 = (bf16[4096,384]{1,0:T(8,128)(2,1)}, bf16[4096,384]{1,0:T(8,128)(2,1)}, u32[]{:S(2)}, u32[]{:S(2)}) collective-permute-start(bf16[4096,384]{1,0:T(8,128)(2,1)} %bitcast.45), channel_id=1, source_target_pairs={{0,1},{1,0},{2,3},{3,2},{4,5},{5,4},{6,7},{7,6},{8,9},{9,8},{10,11... | collective-permute-start | bytes 9437192 | tf_op jit(solution)/shard_map/ppermute | solution.py:12
  98.2 3.9 %collective-permute-done = bf16[512,1024]{1,0:T(8,128)(2,1)S(1)} collective-permute-done((bf16[512,1024]{1,0:T(8,128)(2,1)S(1)}, bf16[512,1024]{1,0:T(8,128)(2,1)S(1)}, u32[]{:S(2)}, u32[]{:S(2)}) %collective-permute-start) | collective-permute-done | bytes 1048608 | tf_op jit(solution)/shard_map/ppermute | solution.py:12
  102.2 3.5 convolution_convert_fusion.3
  105.7 18.1 %all-to-all-done.1 = bf16[16,48,2048]{2,1,0:T(8,128)(2,1)S(1)} async-done(((bf16[16,48,2048]{2,1,0:T(8,128)(2,1)}), bf16[16,48,2048]{2,1,0:T(8,128)(2,1)S(1)}, u32[]{:S(2)}, u32[]{:S(2)}) %all-to-all-start.1) | async-done | bytes 3145760 | tf_op jit(solution)/shard_map/all_to_all | solution.py:78
  123.8 9.1 %all-to-all-start = ((bf16[16,48,2048]{2,1,0:T(8,128)(2,1)}), bf16[16,48,2048]{2,1,0:T(8,128)(2,1)}, u32[]{:S(2)}, u32[]{:S(2)}) async-start(bf16[16,48,2048]{2,1,0:T(8,128)(2,1)} %bitcast.41), calls=%async_computation | async-start | bytes 6291456 | tf_op jit(solution)/shard_map/all_to_all | solution.py:78
  132.9 4.4 %fusion.39 = (bf16[1024,768]{1,0:T(8,128)(2,1)S(1)}, bf16[1024,768]{1,0:T(8,128)(2,1)}, bf16[1024,768]{1,0:T(8,128)(2,1)}, bf16[1024,768]{1,0:T(8,128)(2,1)S(1)}) fusion(s32[]{:T(128)S(6)} %select_n.73, bf16[4096,384]{1,0:T(8,128)(2,1)} %bitcast.46, bf16[4096,384]{1,0:T(8,128)(2,1)} %collective-permute-done.1, s32[]{:T(128)S(6)} %select_n.71, ...), kind=kLoop, calls=%fused_computation.72 | loop fusion | flops 12582912 | bytes 12582928 | tf_op jit(solution)/shard_map/concatenate | solution.py:54
  141.1 4.1 %fusion.29 = (bf16[768,1024]{1,0:T(8,128)(2,1)}, bf16[768,1024]{1,0:T(8,128)(2,1)}, bf16[768,1024]{1,0:T(8,128)(2,1)}, bf16[768,1024]{1,0:T(8,128)(2,1)}) fusion(s32[]{:T(128)S(6)} %select_n.71, bf16[384,4096]{1,0:T(8,128)(2,1)S(1)} %bitcast.50, bf16[384,4096]{1,0:T(8,128)(2,1)} %collective-permute-done.4, s32[]{:T(128)S(6)} %select_n.72, s32[]{:T(128)S(6)} %select_n.73, ...), kind=kLoop, calls=%fused_computation.62 | loop fusion | flops 12582912 | bytes 12582928 | tf_op jit(solution)/shard_map/concatenate | solution.py:56
  145.3 4.0 %fusion.4 = f32[768,768]{1,0:T(8,128)} fusion(bf16[768,2048]{1,0:T(8,128)(2,1)S(1)} %bitcast.39, bf16[1024,768]{1,0:T(8,128)(2,1)S(1)} %get-tuple-element.16, bf16[1024,768]{1,0:T(8,128)(2,1)S(1)} %get-tuple-element.13), kind=kOutput, calls=%fused_computation.34 | convolution fusion | flops 2422210560 | bytes 8650752 | tf_op jit(solution)/shard_map/dot_general | solution.py:80
  149.2 4.0 %fusion.12 = f32[768,768]{1,0:T(8,128)} fusion(bf16[768,2048]{1,0:T(8,128)(2,1)S(1)} %bitcast.40, bf16[1024,768]{1,0:T(8,128)(2,1)S(1)} %get-tuple-element.12, bf16[1024,768]{1,0:T(8,128)(2,1)S(1)} %get-tuple-element.11), kind=kOutput, calls=%fused_computation.42 | convolution fusion | flops 2422210560 | bytes 8650752 | tf_op jit(solution)/shard_map/dot_general | solution.py:83
  153.3 17.7 %all-to-all-done = bf16[16,48,2048]{2,1,0:T(8,128)(2,1)} async-done(((bf16[16,48,2048]{2,1,0:T(8,128)(2,1)}), bf16[16,48,2048]{2,1,0:T(8,128)(2,1)}, u32[]{:S(2)}, u32[]{:S(2)}) %all-to-all-start) | async-done | bytes 3145760 | tf_op jit(solution)/shard_map/all_to_all | solution.py:78
  171.0 5.6 %fusion = f32[768,768]{1,0:T(8,128)S(1)} fusion(bf16[768,2048]{1,0:T(8,128)(2,1)} %bitcast.3, bf16[1024,768]{1,0:T(8,128)(2,1)} %get-tuple-element.15, bf16[1024,768]{1,0:T(8,128)(2,1)} %get-tuple-element.14), kind=kOutput, calls=%fused_computation.30 | convolution fusion | flops 2422210560 | bytes 8650752 | tf_op jit(solution)/shard_map/dot_general | solution.py:80
  176.6 5.0 %multiply_convert_fusion = bf16[768,768]{1,0:T(8,128)(2,1)S(1)} fusion(f32[768,768]{1,0:T(8,128)S(1)} %copy-done.18, f32[768,768]{1,0:T(8,128)S(1)} %fusion, f32[768,768]{1,0:T(8,128)S(1)} %copy-done.17, bf16[768,2048]{1,0:T(8,128)(2,1)} %bitcast.3, bf16[1024,768]{1,0:T(8,128)(2,1)S(1)} %copy-done.6, bf16[1024,768]{1,0:T(8,128)(2,1)S(1)} %copy-done.5), kind=kOutput, calls=%fused_computation.52 | convolution fusion | flops 2426929152 | bytes 14548992 | tf_op jit(solution)/shard_map/dot_general | solution.py:83
  181.7 4.2 %convolution_convert_fusion.1 = bf16[768,2048]{1,0:T(8,128)(2,1)} fusion(bf16[768,768]{1,0:T(8,128)(2,1)S(1)} %multiply_convert_fusion, bf16[768,1024]{1,0:T(8,128)(2,1)S(1)} %copy-done.8, bf16[768,1024]{1,0:T(8,128)(2,1)S(1)} %copy-done.7), kind=kOutput, calls=%fused_computation.27 | convolution fusion | flops 2423783424 | bytes 7471104 | tf_op jit(solution)/shard_map/dot_general | solution.py:88
  185.9 8.7 %all-to-all-start.2 = ((bf16[16,48,2048]{2,1,0:T(8,128)(2,1)}), bf16[16,48,2048]{2,1,0:T(8,128)(2,1)S(1)}, u32[]{:S(2)}, u32[]{:S(2)}) async-start(bf16[16,48,2048]{2,1,0:T(8,128)(2,1)} %bitcast.44), calls=%async_computation.2 | async-start | bytes 6291456 | tf_op jit(solution)/shard_map/all_to_all | solution.py:90
  194.7 45.4 %all-to-all-done.2 = bf16[16,48,2048]{2,1,0:T(8,128)(2,1)S(1)} async-done(((bf16[16,48,2048]{2,1,0:T(8,128)(2,1)}), bf16[16,48,2048]{2,1,0:T(8,128)(2,1)S(1)}, u32[]{:S(2)}, u32[]{:S(2)}) %all-to-all-start.2) | async-done | bytes 3145760 | tf_op jit(solution)/shard_map/all_to_all | solution.py:90
  246.7 4.2 %convolution_convert_fusion = bf16[768,2048]{1,0:T(8,128)(2,1)} fusion(bf16[768,768]{1,0:T(8,128)(2,1)S(1)} %copy-done.20, bf16[768,1024]{1,0:T(8,128)(2,1)S(1)} %copy-done.4, bf16[768,1024]{1,0:T(8,128)(2,1)S(1)} %copy-done.3), kind=kOutput, calls=%fused_computation.26 | convolution fusion | flops 2423783424 | bytes 7471104 | tf_op jit(solution)/shard_map/dot_general | solution.py:88
  250.8 3.7 %all-to-all-start.3 = ((bf16[16,48,2048]{2,1,0:T(8,128)(2,1)}), bf16[16,48,2048]{2,1,0:T(8,128)(2,1)S(1)}, u32[]{:S(2)}, u32[]{:S(2)}) async-start(bf16[16,48,2048]{2,1,0:T(8,128)(2,1)} %bitcast.43), calls=%async_computation.4 | async-start | bytes 6291456 | tf_op jit(solution)/shard_map/all_to_all | solution.py:90
  257.9 45.8 %all-to-all-done.3 = bf16[16,48,2048]{2,1,0:T(8,128)(2,1)S(1)} async-done(((bf16[16,48,2048]{2,1,0:T(8,128)(2,1)}), bf16[16,48,2048]{2,1,0:T(8,128)(2,1)S(1)}, u32[]{:S(2)}, u32[]{:S(2)}) %all-to-all-start.3) | async-done | bytes 3145760 | tf_op jit(solution)/shard_map/all_to_all | solution.py:90
  310.6 35.1 %reduce-scatter.5.cloned.1.call-done = bf16[128,1024]{1,0:T(8,128)(2,1)} async-done(((bf16[1024,1024]{1,0:T(8,128)(2,1)}), bf16[128,1024]{1,0:T(8,128)(2,1)}) %reduce-scatter.5.cloned.1.call-update) | async-done | bytes 262160 | tf_op jit(solution)/shard_map/reduce_scatter | solution.py:99
  (89 shorter events, 32.2 us)
Async XLA Ops:
  6.5 50.1 %copy-start.13 = (s32[128,8]{0,1:T(8,128)S(1)}, s32[128,8]{0,1:T(8,128)}, u32[]{:S(2)}) copy-start(s32[128,8]{0,1:T(8,128)} %param.8) | copy-start | bytes 12292
  6.5 50.1 %copy-start.14 = (s32[128,8]{0,1:T(8,128)S(1)}, s32[128,8]{0,1:T(8,128)}, u32[]{:S(2)}) copy-start(s32[128,8]{0,1:T(8,128)} %param.7) | copy-start | bytes 12292
  6.5 43.8 %all-gather.5.cloned.1.call-start = ((), (), s32[]{:S(2)}) async-start(), calls=%async_computation.7 | async-start | bytes 2359296 | tf_op jit(solution)/shard_map/all_gather | solution.py:72
  8.4 86.0 %all-gather.3.cloned.1.call-start = ((), (), s32[]{:S(2)}) async-start(), calls=%async_computation.6 | async-start | bytes 2359296 | tf_op jit(solution)/shard_map/all_gather | solution.py:72
  52.1 24.6 %collective-permute-start.2 = (bf16[512,1024]{1,0:T(8,128)(2,1)S(1)}, bf16[512,1024]{1,0:T(8,128)(2,1)}, u32[]{:S(2)}, u32[]{:S(2)}) collective-permute-start(bf16[512,1024]{1,0:T(8,128)(2,1)S(1)} %get-tuple-element.24), channel_id=1, source_target_pairs={{0,1},{1,0},{2,3},{3,2},{4,5},{5,4},{6,7},{7,6},{8,9},{9,8},{10,11... | collective-permute-start | bytes 3145736 | tf_op jit(solution)/shard_map/ppermute | solution.py:12
  81.4 42.4 %all-to-all-start.1 = ((bf16[16,48,2048]{2,1,0:T(8,128)(2,1)}), bf16[16,48,2048]{2,1,0:T(8,128)(2,1)S(1)}, u32[]{:S(2)}, u32[]{:S(2)}) async-start(bf16[16,48,2048]{2,1,0:T(8,128)(2,1)} %bitcast.42), calls=%async_computation.1 | async-start | bytes 6291456 | tf_op jit(solution)/shard_map/all_to_all | solution.py:78
  87.9 45.0 %collective-permute-start.1 = (bf16[4096,384]{1,0:T(8,128)(2,1)}, bf16[4096,384]{1,0:T(8,128)(2,1)}, u32[]{:S(2)}, u32[]{:S(2)}) collective-permute-start(bf16[4096,384]{1,0:T(8,128)(2,1)} %bitcast.45), channel_id=1, source_target_pairs={{0,1},{1,0},{2,3},{3,2},{4,5},{5,4},{6,7},{7,6},{8,9},{9,8},{10,11... | collective-permute-start | bytes 9437192 | tf_op jit(solution)/shard_map/ppermute | solution.py:12
  93.9 43.4 %collective-permute-start.3 = (bf16[4096,384]{1,0:T(8,128)(2,1)}, bf16[4096,384]{1,0:T(8,128)(2,1)}, u32[]{:S(2)}, u32[]{:S(2)}) collective-permute-start(bf16[4096,384]{1,0:T(8,128)(2,1)} %bitcast.47), channel_id=1, source_target_pairs={{0,1},{1,0},{2,3},{3,2},{4,5},{5,4},{6,7},{7,6},{8,9},{9,8},{10,11... | collective-permute-start | bytes 9437192 | tf_op jit(solution)/shard_map/ppermute | solution.py:12
  94.0 47.1 %collective-permute-start.4 = (bf16[384,4096]{1,0:T(8,128)(2,1)}, bf16[384,4096]{1,0:T(8,128)(2,1)}, u32[]{:S(2)}, u32[]{:S(2)}) collective-permute-start(bf16[384,4096]{1,0:T(8,128)(2,1)} %bitcast.49), channel_id=1, source_target_pairs={{0,1},{1,0},{2,3},{3,2},{4,5},{5,4},{6,7},{7,6},{8,9},{9,8},{10,11... | collective-permute-start | bytes 9437192 | tf_op jit(solution)/shard_map/ppermute | solution.py:12
  96.1 6.1 %collective-permute-start = (bf16[512,1024]{1,0:T(8,128)(2,1)S(1)}, bf16[512,1024]{1,0:T(8,128)(2,1)S(1)}, u32[]{:S(2)}, u32[]{:S(2)}) collective-permute-start(bf16[512,1024]{1,0:T(8,128)(2,1)S(1)} %get-tuple-element.22), channel_id=1, source_target_pairs={{0,1},{1,0},{2,3},{3,2},{4,5},{5,4},{6,7},{7,6},{8,9},{9,8},{10,11... | collective-permute-start | bytes 3145736 | tf_op jit(solution)/shard_map/ppermute | solution.py:12
  123.8 47.2 %all-to-all-start = ((bf16[16,48,2048]{2,1,0:T(8,128)(2,1)}), bf16[16,48,2048]{2,1,0:T(8,128)(2,1)}, u32[]{:S(2)}, u32[]{:S(2)}) async-start(bf16[16,48,2048]{2,1,0:T(8,128)(2,1)} %bitcast.41), calls=%async_computation | async-start | bytes 6291456 | tf_op jit(solution)/shard_map/all_to_all | solution.py:78
  171.0 5.6 %copy-start.18 = (f32[768,768]{1,0:T(8,128)S(1)}, f32[768,768]{1,0:T(8,128)}, u32[]{:S(2)}) copy-start(f32[768,768]{1,0:T(8,128)} %fusion.12) | copy-start | bytes 7077892
  185.8 8.7 %copy-start.10 = (s32[1024,16]{0,1:T(8,128)S(1)}, s32[1024,16]{0,1:T(8,128)}, u32[]{:S(2)}) copy-start(s32[1024,16]{0,1:T(8,128)} %copy-done.9) | copy-start | bytes 196612
  185.8 8.7 %copy-start.16 = (s32[16]{0:T(128)S(1)}, s32[16]{0:T(128)}, u32[]{:S(2)}) copy-start(s32[16]{0:T(128)} %copy-done.15) | copy-start | bytes 196
  185.8 54.3 %copy-start.12 = (s32[16,512]{1,0:T(8,128)S(1)}, s32[16,512]{1,0:T(8,128)}, u32[]{:S(2)}) copy-start(s32[16,512]{1,0:T(8,128)} %copy-done.11) | copy-start | bytes 98308
  185.9 54.3 %all-to-all-start.2 = ((bf16[16,48,2048]{2,1,0:T(8,128)(2,1)}), bf16[16,48,2048]{2,1,0:T(8,128)(2,1)S(1)}, u32[]{:S(2)}, u32[]{:S(2)}) async-start(bf16[16,48,2048]{2,1,0:T(8,128)(2,1)} %bitcast.44), calls=%async_computation.2 | async-start | bytes 6291456 | tf_op jit(solution)/shard_map/all_to_all | solution.py:90
  240.2 6.5 %copy-start.3 = (bf16[768,1024]{1,0:T(8,128)(2,1)S(1)}, bf16[768,1024]{1,0:T(8,128)(2,1)}, u32[]{:S(2)}) copy-start(bf16[768,1024]{1,0:T(8,128)(2,1)} %get-tuple-element.7) | copy-start | bytes 4718596
  240.2 6.5 %copy-start.4 = (bf16[768,1024]{1,0:T(8,128)(2,1)S(1)}, bf16[768,1024]{1,0:T(8,128)(2,1)}, u32[]{:S(2)}) copy-start(bf16[768,1024]{1,0:T(8,128)(2,1)} %get-tuple-element.8) | copy-start | bytes 4718596
  240.2 6.5 %copy-start.20 = (bf16[768,768]{1,0:T(8,128)(2,1)S(1)}, bf16[768,768]{1,0:T(8,128)(2,1)}, u32[]{:S(2)}) copy-start(bf16[768,768]{1,0:T(8,128)(2,1)} %copy-done.19) | copy-start | bytes 3538948
  244.5 10.2 %collective-permute-start.5 = (bf16[512,1024]{1,0:T(8,128)(2,1)}, bf16[512,1024]{1,0:T(8,128)(2,1)}, u32[]{:S(2)}, u32[]{:S(2)}) collective-permute-start(bf16[512,1024]{1,0:T(8,128)(2,1)} %slice.33), channel_id=1, source_target_pairs={{0,1},{1,0},{2,3},{3,2},{4,5},{5,4},{6,7},{7,6},{8,9},{9,8},{10,11... | collective-permute-start | bytes 3145736 | tf_op jit(solution)/shard_map/ppermute | solution.py:12
  250.8 52.9 %all-to-all-start.3 = ((bf16[16,48,2048]{2,1,0:T(8,128)(2,1)}), bf16[16,48,2048]{2,1,0:T(8,128)(2,1)S(1)}, u32[]{:S(2)}, u32[]{:S(2)}) async-start(bf16[16,48,2048]{2,1,0:T(8,128)(2,1)} %bitcast.43), calls=%async_computation.4 | async-start | bytes 6291456 | tf_op jit(solution)/shard_map/all_to_all | solution.py:90
  254.6 56.0 %reduce-scatter.3.cloned.1.call-start = ((), (), s32[]{:S(2)}) async-start(), calls=%async_computation.8 | async-start | bytes 2359296 | tf_op jit(solution)/shard_map/reduce_scatter | solution.py:99
  257.9 87.8 %reduce-scatter.5.cloned.1.call-start = ((), (), s32[]{:S(2)}) async-start(), calls=%async_computation.9 | async-start | bytes 2359296 | tf_op jit(solution)/shard_map/reduce_scatter | solution.py:99
  305.6 3.2 collective-permute-start.6
  (12 other events, 47.3 us)
Sparse Core Ops, SparseCore 0:
  9.1 41.1 all-gather.4
  52.2 39.9 all-gather.2
  258.0 36.9 reduce-scatter.2
  310.7 34.9 reduce-scatter.4

commit v2 on v1

v2 whole, which is shorter than its diff:
```python
import jax
import jax.numpy as jnp
from jax import lax
from jax.sharding import Mesh, PartitionSpec as P

PLANE = (4, 4)
CUTS = (0, 16, 32, 48)


def swap(array):
    return lax.ppermute(array, "tp", [(0, 1), (1, 0)])


def around(array, step):
    planes = lax.axis_size("z")
    pairs = []
    for plane in range(planes):
        pairs.append((2 * plane, 2 * ((plane + step) % planes)))
        pairs.append((2 * plane + 1, 2 * ((plane - step) % planes) + 1))
    return lax.ppermute(array, ("z", "tp"), pairs)


def exchange(array):
    return lax.all_to_all(array, ("y", "x"), split_axis=0, concat_axis=0, tiled=True)


def on_device(tokens, expert_ids, gate_levels, gate_weight, up_weight, down_weight):
    planes = lax.axis_size("z")
    plane_experts = lax.axis_size("y") * lax.axis_size("x")
    core = lax.axis_index("tp")
    tok_count, top_count = expert_ids.shape
    half_width = tokens.shape[1]
    model_width = 2 * half_width
    capacity = 3 * tok_count * top_count // (2 * planes * plane_experts)
    far = planes // 2
    half_slots = capacity // 2
    starts = [0] + [half_slots + capacity * (k - 1) for k in range(1, far + 1)]
    ends = starts[1:] + [starts[-1] + half_slots]
    chunks = list(zip(CUTS[:-1], CUTS[1:]))

    routes = jnp.concatenate([expert_ids, gate_levels], axis=1).T.astype(jnp.bfloat16)
    routes = jnp.pad(routes, ((0, tok_count - 2 * top_count), (0, 128 - tok_count)))
    received = swap(tokens)
    low = jnp.where(core == 0, tokens, received)
    high = jnp.where(core == 0, received, tokens)
    blocks = [jnp.concatenate([low, high, routes], axis=1)]
    for k in range(far):
        blocks.append(around(blocks[k], 1))

    first = lax.axis_index("z") * plane_experts
    plane_ids = first + jnp.arange(plane_experts, dtype=jnp.int32)
    order = jnp.arange(tok_count)
    before = (order[:, None] < order[None, :]).astype(jnp.bfloat16)

    def places(k):
        table = blocks[k][: 2 * top_count, model_width : model_width + tok_count]
        ids = table[:top_count].astype(jnp.int32)
        levels = table[top_count:].astype(jnp.float32)
        weights = levels / jnp.sum(levels, axis=0, keepdims=True)
        hits = ids[None, :, :] == plane_ids[:, None, None]
        named = jnp.any(hits, axis=1)
        scale = jnp.sum(jnp.where(hits, weights[None, :, :], 0.0), axis=1)
        rank = jnp.dot(
            named.astype(jnp.bfloat16), before, preferred_element_type=jnp.float32
        ).astype(jnp.int32)
        if k in (0, far):
            rank = rank - core * half_slots
            named = named & (rank >= 0) & (rank < half_slots)
        return jnp.where(named, rank + starts[k], -1), scale

    placed = [places(k) for k in range(far + 1)]

    def within(k, chunk):
        return starts[k] < chunk[1] and chunk[0] < ends[k]

    def fits(k, chunk):
        slots = jnp.arange(chunk[0], chunk[1], dtype=jnp.int32)
        return placed[k][0][:, None, :] == slots[None, :, None]

    w_gate = jnp.concatenate([gate_weight[0], swap(gate_weight[0])], axis=1)
    w_up = jnp.concatenate([up_weight[0], swap(up_weight[0])], axis=1)
    w_down = jnp.concatenate([down_weight[0], swap(down_weight[0])], axis=0)

    arrivals = []
    for chunk in chunks:
        rows = plane_experts * (chunk[1] - chunk[0])
        outgoing = 0.0
        for k in range(far + 1):
            if within(k, chunk):
                select = fits(k, chunk).astype(jnp.bfloat16).reshape(rows, tok_count)
                outgoing += jnp.dot(
                    select, blocks[k][:, :model_width], preferred_element_type=jnp.float32
                )
        outgoing = outgoing.astype(jnp.bfloat16).reshape(plane_experts, -1, model_width)
        arrivals.append(exchange(outgoing))

    returns = [None] * len(chunks)
    for index in reversed(range(len(chunks))):
        arrived = arrivals[index].reshape(-1, model_width)
        gate_values = jnp.dot(arrived, w_gate, preferred_element_type=jnp.float32)
        up_values = jnp.dot(arrived, w_up, preferred_element_type=jnp.float32)
        hidden = (jax.nn.silu(gate_values) * up_values).astype(jnp.bfloat16)
        produced = jnp.dot(hidden, w_down, preferred_element_type=jnp.float32)
        produced = produced.astype(jnp.bfloat16).reshape(plane_experts, -1, model_width)
        returns[index] = exchange(produced).reshape(-1, model_width)

    total = 0.0
    for k in reversed(range(far + 1)):
        for index in reversed(range(len(chunks))):
            chunk = chunks[index]
            if within(k, chunk):
                mix = jnp.where(fits(k, chunk), placed[k][1][:, None, :], 0.0)
                mix = mix.astype(jnp.bfloat16).reshape(-1, tok_count)
                total += lax.dot_general(
                    mix,
                    returns[index],
                    (((0,), (0,)), ((), ())),
                    preferred_element_type=jnp.float32,
                )
        if k > 0:
            total = around(total.astype(jnp.bfloat16), -1).astype(jnp.float32)
    low, high = total[:, :half_width], total[:, half_width:]
    own = jnp.where(core == 0, low, high)
    other = jnp.where(core == 0, high, low).astype(jnp.bfloat16)
    return (own + swap(other).astype(jnp.float32)).astype(jnp.bfloat16)


def solution(mesh):
    n_ep, n_tp = mesh.shape["ep"], mesh.shape["tp"]
    n_y, n_x = PLANE
    torus = Mesh(
        mesh.devices.reshape(n_ep // (n_y * n_x), n_y, n_x, n_tp), ("z", "y", "x", "tp")
    )
    ep = ("z", "y", "x")
    in_specs = (
        P(ep, "tp"),
        P(ep, None),
        P(ep, None),
        P(ep, None, "tp"),
        P(ep, None, "tp"),
        P(ep, "tp", None),
    )
    return jax.shard_map(
        on_device, mesh=torus, in_specs=in_specs, out_specs=P(ep, "tp"), check_vma=False
    )
```

time: 358 us -> 324 us (0.905)
  waiting for transfers between devices: 210 us -> 156 us
  matrix products: 38.9 us -> 77.8 us
  starting transfers between devices: 44.4 us -> 76.6 us
  blocking collectives: 19 us -> 0 us
  between operations: 13.5 us -> 0.21 us
  other arithmetic: 19.3 us -> 9.96 us
  local copies, waits for them, and re-layouts: 8.72 us -> 2.88 us
    ppermute x7 -> x13, waiting for transfers between devices: 6.22 us -> 92.8 us  [the longest x8 90.9 us: around(): return lax.ppermute(array, ('z', 'tp'), pairs)]
    all_to_all x4 -> x6, waiting for transfers between devices: 127 us -> 63.1 us  [exchange(): lax.all_to_all(array, ('y', 'x'), split_axis=0, concat_axis=0, tiled=True)]
    all_gather x2 -> x0, waiting for transfers between devices: 41.2 us -> none  [on_device(): column = lax.all_gather(piece, 'z', axis=0, tiled=True)]
    dot_general x11 -> x25, matrix products: 38.9 us -> 77.8 us  [the longest x3 34.2 us: on_device(): produced = jnp.dot(hidden, w_down, preferred_element_type=jnp.float32)]
    reduce_scatter x2 -> x0, waiting for transfers between devices: 35.1 us -> none  [on_device(): lax.psum_scatter(column, 'z', scatter_dimension=0, tiled=True)]
    ppermute x7 -> x13, starting transfers between devices: 16.2 us -> 40.9 us  [the longest x8 26.8 us: around(): return lax.ppermute(array, ('z', 'tp'), pairs)]
    all_gather x1 -> x0, blocking collectives: 19 us -> none  [on_device(): lax.all_gather(jnp.concatenate([expert_ids, gate_levels], axis=1), 'z', a...]
    concatenate x7 -> x1, other arithmetic: 16.8 us -> 0.08 us  [on_device(): blocks = [jnp.concatenate([low, high, routes], axis=1)]]
  transfers between devices with their start and end apart: 15 -> 19, of which waited for: 8 -> 16; matrix products, arithmetic and copies ran while one was open for 12% -> 23% of each run, Pallas kernels for 0% -> 0%
where the time goes in v2:
time: 324 us; the launch traced here: 323 us
  waiting for transfers between devices  156 us (48%)
  matrix products  77.8 us (24%)
  starting transfers between devices  76.6 us (24%)
  other arithmetic  9.96 us (3%)
    ppermute x8, waiting for transfers between devices, around(): return lax.ppermute(array, ('z', 'tp'), pairs)  90.9 us
    all_to_all x6, waiting for transfers between devices, exchange(): lax.all_to_all(array, ('y', 'x'), split_axis=0, concat_axis=0, tiled=True)  63.1 us
    all_to_all x6, starting transfers between devices, exchange(): lax.all_to_all(array, ('y', 'x'), split_axis=0, concat_axis=0, tiled=True)  35.7 us
    dot_general x3, matrix products, on_device(): produced = jnp.dot(hidden, w_down, preferred_element_type=jnp.float32)  34.2 us
    ppermute x8, starting transfers between devices, around(): return lax.ppermute(array, ('z', 'tp'), pairs)  26.8 us
    dot_general x3, matrix products, on_device(): up_values = jnp.dot(arrived, w_up, preferred_element_type=jnp.float32)  17.5 us
    ppermute x5, starting transfers between devices, swap(): return lax.ppermute(array, 'tp', [(0, 1), (1, 0)])  14.2 us
    dot_general x7, matrix products, on_device(): lax.dot_general(mix, returns[index], (((0,), (0,)), ((), ())), preferred_...  13.8 us
  transfers between devices with their start and end apart: 19, of which 16 were waited for; matrix products, arithmetic and copies ran while one was open for 23% of the time, Pallas kernels for 0%

profile of v2, /device:TPU:1, one launch (start us, length us, event | category | flops | bytes accessed | tf_op | source)
XLA Modules:
  0.0 323.4 jit_solution(16338107892221387571)
XLA Ops:
  10.1 12.1 %collective-permute-done.1 = bf16[128,4224]{1,0:T(8,128)(2,1)S(1)} collective-permute-done((bf16[128,4224]{1,0:T(8,128)(2,1)S(1)}, bf16[128,4224]{1,0:T(8,128)(2,1)S(1)}, u32[]{:S(2)}, u32[]{:S(2)}) %collective-permute-start.1) | collective-permute-done | bytes 1081376 | tf_op jit(solution)/shard_map/ppermute | solution.py:20
  25.3 12.1 %collective-permute-done.2 = bf16[128,4224]{1,0:T(8,128)(2,1)} collective-permute-done((bf16[128,4224]{1,0:T(8,128)(2,1)S(1)}, bf16[128,4224]{1,0:T(8,128)(2,1)}, u32[]{:S(2)}, u32[]{:S(2)}) %collective-permute-start.2) | collective-permute-done | bytes 1081376 | tf_op jit(solution)/shard_map/ppermute | solution.py:20
  40.7 12.3 %collective-permute-done.3 = bf16[128,4224]{1,0:T(8,128)(2,1)S(1)} collective-permute-done((bf16[128,4224]{1,0:T(8,128)(2,1)}, bf16[128,4224]{1,0:T(8,128)(2,1)S(1)}, u32[]{:S(2)}, u32[]{:S(2)}) %collective-permute-start.3) | collective-permute-done | bytes 1081376 | tf_op jit(solution)/shard_map/ppermute | solution.py:20
  57.0 11.2 %collective-permute-done.4 = bf16[128,4224]{1,0:T(8,128)(2,1)} collective-permute-done((bf16[128,4224]{1,0:T(8,128)(2,1)S(1)}, bf16[128,4224]{1,0:T(8,128)(2,1)}, u32[]{:S(2)}, u32[]{:S(2)}) %collective-permute-start.4) | collective-permute-done | bytes 1081376 | tf_op jit(solution)/shard_map/ppermute | solution.py:20
  72.8 6.8 %all-to-all-start.4 = ((bf16[16,16,4096]{2,1,0:T(8,128)(2,1)}), bf16[16,16,4096]{2,1,0:T(8,128)(2,1)}, u32[]{:S(2)}, u32[]{:S(2)}) async-start(bf16[16,16,4096]{2,1,0:T(8,128)(2,1)} %bitcast.20), calls=%async_computation.4 | async-start | bytes 4194304 | tf_op jit(solution)/shard_map/all_to_all | solution.py:24
  89.7 14.1 %all-to-all-done.4 = bf16[16,16,4096]{2,1,0:T(8,128)(2,1)} async-done(((bf16[16,16,4096]{2,1,0:T(8,128)(2,1)}), bf16[16,16,4096]{2,1,0:T(8,128)(2,1)}, u32[]{:S(2)}, u32[]{:S(2)}) %all-to-all-start.4) | async-done | bytes 2097184 | tf_op jit(solution)/shard_map/all_to_all | solution.py:24
  113.7 18.4 %all-to-all-done = bf16[16,16,4096]{2,1,0:T(8,128)(2,1)} async-done(((bf16[16,16,4096]{2,1,0:T(8,128)(2,1)}), bf16[16,16,4096]{2,1,0:T(8,128)(2,1)}, u32[]{:S(2)}, u32[]{:S(2)}) %all-to-all-start) | async-done | bytes 2097184 | tf_op jit(solution)/shard_map/all_to_all | solution.py:24
  132.1 5.7 %all-to-all-start.2 = ((bf16[16,16,4096]{2,1,0:T(8,128)(2,1)}), bf16[16,16,4096]{2,1,0:T(8,128)(2,1)S(1)}, u32[]{:S(2)}, u32[]{:S(2)}) async-start(bf16[16,16,4096]{2,1,0:T(8,128)(2,1)} %bitcast.13), calls=%async_computation.2 | async-start | bytes 4194304 | tf_op jit(solution)/shard_map/all_to_all | solution.py:24
  137.9 6.1 %fusion.7 = f32[256,768]{1,0:T(8,128)} fusion(bf16[256,4096]{1,0:T(8,128)(2,1)} %bitcast.4, bf16[4096,384]{1,0:T(8,128)(2,1)} %collective-permute-done.6, bf16[4096,384]{1,0:T(8,128)(2,1)} %bitcast.79), kind=kOutput, calls=%fused_computation.29 | convolution fusion | flops 1623195648 | bytes 9175040 | tf_op jit(solution)/shard_map/dot_general | solution.py:101
  144.0 11.3 %convolution_convert_fusion.2 = bf16[256,4096]{1,0:T(8,128)(2,1)} fusion(bf16[384,4096]{1,0:T(8,128)(2,1)} %collective-permute-done.7, bf16[384,4096]{1,0:T(8,128)(2,1)} %bitcast.83, f32[256,768]{1,0:T(8,128)} %fusion.7, bf16[256,4096]{1,0:T(8,128)(2,1)} %bitcast.4, bf16[4096,384]{1,0:T(8,128)(2,1)} %collective-permute-done.5, bf16[4096,384]{1,0:T(8,128)(2,1)} %bitcast.87), kind=kOutput, calls=%fused_computation.12 | convolution fusion | flops 3248619520 | bytes 17563648 | tf_op jit(solution)/shard_map/dot_general | solution.py:103
  155.4 5.6 %all-to-all-done.2 = bf16[16,16,4096]{2,1,0:T(8,128)(2,1)S(1)} async-done(((bf16[16,16,4096]{2,1,0:T(8,128)(2,1)}), bf16[16,16,4096]{2,1,0:T(8,128)(2,1)S(1)}, u32[]{:S(2)}, u32[]{:S(2)}) %all-to-all-start.2) | async-done | bytes 2097184 | tf_op jit(solution)/shard_map/all_to_all | solution.py:24
  162.3 5.7 %all-to-all-start.1 = ((bf16[16,16,4096]{2,1,0:T(8,128)(2,1)}), bf16[16,16,4096]{2,1,0:T(8,128)(2,1)S(1)}, u32[]{:S(2)}, u32[]{:S(2)}) async-start(bf16[16,16,4096]{2,1,0:T(8,128)(2,1)} %bitcast.77), calls=%async_computation.1 | async-start | bytes 4194304 | tf_op jit(solution)/shard_map/all_to_all | solution.py:24
  170.1 6.1 %fusion.6 = f32[256,768]{1,0:T(8,128)} fusion(bf16[256,4096]{1,0:T(8,128)(2,1)} %bitcast.74, bf16[4096,384]{1,0:T(8,128)(2,1)} %collective-permute-done.6, bf16[4096,384]{1,0:T(8,128)(2,1)} %bitcast.80), kind=kOutput, calls=%fused_computation.28 | convolution fusion | flops 1623195648 | bytes 9175040 | tf_op jit(solution)/shard_map/dot_general | solution.py:101
  176.2 11.5 %convolution_convert_fusion.1 = bf16[256,4096]{1,0:T(8,128)(2,1)} fusion(bf16[384,4096]{1,0:T(8,128)(2,1)} %collective-permute-done.7, bf16[384,4096]{1,0:T(8,128)(2,1)} %bitcast.84, f32[256,768]{1,0:T(8,128)} %fusion.6, bf16[256,4096]{1,0:T(8,128)(2,1)} %bitcast.75, bf16[4096,384]{1,0:T(8,128)(2,1)} %collective-permute-done.5, bf16[4096,384]{1,0:T(8,128)(2,1)} %bitcast.88), kind=kOutput, calls=%fused_computation.11 | convolution fusion | flops 3248619520 | bytes 17563648 | tf_op jit(solution)/shard_map/dot_general | solution.py:103
  192.5 5.6 %all-to-all-start.3 = ((bf16[16,16,4096]{2,1,0:T(8,128)(2,1)}), bf16[16,16,4096]{2,1,0:T(8,128)(2,1)S(1)}, u32[]{:S(2)}, u32[]{:S(2)}) async-start(bf16[16,16,4096]{2,1,0:T(8,128)(2,1)} %bitcast.73), calls=%async_computation.3 | async-start | bytes 4194304 | tf_op jit(solution)/shard_map/all_to_all | solution.py:24
  209.0 12.3 %all-to-all-done.3 = bf16[16,16,4096]{2,1,0:T(8,128)(2,1)S(1)} async-done(((bf16[16,16,4096]{2,1,0:T(8,128)(2,1)}), bf16[16,16,4096]{2,1,0:T(8,128)(2,1)S(1)}, u32[]{:S(2)}, u32[]{:S(2)}) %all-to-all-start.3) | async-done | bytes 2097184 | tf_op jit(solution)/shard_map/all_to_all | solution.py:24
  221.8 18.3 %collective-permute-done.8 = bf16[128,4096]{1,0:T(8,128)(2,1)S(1)} collective-permute-done((bf16[128,4096]{1,0:T(8,128)(2,1)}, bf16[128,4096]{1,0:T(8,128)(2,1)S(1)}, u32[]{:S(2)}, u32[]{:S(2)}) %collective-permute-start.8) | collective-permute-done | bytes 1048608 | tf_op jit(solution)/shard_map/ppermute | solution.py:20
  242.0 11.4 %convolution_convert_fusion = bf16[256,4096]{1,0:T(8,128)(2,1)} fusion(bf16[384,4096]{1,0:T(8,128)(2,1)} %collective-permute-done.7, bf16[384,4096]{1,0:T(8,128)(2,1)} %bitcast.85, f32[256,768]{1,0:T(8,128)} %fusion.5, bf16[256,4096]{1,0:T(8,128)(2,1)} %bitcast.21, bf16[4096,384]{1,0:T(8,128)(2,1)} %collective-permute-done.5, bf16[4096,384]{1,0:T(8,128)(2,1)} %bitcast.89), kind=kOutput, calls=%fused_computation.10 | convolution fusion | flops 3248619520 | bytes 17563648 | tf_op jit(solution)/shard_map/dot_general | solution.py:103
  253.4 6.7 %all-to-all-start.5 = ((bf16[16,16,4096]{2,1,0:T(8,128)(2,1)}), bf16[16,16,4096]{2,1,0:T(8,128)(2,1)}, u32[]{:S(2)}, u32[]{:S(2)}) async-start(bf16[16,16,4096]{2,1,0:T(8,128)(2,1)} %bitcast.76), calls=%async_computation.5 | async-start | bytes 4194304 | tf_op jit(solution)/shard_map/all_to_all | solution.py:24
  260.1 7.5 %collective-permute-done.9 = bf16[128,4096]{1,0:T(8,128)(2,1)S(1)} collective-permute-done((bf16[128,4096]{1,0:T(8,128)(2,1)}, bf16[128,4096]{1,0:T(8,128)(2,1)S(1)}, u32[]{:S(2)}, u32[]{:S(2)}) %collective-permute-start.9) | collective-permute-done | bytes 1048608 | tf_op jit(solution)/shard_map/ppermute | solution.py:20
  271.0 9.1 %all-to-all-done.5 = bf16[16,16,4096]{2,1,0:T(8,128)(2,1)} async-done(((bf16[16,16,4096]{2,1,0:T(8,128)(2,1)}), bf16[16,16,4096]{2,1,0:T(8,128)(2,1)}, u32[]{:S(2)}, u32[]{:S(2)}) %all-to-all-start.5) | async-done | bytes 2097184 | tf_op jit(solution)/shard_map/all_to_all | solution.py:24
  280.1 5.7 %collective-permute-done.10 = bf16[128,4096]{1,0:T(8,128)(2,1)S(1)} collective-permute-done((bf16[128,4096]{1,0:T(8,128)(2,1)}, bf16[128,4096]{1,0:T(8,128)(2,1)S(1)}, u32[]{:S(2)}, u32[]{:S(2)}) %collective-permute-start.10) | collective-permute-done | bytes 1048608 | tf_op jit(solution)/shard_map/ppermute | solution.py:20
  288.6 13.5 %collective-permute-start.11 = (bf16[128,4096]{1,0:T(8,128)(2,1)S(1)}, bf16[128,4096]{1,0:T(8,128)(2,1)S(1)}, u32[]{:S(2)}, u32[]{:S(2)}) collective-permute-start(bf16[128,4096]{1,0:T(8,128)(2,1)S(1)} %add_convert_fusion), channel_id=1, source_target_pairs={{0,224},{1,33},{32,0},{33,65},{64,32},{65,97},{96,64},{97,129},{12... | collective-permute-start | bytes 3145736 | tf_op jit(solution)/shard_map/ppermute | solution.py:20
  302.1 11.7 %collective-permute-done.11 = bf16[128,4096]{1,0:T(8,128)(2,1)S(1)} collective-permute-done((bf16[128,4096]{1,0:T(8,128)(2,1)S(1)}, bf16[128,4096]{1,0:T(8,128)(2,1)S(1)}, u32[]{:S(2)}, u32[]{:S(2)}) %collective-permute-start.11) | collective-permute-done | bytes 1048608 | tf_op jit(solution)/shard_map/ppermute | solution.py:20
  (83 shorter events, 82.2 us)
Async XLA Ops:
  0.0 5.0 %collective-permute-start = (bf16[128,2048]{1,0:T(8,128)(2,1)}, bf16[128,2048]{1,0:T(8,128)(2,1)S(1)}, u32[]{:S(2)}, u32[]{:S(2)}) collective-permute-start(bf16[128,2048]{1,0:T(8,128)(2,1)} %param.6), channel_id=1, source_target_pairs={{0,1},{1,0},{2,3},{3,2},{4,5},{5,4},{6,7},{7,6},{8,9},{9,8},{10,11... | collective-permute-start | bytes 1572872 | tf_op jit(solution)/shard_map/ppermute | solution.py:11
  6.2 16.0 %collective-permute-start.1 = (bf16[128,4224]{1,0:T(8,128)(2,1)S(1)}, bf16[128,4224]{1,0:T(8,128)(2,1)S(1)}, u32[]{:S(2)}, u32[]{:S(2)}) collective-permute-start(bf16[128,4224]{1,0:T(8,128)(2,1)S(1)} %fusion.19), channel_id=1, source_target_pairs={{0,32},{1,225},{32,64},{33,1},{64,96},{65,33},{96,128},{97,65},{12... | collective-permute-start | bytes 3244040 | tf_op jit(solution)/shard_map/ppermute | solution.py:20
  22.2 86.8 %copy-start.2 = (bf16[128,4224]{1,0:T(8,128)(2,1)}, bf16[128,4224]{1,0:T(8,128)(2,1)S(1)}, u32[]{:S(2)}) copy-start(bf16[128,4224]{1,0:T(8,128)(2,1)S(1)} %collective-permute-done.1) | copy-start | bytes 3244036
  22.2 15.2 %collective-permute-start.2 = (bf16[128,4224]{1,0:T(8,128)(2,1)S(1)}, bf16[128,4224]{1,0:T(8,128)(2,1)}, u32[]{:S(2)}, u32[]{:S(2)}) collective-permute-start(bf16[128,4224]{1,0:T(8,128)(2,1)S(1)} %collective-permute-done.1), channel_id=1, source_target_pairs={{0,32},{1,225},{32,64},{33,1},{64,96},{65,33},{96,128},{97,65},{12... | collective-permute-start | bytes 3244040 | tf_op jit(solution)/shard_map/ppermute | solution.py:20
  37.4 15.6 %collective-permute-start.3 = (bf16[128,4224]{1,0:T(8,128)(2,1)}, bf16[128,4224]{1,0:T(8,128)(2,1)S(1)}, u32[]{:S(2)}, u32[]{:S(2)}) collective-permute-start(bf16[128,4224]{1,0:T(8,128)(2,1)} %collective-permute-done.2), channel_id=1, source_target_pairs={{0,32},{1,225},{32,64},{33,1},{64,96},{65,33},{96,128},{97,65},{12... | collective-permute-start | bytes 3244040 | tf_op jit(solution)/shard_map/ppermute | solution.py:20
  53.0 15.1 %collective-permute-start.4 = (bf16[128,4224]{1,0:T(8,128)(2,1)S(1)}, bf16[128,4224]{1,0:T(8,128)(2,1)}, u32[]{:S(2)}, u32[]{:S(2)}) collective-permute-start(bf16[128,4224]{1,0:T(8,128)(2,1)S(1)} %collective-permute-done.3), channel_id=1, source_target_pairs={{0,32},{1,225},{32,64},{33,1},{64,96},{65,33},{96,128},{97,65},{12... | collective-permute-start | bytes 3244040 | tf_op jit(solution)/shard_map/ppermute | solution.py:20
  72.8 31.0 %all-to-all-start.4 = ((bf16[16,16,4096]{2,1,0:T(8,128)(2,1)}), bf16[16,16,4096]{2,1,0:T(8,128)(2,1)}, u32[]{:S(2)}, u32[]{:S(2)}) async-start(bf16[16,16,4096]{2,1,0:T(8,128)(2,1)} %bitcast.20), calls=%async_computation.4 | async-start | bytes 4194304 | tf_op jit(solution)/shard_map/all_to_all | solution.py:24
  79.6 58.3 %collective-permute-start.6 = (bf16[4096,384]{1,0:T(8,128)(2,1)}, bf16[4096,384]{1,0:T(8,128)(2,1)}, u32[]{:S(2)}, u32[]{:S(2)}) collective-permute-start(bf16[4096,384]{1,0:T(8,128)(2,1)} %bitcast.78), channel_id=1, source_target_pairs={{0,1},{1,0},{2,3},{3,2},{4,5},{5,4},{6,7},{7,6},{8,9},{9,8},{10,11... | collective-permute-start | bytes 9437192 | tf_op jit(solution)/shard_map/ppermute | solution.py:11
  85.2 58.8 %collective-permute-start.5 = (bf16[4096,384]{1,0:T(8,128)(2,1)}, bf16[4096,384]{1,0:T(8,128)(2,1)}, u32[]{:S(2)}, u32[]{:S(2)}) collective-permute-start(bf16[4096,384]{1,0:T(8,128)(2,1)} %bitcast.86), channel_id=1, source_target_pairs={{0,1},{1,0},{2,3},{3,2},{4,5},{5,4},{6,7},{7,6},{8,9},{9,8},{10,11... | collective-permute-start | bytes 9437192 | tf_op jit(solution)/shard_map/ppermute | solution.py:11
  85.3 58.7 %collective-permute-start.7 = (bf16[384,4096]{1,0:T(8,128)(2,1)}, bf16[384,4096]{1,0:T(8,128)(2,1)}, u32[]{:S(2)}, u32[]{:S(2)}) collective-permute-start(bf16[384,4096]{1,0:T(8,128)(2,1)} %bitcast.82), channel_id=1, source_target_pairs={{0,1},{1,0},{2,3},{3,2},{4,5},{5,4},{6,7},{7,6},{8,9},{9,8},{10,11... | collective-permute-start | bytes 9437192 | tf_op jit(solution)/shard_map/ppermute | solution.py:11
  103.8 28.3 %all-to-all-start = ((bf16[16,16,4096]{2,1,0:T(8,128)(2,1)}), bf16[16,16,4096]{2,1,0:T(8,128)(2,1)}, u32[]{:S(2)}, u32[]{:S(2)}) async-start(bf16[16,16,4096]{2,1,0:T(8,128)(2,1)} %bitcast.3), calls=%async_computation | async-start | bytes 4194304 | tf_op jit(solution)/shard_map/all_to_all | solution.py:24
  132.1 28.9 %all-to-all-start.2 = ((bf16[16,16,4096]{2,1,0:T(8,128)(2,1)}), bf16[16,16,4096]{2,1,0:T(8,128)(2,1)S(1)}, u32[]{:S(2)}, u32[]{:S(2)}) async-start(bf16[16,16,4096]{2,1,0:T(8,128)(2,1)} %bitcast.13), calls=%async_computation.2 | async-start | bytes 4194304 | tf_op jit(solution)/shard_map/all_to_all | solution.py:24
  161.0 1.3 copy-start.3
  162.3 28.9 %all-to-all-start.1 = ((bf16[16,16,4096]{2,1,0:T(8,128)(2,1)}), bf16[16,16,4096]{2,1,0:T(8,128)(2,1)S(1)}, u32[]{:S(2)}, u32[]{:S(2)}) async-start(bf16[16,16,4096]{2,1,0:T(8,128)(2,1)} %bitcast.77), calls=%async_computation.1 | async-start | bytes 4194304 | tf_op jit(solution)/shard_map/all_to_all | solution.py:24
  191.2 1.3 copy-start
  192.5 28.8 %all-to-all-start.3 = ((bf16[16,16,4096]{2,1,0:T(8,128)(2,1)}), bf16[16,16,4096]{2,1,0:T(8,128)(2,1)S(1)}, u32[]{:S(2)}, u32[]{:S(2)}) async-start(bf16[16,16,4096]{2,1,0:T(8,128)(2,1)} %bitcast.73), calls=%async_computation.3 | async-start | bytes 4194304 | tf_op jit(solution)/shard_map/all_to_all | solution.py:24
  198.1 5.6 %copy-start.4 = (bf16[1,4096,384]{2,1,0:T(8,128)(2,1)S(1)}, bf16[1,4096,384]{2,1,0:T(8,128)(2,1)}, u32[]{:S(2)}) copy-start(bf16[1,4096,384]{2,1,0:T(8,128)(2,1)} %param.10) | copy-start | bytes 9437188
  203.8 36.4 %collective-permute-start.8 = (bf16[128,4096]{1,0:T(8,128)(2,1)}, bf16[128,4096]{1,0:T(8,128)(2,1)S(1)}, u32[]{:S(2)}, u32[]{:S(2)}) collective-permute-start(bf16[128,4096]{1,0:T(8,128)(2,1)} %fusion.3), channel_id=1, source_target_pairs={{0,224},{1,33},{32,0},{33,65},{64,32},{65,97},{96,64},{97,129},{12... | collective-permute-start | bytes 3145736 | tf_op jit(solution)/shard_map/ppermute | solution.py:20
  221.3 18.9 %copy-start.1 = (bf16[16,16,4096]{2,1,0:T(8,128)(2,1)S(1)}, bf16[16,16,4096]{2,1,0:T(8,128)(2,1)}, u32[]{:S(2)}) copy-start(bf16[16,16,4096]{2,1,0:T(8,128)(2,1)} %copy-done) | copy-start | bytes 6291460
  242.0 25.6 %collective-permute-start.9 = (bf16[128,4096]{1,0:T(8,128)(2,1)}, bf16[128,4096]{1,0:T(8,128)(2,1)S(1)}, u32[]{:S(2)}, u32[]{:S(2)}) collective-permute-start(bf16[128,4096]{1,0:T(8,128)(2,1)} %add_convert_fusion.2), channel_id=1, source_target_pairs={{0,224},{1,33},{32,0},{33,65},{64,32},{65,97},{96,64},{97,129},{12... | collective-permute-start | bytes 3145736 | tf_op jit(solution)/shard_map/ppermute | solution.py:20
  253.4 26.7 %all-to-all-start.5 = ((bf16[16,16,4096]{2,1,0:T(8,128)(2,1)}), bf16[16,16,4096]{2,1,0:T(8,128)(2,1)}, u32[]{:S(2)}, u32[]{:S(2)}) async-start(bf16[16,16,4096]{2,1,0:T(8,128)(2,1)} %bitcast.76), calls=%async_computation.5 | async-start | bytes 4194304 | tf_op jit(solution)/shard_map/all_to_all | solution.py:24
  269.1 16.6 %collective-permute-start.10 = (bf16[128,4096]{1,0:T(8,128)(2,1)}, bf16[128,4096]{1,0:T(8,128)(2,1)S(1)}, u32[]{:S(2)}, u32[]{:S(2)}) collective-permute-start(bf16[128,4096]{1,0:T(8,128)(2,1)} %add_convert_fusion.1), channel_id=1, source_target_pairs={{0,224},{1,33},{32,0},{33,65},{64,32},{65,97},{96,64},{97,129},{12... | collective-permute-start | bytes 3145736 | tf_op jit(solution)/shard_map/ppermute | solution.py:20
  288.6 25.3 %collective-permute-start.11 = (bf16[128,4096]{1,0:T(8,128)(2,1)S(1)}, bf16[128,4096]{1,0:T(8,128)(2,1)S(1)}, u32[]{:S(2)}, u32[]{:S(2)}) collective-permute-start(bf16[128,4096]{1,0:T(8,128)(2,1)S(1)} %add_convert_fusion), channel_id=1, source_target_pairs={{0,224},{1,33},{32,0},{33,65},{64,32},{65,97},{96,64},{97,129},{12... | collective-permute-start | bytes 3145736 | tf_op jit(solution)/shard_map/ppermute | solution.py:20
  316.0 6.3 %collective-permute-start.12 = (bf16[128,2048]{1,0:T(8,128)(2,1)S(1)}, bf16[128,2048]{1,0:T(8,128)(2,1)S(1)}, u32[]{:S(2)}, u32[]{:S(2)}) collective-permute-start(bf16[128,2048]{1,0:T(8,128)(2,1)S(1)} %select_convert_fusion), channel_id=1, source_target_pairs={{0,1},{1,0},{2,3},{3,2},{4,5},{5,4},{6,7},{7,6},{8,9},{9,8},{10,11... | collective-permute-start | bytes 1572872 | tf_op jit(solution)/shard_map/ppermute | solution.py:11

commit v3 on v2

--- a/solution.py
+++ b/solution.py
@@ -1,10 +1,13 @@
 import jax
 import jax.numpy as jnp
 from jax import lax
+from jax.experimental import pallas as pl
+from jax.experimental.pallas import tpu as pltpu
 from jax.sharding import Mesh, PartitionSpec as P
 
 PLANE = (4, 4)
-CUTS = (0, 16, 32, 48)
+CUTS = (0, 16, 24, 48)
+TILE = 1024
 
 
 def swap(array):
@@ -18,6 +21,93 @@
         pairs.append((2 * plane, 2 * ((plane + step) % planes)))
         pairs.append((2 * plane + 1, 2 * ((plane - step) % planes) + 1))
     return lax.ppermute(array, ("z", "tp"), pairs)
+
+
+def expert_kernel(
+    x, gate_a, gate_b, up_a, up_b, down_a, down_b, out,
+    rows_in, into, out_of, rows_out, sums, hidden, into_sems, out_of_sems, done_sems,
+):
+    tiles, tile = into.shape[0], into.shape[1]
+    half = gate_a.shape[1]
+    units = 2 * half
+
+    def inward(k):
+        part = pl.ds(pl.multiple_of(k * tile, tile), tile)
+        copies = [pltpu.make_async_copy(x.at[:, part], rows_in.at[k], into_sems.at[k, 4])]
+        for j, weight in enumerate((gate_a, gate_b, up_a, up_b)):
+            columns = into.at[k, :, pl.ds(j * half, half)]
+            copies.append(pltpu.make_async_copy(weight.at[part, :], columns, into_sems.at[k, j]))
+        return copies
+
+    def outward(k):
+        part = pl.ds(pl.multiple_of(k * tile, tile), tile)
+        return [
+            pltpu.make_async_copy(
+                weight.at[:, part], out_of.at[k, pl.ds(j * half, half), :], out_of_sems.at[k, j]
+            )
+            for j, weight in enumerate((down_a, down_b))
+        ]
+
+    def result(k):
+        part = pl.ds(pl.multiple_of(k * tile, tile), tile)
+        return pltpu.make_async_copy(rows_out.at[k], out.at[:, part], done_sems.at[k])
+
+    for k in range(tiles):
+        for copy in inward(k):
+            copy.start()
+    for k in range(tiles):
+        for copy in outward(k):
+            copy.start()
+    sums[...] = jnp.zeros_like(sums)
+
+    @pl.loop(0, tiles)
+    def _(k):
+        for copy in inward(k):
+            copy.wait()
+        sums[...] += jnp.dot(rows_in[k], into[k], preferred_element_type=jnp.float32)
+
+    gate = sums[:, :units]
+    hidden[...] = (gate / (1.0 + jnp.exp(-gate)) * sums[:, units:]).astype(jnp.bfloat16)
+
+    @pl.loop(0, tiles)
+    def _(k):
+        for copy in outward(k):
+            copy.wait()
+        product = jnp.dot(hidden[...], out_of[k], preferred_element_type=jnp.float32)
+        rows_out[k] = product.astype(jnp.bfloat16)
+        result(k).start()
+
+    for k in range(tiles):
+        result(k).wait()
+
+
+def run_expert(x, gates, ups, downs):
+    rows, width = x.shape
+    half = gates[0].shape[1]
+    tile = min(TILE, width)
+    tiles = width // tile
+    return pl.pallas_call(
+        expert_kernel,
+        in_specs=[pl.BlockSpec(memory_space=pl.ANY)] * 7,
+        out_specs=pl.BlockSpec(memory_space=pl.ANY),
+        out_shape=jax.ShapeDtypeStruct((rows, width), jnp.bfloat16),
+        scratch_shapes=[
+            pltpu.VMEM((tiles, rows, tile), jnp.bfloat16),
+            pltpu.VMEM((tiles, tile, 4 * half), jnp.bfloat16),
+            pltpu.VMEM((tiles, 2 * half, tile), jnp.bfloat16),
+            pltpu.VMEM((tiles, rows, tile), jnp.bfloat16),
+            pltpu.VMEM((rows, 4 * half), jnp.float32),
+            pltpu.VMEM((rows, 2 * half), jnp.bfloat16),
+            pltpu.SemaphoreType.DMA((tiles, 5)),
+            pltpu.SemaphoreType.DMA((tiles, 2)),
+            pltpu.SemaphoreType.DMA((tiles,)),
+        ],
+        compiler_params=pltpu.CompilerParams(vmem_limit_bytes=60 * 1024 * 1024),
+    )(x, *gates, *ups, *downs)
+
+
+def tied(array, *after):
+    return lax.optimization_barrier((array, *after))[0] if after else array
 
 
 def exchange(array):
@@ -44,8 +134,6 @@
     low = jnp.where(core == 0, tokens, received)
     high = jnp.where(core == 0, received, tokens)
     blocks = [jnp.concatenate([low, high, routes], axis=1)]
-    for k in range(far):
-        blocks.append(around(blocks[k], 1))
 
     first = lax.axis_index("z") * plane_experts
     plane_ids = first + jnp.arange(plane_experts, dtype=jnp.int32)
@@ -68,7 +156,13 @@
             named = named & (rank >= 0) & (rank < half_slots)
         return jnp.where(named, rank + starts[k], -1), scale
 
-    placed = [places(k) for k in range(far + 1)]
+    placed = []
+
+    def reach(k, *after):
+        while len(placed) <= k:
+            if placed:
+                blocks.append(around(tied(blocks[-1], *after), 1))
+            placed.append(places(len(placed)))
 
     def within(k, chunk):
         return starts[k] < chunk[1] and chunk[0] < ends[k]
@@ -77,12 +171,13 @@
         slots = jnp.arange(chunk[0], chunk[1], dtype=jnp.int32)
         return placed[k][0][:, None, :] == slots[None, :, None]
 
-    w_gate = jnp.concatenate([gate_weight[0], swap(gate_weight[0])], axis=1)
-    w_up = jnp.concatenate([up_weight[0], swap(up_weight[0])], axis=1)
-    w_down = jnp.concatenate([down_weight[0], swap(down_weight[0])], axis=0)
-
-    arrivals = []
-    for chunk in chunks:
+    def pair(weight):
+        return weight, swap(weight)
+
+    gates, ups, downs = pair(gate_weight[0]), pair(up_weight[0]), pair(down_weight[0])
+
+    def selected(index):
+        chunk = chunks[index]
         rows = plane_experts * (chunk[1] - chunk[0])
         outgoing = 0.0
         for k in range(far + 1):
@@ -91,18 +186,35 @@
                 outgoing += jnp.dot(
                     select, blocks[k][:, :model_width], preferred_element_type=jnp.float32
                 )
-        outgoing = outgoing.astype(jnp.bfloat16).reshape(plane_experts, -1, model_width)
-        arrivals.append(exchange(outgoing))
+        return outgoing.astype(jnp.bfloat16).reshape(plane_experts, -1, model_width)
+
+    def expert(arrived):
+        produced = run_expert(arrived.reshape(-1, model_width), gates, ups, downs)
+        return produced.reshape(plane_experts, -1, model_width)
+
+    def last_block(index):
+        return max(k for k in range(far + 1) if within(k, chunks[index]))
+
+    reach(last_block(0))
+    outgoing = [selected(0)]
+    reach(2)
+    reach(3, outgoing[0])
+    arrived = [exchange(outgoing[0])]
+    for index in range(1, len(chunks)):
+        reach(last_block(index), arrived[0], *outgoing)
+        outgoing.append(selected(index))
+        arrived.append(exchange(outgoing[index]))
+    produced = []
+    for index in range(len(chunks)):
+        here = tied(arrived[index], *arrived[index + 1 : len(chunks) - 1])
+        produced.append(expert(here))
 
     returns = [None] * len(chunks)
+    before_it = tuple(produced[:-1])
     for index in reversed(range(len(chunks))):
-        arrived = arrivals[index].reshape(-1, model_width)
-        gate_values = jnp.dot(arrived, w_gate, preferred_element_type=jnp.float32)
-        up_values = jnp.dot(arrived, w_up, preferred_element_type=jnp.float32)
-        hidden = (jax.nn.silu(gate_values) * up_values).astype(jnp.bfloat16)
-        produced = jnp.dot(hidden, w_down, preferred_element_type=jnp.float32)
-        produced = produced.astype(jnp.bfloat16).reshape(plane_experts, -1, model_width)
-        returns[index] = exchange(produced).reshape(-1, model_width)
+        returns[index] = exchange(tied(produced[index], *before_it))
+        before_it = (returns[index],)
+    returns = [one.reshape(-1, model_width) for one in returns]
 
     total = 0.0
     for k in reversed(range(far + 1)):

time: 324 us -> 291 us (0.90)
  matrix products: 77.8 us -> 28.1 us
  Pallas kernels: 0 us -> 34.2 us
  starting transfers between devices: 76.6 us -> 51.1 us
  waiting for transfers between devices: 156 us -> 162 us
    dot_general x13 -> x7, matrix products: 63.3 us -> 13.2 us  [selected(): jnp.dot(select, blocks[k][:, :model_width], preferred_element_type=jnp.fl...]
    pallas_call x0 -> x3, Pallas kernels: none -> 34.2 us  [run_expert(): pl.pallas_call(expert_kernel, in_specs=[pl.BlockSpec(memory_space=pl.ANY)...]
    ppermute x8, starting transfers between devices: 26.8 us -> 10.4 us  [around(): return lax.ppermute(array, ('z', 'tp'), pairs)]
    all_to_all x6, waiting for transfers between devices: 63.1 us -> 79.3 us  [exchange(): lax.all_to_all(array, ('y', 'x'), split_axis=0, concat_axis=0, tiled=True)]
    ppermute x8, waiting for transfers between devices: 90.9 us -> 80.8 us  [around(): return lax.ppermute(array, ('z', 'tp'), pairs)]
    all_to_all x6, starting transfers between devices: 35.7 us -> 30.1 us  [exchange(): lax.all_to_all(array, ('y', 'x'), split_axis=0, concat_axis=0, tiled=True)]
    ppermute x5, starting transfers between devices: 14.2 us -> 10.6 us  [swap(): return lax.ppermute(array, 'tp', [(0, 1), (1, 0)])]
  transfers between devices with their start and end apart: 19 -> 19, of which waited for: 16 -> 14; matrix products, arithmetic and copies ran while one was open for 23% -> 11% of each run, Pallas kernels for 0% -> 7%
where the time goes in v3:
time: 291 us; the launch traced here: 287 us
  waiting for transfers between devices  162 us (56%)
  starting transfers between devices  51.1 us (18%)
  Pallas kernels  34.2 us (12%)
  matrix products  28.1 us (10%)
  other arithmetic  11.3 us (4%)
    ppermute x8, waiting for transfers between devices, around(): return lax.ppermute(array, ('z', 'tp'), pairs)  80.8 us
    all_to_all x6, waiting for transfers between devices, exchange(): lax.all_to_all(array, ('y', 'x'), split_axis=0, concat_axis=0, tiled=True)  79.3 us
    pallas_call x3, Pallas kernels, run_expert(): pl.pallas_call(expert_kernel, in_specs=[pl.BlockSpec(memory_space=pl.ANY)...  34.2 us
    all_to_all x6, starting transfers between devices, exchange(): lax.all_to_all(array, ('y', 'x'), split_axis=0, concat_axis=0, tiled=True)  30.1 us
    dot_general x7, matrix products, on_device(): lax.dot_general(mix, returns[index], (((0,), (0,)), ((), ())), preferred_...  14.1 us
    dot_general x7, matrix products, selected(): jnp.dot(select, blocks[k][:, :model_width], preferred_element_type=jnp.fl...  13.2 us
    ppermute x5, starting transfers between devices, swap(): return lax.ppermute(array, 'tp', [(0, 1), (1, 0)])  10.6 us
    ppermute x8, starting transfers between devices, around(): return lax.ppermute(array, ('z', 'tp'), pairs)  10.4 us
  transfers between devices with their start and end apart: 19, of which 14 were waited for; matrix products, arithmetic and copies ran while one was open for 11% of the time, Pallas kernels for 7%

profile of v3, /device:TPU:1, one launch (start us, length us, event | category | flops | bytes accessed | tf_op | source)
XLA Modules:
  0.0 287.3 jit_solution(13094185958261209391)
XLA Ops:
  0.0 3.2 %collective-permute-start = (bf16[128,2048]{1,0:T(8,128)(2,1)}, bf16[128,2048]{1,0:T(8,128)(2,1)S(1)}, u32[]{:S(2)}, u32[]{:S(2)}) collective-permute-start(bf16[128,2048]{1,0:T(8,128)(2,1)} %param.6), channel_id=1, source_target_pairs={{0,1},{1,0},{2,3},{3,2},{4,5},{5,4},{6,7},{7,6},{8,9},{9,8},{10,11... | collective-permute-start | bytes 1572872 | tf_op jit(solution)/shard_map/ppermute | solution.py:14
  6.2 3.9 %collective-permute-start.1 = (bf16[128,4224]{1,0:T(8,128)(2,1)S(1)}, bf16[128,4224]{1,0:T(8,128)(2,1)S(1)}, u32[]{:S(2)}, u32[]{:S(2)}) collective-permute-start(bf16[128,4224]{1,0:T(8,128)(2,1)S(1)} %fusion.13), channel_id=1, source_target_pairs={{0,32},{1,225},{32,64},{33,1},{64,96},{65,33},{96,128},{97,65},{12... | collective-permute-start | bytes 3244040 | tf_op jit(solution)/shard_map/ppermute | solution.py:23
  10.2 12.0 %collective-permute-done.1 = bf16[128,4224]{1,0:T(8,128)(2,1)S(1)} collective-permute-done((bf16[128,4224]{1,0:T(8,128)(2,1)S(1)}, bf16[128,4224]{1,0:T(8,128)(2,1)S(1)}, u32[]{:S(2)}, u32[]{:S(2)}) %collective-permute-start.1) | collective-permute-done | bytes 1081376 | tf_op jit(solution)/shard_map/ppermute | solution.py:23
  22.3 3.2 %collective-permute-start.2 = (bf16[128,4224]{1,0:T(8,128)(2,1)S(1)}, bf16[128,4224]{1,0:T(8,128)(2,1)S(1)}, u32[]{:S(2)}, u32[]{:S(2)}) collective-permute-start(bf16[128,4224]{1,0:T(8,128)(2,1)S(1)} %collective-permute-done.1), channel_id=1, source_target_pairs={{0,32},{1,225},{32,64},{33,1},{64,96},{65,33},{96,128},{97,65},{12... | collective-permute-start | bytes 3244040 | tf_op jit(solution)/shard_map/ppermute | solution.py:23
  28.7 6.8 %all-to-all-start = ((bf16[16,16,4096]{2,1,0:T(8,128)(2,1)}), bf16[16,16,4096]{2,1,0:T(8,128)(2,1)}, u32[]{:S(2)}, u32[]{:S(2)}) async-start(bf16[16,16,4096]{2,1,0:T(8,128)(2,1)} %bitcast.3), calls=%async_computation | async-start | bytes 4194304 | tf_op jit(solution)/shard_map/all_to_all | solution.py:114
  41.3 11.5 %collective-permute-done.3 = bf16[128,4224]{1,0:T(8,128)(2,1)} collective-permute-done((bf16[128,4224]{1,0:T(8,128)(2,1)S(1)}, bf16[128,4224]{1,0:T(8,128)(2,1)}, u32[]{:S(2)}, u32[]{:S(2)}) %collective-permute-start.3) | collective-permute-done | bytes 1081376 | tf_op jit(solution)/shard_map/ppermute | solution.py:23
  56.7 12.1 %all-to-all-done = bf16[16,16,4096]{2,1,0:T(8,128)(2,1)} async-done(((bf16[16,16,4096]{2,1,0:T(8,128)(2,1)}), bf16[16,16,4096]{2,1,0:T(8,128)(2,1)}, u32[]{:S(2)}, u32[]{:S(2)}) %all-to-all-start) | async-done | bytes 2097184 | tf_op jit(solution)/shard_map/all_to_all | solution.py:114
  69.5 4.3 %all-to-all-start.2 = ((bf16[16,8,4096]{2,1,0:T(8,128)(2,1)}), bf16[16,8,4096]{2,1,0:T(8,128)(2,1)}, u32[]{:S(2)}, u32[]{:S(2)}) async-start(bf16[16,8,4096]{2,1,0:T(8,128)(2,1)} %fusion.3), calls=%async_computation.2 | async-start | bytes 2097152 | tf_op jit(solution)/shard_map/all_to_all | solution.py:114
  74.0 9.4 %collective-permute-done.4 = bf16[128,4224]{1,0:T(8,128)(2,1)} collective-permute-done((bf16[128,4224]{1,0:T(8,128)(2,1)}, bf16[128,4224]{1,0:T(8,128)(2,1)}, u32[]{:S(2)}, u32[]{:S(2)}) %collective-permute-start.4) | collective-permute-done | bytes 1081376 | tf_op jit(solution)/shard_map/ppermute | solution.py:23
  91.6 4.7 %all-to-all-start.1 = ((bf16[16,24,4096]{2,1,0:T(8,128)(2,1)}), bf16[16,24,4096]{2,1,0:T(8,128)(2,1)}, u32[]{:S(2)}, u32[]{:S(2)}) async-start(bf16[16,24,4096]{2,1,0:T(8,128)(2,1)} %bitcast.83), calls=%async_computation.1 | async-start | bytes 6291456 | tf_op jit(solution)/shard_map/all_to_all | solution.py:114
  96.3 11.4 %shard_map.65 = bf16[256,4096]{1,0:T(8,128)(2,1)} custom-call(bf16[256,4096]{1,0:T(8,128)(2,1)} %bitcast.16.x, bf16[4096,384]{1,0:T(8,128)(2,1)} %bitcast.70, bf16[4096,384]{1,0:T(8,128)(2,1)} %collective-permute-done.5.gate_b, bf16[4096,384]{1,0:T(8,128)(2,1)} %bitcast.75, bf16[4096,384]{1,0:T(8,128)(2,1)} %collective-permute-done.6.up_b, ...), custom_call_target="tpu_custom_call" | custom-call | tf_op jit(solution)/shard_map/pallas_call | solution.py:89
  107.7 9.8 %shard_map.66 = bf16[128,4096]{1,0:T(8,128)(2,1)} custom-call(bf16[128,4096]{1,0:T(8,128)(2,1)} %bitcast.18.x, bf16[4096,384]{1,0:T(8,128)(2,1)} %bitcast.71, bf16[4096,384]{1,0:T(8,128)(2,1)} %collective-permute-done.5.gate_b, bf16[4096,384]{1,0:T(8,128)(2,1)} %bitcast.76, bf16[4096,384]{1,0:T(8,128)(2,1)} %collective-permute-done.6.up_b, ...), custom_call_target="tpu_custom_call" | custom-call | tf_op jit(solution)/shard_map/pallas_call | solution.py:89
  117.5 21.4 %all-to-all-done.1 = bf16[16,24,4096]{2,1,0:T(8,128)(2,1)} async-done(((bf16[16,24,4096]{2,1,0:T(8,128)(2,1)}), bf16[16,24,4096]{2,1,0:T(8,128)(2,1)}, u32[]{:S(2)}, u32[]{:S(2)}) %all-to-all-start.1) | async-done | bytes 3145760 | tf_op jit(solution)/shard_map/all_to_all | solution.py:114
  138.9 13.1 %shard_map.64 = bf16[384,4096]{1,0:T(8,128)(2,1)} custom-call(bf16[384,4096]{1,0:T(8,128)(2,1)} %bitcast.11.x, bf16[4096,384]{1,0:T(8,128)(2,1)} %bitcast.72, bf16[4096,384]{1,0:T(8,128)(2,1)} %collective-permute-done.5.gate_b, bf16[4096,384]{1,0:T(8,128)(2,1)} %bitcast.77, bf16[4096,384]{1,0:T(8,128)(2,1)} %collective-permute-done.6.up_b, ...), custom_call_target="tpu_custom_call" | custom-call | tf_op jit(solution)/shard_map/pallas_call | solution.py:89
  152.0 5.0 %all-to-all-start.3 = ((bf16[16,24,4096]{2,1,0:T(8,128)(2,1)}), bf16[16,24,4096]{2,1,0:T(8,128)(2,1)S(1)}, u32[]{:S(2)}, u32[]{:S(2)}) async-start(bf16[16,24,4096]{2,1,0:T(8,128)(2,1)} %bitcast.82), calls=%async_computation.3 | async-start | bytes 6291456 | tf_op jit(solution)/shard_map/all_to_all | solution.py:114
  162.7 37.4 %all-to-all-done.3 = bf16[16,24,4096]{2,1,0:T(8,128)(2,1)S(1)} async-done(((bf16[16,24,4096]{2,1,0:T(8,128)(2,1)}), bf16[16,24,4096]{2,1,0:T(8,128)(2,1)S(1)}, u32[]{:S(2)}, u32[]{:S(2)}) %all-to-all-start.3) | async-done | bytes 3145760 | tf_op jit(solution)/shard_map/all_to_all | solution.py:114
  201.9 4.8 %all-to-all-start.4 = ((bf16[16,8,4096]{2,1,0:T(8,128)(2,1)}), bf16[16,8,4096]{2,1,0:T(8,128)(2,1)}, u32[]{:S(2)}, u32[]{:S(2)}) async-start(bf16[16,8,4096]{2,1,0:T(8,128)(2,1)} %bitcast.85), calls=%async_computation.4 | async-start | bytes 2097152 | tf_op jit(solution)/shard_map/all_to_all | solution.py:114
  206.8 16.3 %collective-permute-done.8 = bf16[128,4096]{1,0:T(8,128)(2,1)} collective-permute-done((bf16[128,4096]{1,0:T(8,128)(2,1)}, bf16[128,4096]{1,0:T(8,128)(2,1)}, u32[]{:S(2)}, u32[]{:S(2)}) %collective-permute-start.8) | collective-permute-done | bytes 1048608 | tf_op jit(solution)/shard_map/ppermute | solution.py:23
  226.1 4.4 %all-to-all-start.5 = ((bf16[16,16,4096]{2,1,0:T(8,128)(2,1)}), bf16[16,16,4096]{2,1,0:T(8,128)(2,1)}, u32[]{:S(2)}, u32[]{:S(2)}) async-start(bf16[16,16,4096]{2,1,0:T(8,128)(2,1)} %bitcast.84), calls=%async_computation.5 | async-start | bytes 4194304 | tf_op jit(solution)/shard_map/all_to_all | solution.py:114
  231.3 9.9 %collective-permute-done.9 = bf16[128,4096]{1,0:T(8,128)(2,1)} collective-permute-done((bf16[128,4096]{1,0:T(8,128)(2,1)}, bf16[128,4096]{1,0:T(8,128)(2,1)}, u32[]{:S(2)}, u32[]{:S(2)}) %collective-permute-start.9) | collective-permute-done | bytes 1048608 | tf_op jit(solution)/shard_map/ppermute | solution.py:23
  245.3 8.4 %all-to-all-done.5 = bf16[16,16,4096]{2,1,0:T(8,128)(2,1)} async-done(((bf16[16,16,4096]{2,1,0:T(8,128)(2,1)}), bf16[16,16,4096]{2,1,0:T(8,128)(2,1)}, u32[]{:S(2)}, u32[]{:S(2)}) %all-to-all-start.5) | async-done | bytes 2097184 | tf_op jit(solution)/shard_map/all_to_all | solution.py:114
  253.7 4.8 %collective-permute-done.10 = bf16[128,4096]{1,0:T(8,128)(2,1)} collective-permute-done((bf16[128,4096]{1,0:T(8,128)(2,1)S(1)}, bf16[128,4096]{1,0:T(8,128)(2,1)}, u32[]{:S(2)}, u32[]{:S(2)}) %collective-permute-start.10) | collective-permute-done | bytes 1048608 | tf_op jit(solution)/shard_map/ppermute | solution.py:23
  261.0 14.8 %collective-permute-done.11 = bf16[128,4096]{1,0:T(8,128)(2,1)S(1)} collective-permute-done((bf16[128,4096]{1,0:T(8,128)(2,1)S(1)}, bf16[128,4096]{1,0:T(8,128)(2,1)S(1)}, u32[]{:S(2)}, u32[]{:S(2)}) %collective-permute-start.11) | collective-permute-done | bytes 1048608 | tf_op jit(solution)/shard_map/ppermute | solution.py:23
  278.0 6.7 %collective-permute-start.12 = (bf16[128,2048]{1,0:T(8,128)(2,1)S(1)}, bf16[128,2048]{1,0:T(8,128)(2,1)S(1)}, u32[]{:S(2)}, u32[]{:S(2)}) collective-permute-start(bf16[128,2048]{1,0:T(8,128)(2,1)S(1)} %select_convert_fusion), channel_id=1, source_target_pairs={{0,1},{1,0},{2,3},{3,2},{4,5},{5,4},{6,7},{7,6},{8,9},{9,8},{10,11... | collective-permute-start | bytes 1572872 | tf_op jit(solution)/shard_map/ppermute | solution.py:14
  (81 shorter events, 47.6 us)
Async XLA Ops:
  0.0 5.0 %collective-permute-start = (bf16[128,2048]{1,0:T(8,128)(2,1)}, bf16[128,2048]{1,0:T(8,128)(2,1)S(1)}, u32[]{:S(2)}, u32[]{:S(2)}) collective-permute-start(bf16[128,2048]{1,0:T(8,128)(2,1)} %param.6), channel_id=1, source_target_pairs={{0,1},{1,0},{2,3},{3,2},{4,5},{5,4},{6,7},{7,6},{8,9},{9,8},{10,11... | collective-permute-start | bytes 1572872 | tf_op jit(solution)/shard_map/ppermute | solution.py:14
  6.2 16.0 %collective-permute-start.1 = (bf16[128,4224]{1,0:T(8,128)(2,1)S(1)}, bf16[128,4224]{1,0:T(8,128)(2,1)S(1)}, u32[]{:S(2)}, u32[]{:S(2)}) collective-permute-start(bf16[128,4224]{1,0:T(8,128)(2,1)S(1)} %fusion.13), channel_id=1, source_target_pairs={{0,32},{1,225},{32,64},{33,1},{64,96},{65,33},{96,128},{97,65},{12... | collective-permute-start | bytes 3244040 | tf_op jit(solution)/shard_map/ppermute | solution.py:23
  22.2 18.6 %copy-start.3 = (bf16[128,4224]{1,0:T(8,128)(2,1)}, bf16[128,4224]{1,0:T(8,128)(2,1)S(1)}, u32[]{:S(2)}) copy-start(bf16[128,4224]{1,0:T(8,128)(2,1)S(1)} %collective-permute-done.1) | copy-start | bytes 3244036
  22.3 15.3 %collective-permute-start.2 = (bf16[128,4224]{1,0:T(8,128)(2,1)S(1)}, bf16[128,4224]{1,0:T(8,128)(2,1)S(1)}, u32[]{:S(2)}, u32[]{:S(2)}) collective-permute-start(bf16[128,4224]{1,0:T(8,128)(2,1)S(1)} %collective-permute-done.1), channel_id=1, source_target_pairs={{0,32},{1,225},{32,64},{33,1},{64,96},{65,33},{96,128},{97,65},{12... | collective-permute-start | bytes 3244040 | tf_op jit(solution)/shard_map/ppermute | solution.py:23
  28.7 40.1 %all-to-all-start = ((bf16[16,16,4096]{2,1,0:T(8,128)(2,1)}), bf16[16,16,4096]{2,1,0:T(8,128)(2,1)}, u32[]{:S(2)}, u32[]{:S(2)}) async-start(bf16[16,16,4096]{2,1,0:T(8,128)(2,1)} %bitcast.3), calls=%async_computation | async-start | bytes 4194304 | tf_op jit(solution)/shard_map/all_to_all | solution.py:114
  37.6 16.0 %copy-start.1 = (bf16[128,4224]{1,0:T(8,128)(2,1)}, bf16[128,4224]{1,0:T(8,128)(2,1)S(1)}, u32[]{:S(2)}) copy-start(bf16[128,4224]{1,0:T(8,128)(2,1)S(1)} %collective-permute-done.2) | copy-start | bytes 3244036
  37.6 15.2 %collective-permute-start.3 = (bf16[128,4224]{1,0:T(8,128)(2,1)S(1)}, bf16[128,4224]{1,0:T(8,128)(2,1)}, u32[]{:S(2)}, u32[]{:S(2)}) collective-permute-start(bf16[128,4224]{1,0:T(8,128)(2,1)S(1)} %collective-permute-done.2), channel_id=1, source_target_pairs={{0,32},{1,225},{32,64},{33,1},{64,96},{65,33},{96,128},{97,65},{12... | collective-permute-start | bytes 3244040 | tf_op jit(solution)/shard_map/ppermute | solution.py:23
  53.8 15.0 %copy-start = (bf16[1,4096,384]{2,1,0:T(8,128)(2,1)S(1)}, bf16[1,4096,384]{2,1,0:T(8,128)(2,1)}, u32[]{:S(2)}) copy-start(bf16[1,4096,384]{2,1,0:T(8,128)(2,1)} %param.9) | copy-start | bytes 9437188
  68.8 14.6 %collective-permute-start.4 = (bf16[128,4224]{1,0:T(8,128)(2,1)}, bf16[128,4224]{1,0:T(8,128)(2,1)}, u32[]{:S(2)}, u32[]{:S(2)}) collective-permute-start(bf16[128,4224]{1,0:T(8,128)(2,1)} %collective-permute-done.3), channel_id=1, source_target_pairs={{0,32},{1,225},{32,64},{33,1},{64,96},{65,33},{96,128},{97,65},{12... | collective-permute-start | bytes 3244040 | tf_op jit(solution)/shard_map/ppermute | solution.py:23
  68.8 27.5 %collective-permute-start.5 = (bf16[4096,384]{1,0:T(8,128)(2,1)S(1)}, bf16[4096,384]{1,0:T(8,128)(2,1)}, u32[]{:S(2)}, u32[]{:S(2)}) collective-permute-start(bf16[4096,384]{1,0:T(8,128)(2,1)S(1)} %bitcast.73), channel_id=1, source_target_pairs={{0,1},{1,0},{2,3},{3,2},{4,5},{5,4},{6,7},{7,6},{8,9},{9,8},{10,11... | collective-permute-start | bytes 9437192 | tf_op jit(solution)/shard_map/ppermute | solution.py:14
  68.9 27.5 %collective-permute-start.6 = (bf16[4096,384]{1,0:T(8,128)(2,1)}, bf16[4096,384]{1,0:T(8,128)(2,1)}, u32[]{:S(2)}, u32[]{:S(2)}) collective-permute-start(bf16[4096,384]{1,0:T(8,128)(2,1)} %bitcast.74), channel_id=1, source_target_pairs={{0,1},{1,0},{2,3},{3,2},{4,5},{5,4},{6,7},{7,6},{8,9},{9,8},{10,11... | collective-permute-start | bytes 9437192 | tf_op jit(solution)/shard_map/ppermute | solution.py:14
  69.3 27.0 %collective-permute-start.7 = (bf16[384,4096]{1,0:T(8,128)(2,1)}, bf16[384,4096]{1,0:T(8,128)(2,1)}, u32[]{:S(2)}, u32[]{:S(2)}) collective-permute-start(bf16[384,4096]{1,0:T(8,128)(2,1)} %bitcast.78), channel_id=1, source_target_pairs={{0,1},{1,0},{2,3},{3,2},{4,5},{5,4},{6,7},{7,6},{8,9},{9,8},{10,11... | collective-permute-start | bytes 9437192 | tf_op jit(solution)/shard_map/ppermute | solution.py:14
  69.5 22.1 %all-to-all-start.2 = ((bf16[16,8,4096]{2,1,0:T(8,128)(2,1)}), bf16[16,8,4096]{2,1,0:T(8,128)(2,1)}, u32[]{:S(2)}, u32[]{:S(2)}) async-start(bf16[16,8,4096]{2,1,0:T(8,128)(2,1)} %fusion.3), calls=%async_computation.2 | async-start | bytes 2097152 | tf_op jit(solution)/shard_map/all_to_all | solution.py:114
  86.7 2.3 copy-start.2
  91.6 47.3 %all-to-all-start.1 = ((bf16[16,24,4096]{2,1,0:T(8,128)(2,1)}), bf16[16,24,4096]{2,1,0:T(8,128)(2,1)}, u32[]{:S(2)}, u32[]{:S(2)}) async-start(bf16[16,24,4096]{2,1,0:T(8,128)(2,1)} %bitcast.83), calls=%async_computation.1 | async-start | bytes 6291456 | tf_op jit(solution)/shard_map/all_to_all | solution.py:114
  152.0 48.1 %all-to-all-start.3 = ((bf16[16,24,4096]{2,1,0:T(8,128)(2,1)}), bf16[16,24,4096]{2,1,0:T(8,128)(2,1)S(1)}, u32[]{:S(2)}, u32[]{:S(2)}) async-start(bf16[16,24,4096]{2,1,0:T(8,128)(2,1)} %bitcast.82), calls=%async_computation.3 | async-start | bytes 6291456 | tf_op jit(solution)/shard_map/all_to_all | solution.py:114
  201.9 21.1 %collective-permute-start.8 = (bf16[128,4096]{1,0:T(8,128)(2,1)}, bf16[128,4096]{1,0:T(8,128)(2,1)}, u32[]{:S(2)}, u32[]{:S(2)}) collective-permute-start(bf16[128,4096]{1,0:T(8,128)(2,1)} %fusion.2), channel_id=1, source_target_pairs={{0,224},{1,33},{32,0},{33,65},{64,32},{65,97},{96,64},{97,129},{12... | collective-permute-start | bytes 3145736 | tf_op jit(solution)/shard_map/ppermute | solution.py:23
  201.9 24.1 %all-to-all-start.4 = ((bf16[16,8,4096]{2,1,0:T(8,128)(2,1)}), bf16[16,8,4096]{2,1,0:T(8,128)(2,1)}, u32[]{:S(2)}, u32[]{:S(2)}) async-start(bf16[16,8,4096]{2,1,0:T(8,128)(2,1)} %bitcast.85), calls=%async_computation.4 | async-start | bytes 2097152 | tf_op jit(solution)/shard_map/all_to_all | solution.py:114
  226.1 15.2 %collective-permute-start.9 = (bf16[128,4096]{1,0:T(8,128)(2,1)}, bf16[128,4096]{1,0:T(8,128)(2,1)}, u32[]{:S(2)}, u32[]{:S(2)}) collective-permute-start(bf16[128,4096]{1,0:T(8,128)(2,1)} %add_convert_fusion.3), channel_id=1, source_target_pairs={{0,224},{1,33},{32,0},{33,65},{64,32},{65,97},{96,64},{97,129},{12... | collective-permute-start | bytes 3145736 | tf_op jit(solution)/shard_map/ppermute | solution.py:23
  226.1 27.6 %all-to-all-start.5 = ((bf16[16,16,4096]{2,1,0:T(8,128)(2,1)}), bf16[16,16,4096]{2,1,0:T(8,128)(2,1)}, u32[]{:S(2)}, u32[]{:S(2)}) async-start(bf16[16,16,4096]{2,1,0:T(8,128)(2,1)} %bitcast.84), calls=%async_computation.5 | async-start | bytes 4194304 | tf_op jit(solution)/shard_map/all_to_all | solution.py:114
  243.4 15.0 %collective-permute-start.10 = (bf16[128,4096]{1,0:T(8,128)(2,1)S(1)}, bf16[128,4096]{1,0:T(8,128)(2,1)}, u32[]{:S(2)}, u32[]{:S(2)}) collective-permute-start(bf16[128,4096]{1,0:T(8,128)(2,1)S(1)} %add_convert_fusion.2), channel_id=1, source_target_pairs={{0,224},{1,33},{32,0},{33,65},{64,32},{65,97},{96,64},{97,129},{12... | collective-permute-start | bytes 3145736 | tf_op jit(solution)/shard_map/ppermute | solution.py:23
  260.9 14.9 %collective-permute-start.11 = (bf16[128,4096]{1,0:T(8,128)(2,1)S(1)}, bf16[128,4096]{1,0:T(8,128)(2,1)S(1)}, u32[]{:S(2)}, u32[]{:S(2)}) collective-permute-start(bf16[128,4096]{1,0:T(8,128)(2,1)S(1)} %add_convert_fusion.1), channel_id=1, source_target_pairs={{0,224},{1,33},{32,0},{33,65},{64,32},{65,97},{96,64},{97,129},{12... | collective-permute-start | bytes 3145736 | tf_op jit(solution)/shard_map/ppermute | solution.py:23
  278.0 8.3 %collective-permute-start.12 = (bf16[128,2048]{1,0:T(8,128)(2,1)S(1)}, bf16[128,2048]{1,0:T(8,128)(2,1)S(1)}, u32[]{:S(2)}, u32[]{:S(2)}) collective-permute-start(bf16[128,2048]{1,0:T(8,128)(2,1)S(1)} %select_convert_fusion), channel_id=1, source_target_pairs={{0,1},{1,0},{2,3},{3,2},{4,5},{5,4},{6,7},{7,6},{8,9},{9,8},{10,11... | collective-permute-start | bytes 1572872 | tf_op jit(solution)/shard_map/ppermute | solution.py:14

commit v4 on v3

v4 whole, which is shorter than its diff:
```python
import functools

import jax
import jax.numpy as jnp
from jax import lax
from jax.experimental import pallas as pl
from jax.experimental.pallas import tpu as pltpu
from jax.sharding import Mesh, PartitionSpec as P

PLANE = (4, 4)
CHUNKS = ((0,), (1,), (2,), (3, 4))
TILES = 4
AFTER_SELECTED = {3: 1}
WITH_ARRIVED = {1: 0, 3: 1, 4: 2}


def swap(array):
    return lax.ppermute(array, "tp", [(0, 1), (1, 0)])


def around(array, step):
    planes = lax.axis_size("z")
    pairs = []
    for plane in range(planes):
        pairs.append((2 * plane, 2 * ((plane + step) % planes)))
        pairs.append((2 * plane + 1, 2 * ((plane - step) % planes) + 1))
    return lax.ppermute(array, ("z", "tp"), pairs)


def expert_kernel(pieces, *refs):
    count = len(pieces)
    inputs, refs = refs[:count], refs[count:]
    gate_a, gate_b, up_a, up_b, down_a, down_b = refs[:6]
    outputs, refs = refs[6 : 6 + count], refs[6 + count :]
    rows_in, into, out_of, rows_out, sums, hidden, in_sems, into_sems, out_of_sems, done_sems = refs
    tiles, tile = into.shape[0], into.shape[1]
    half = gate_a.shape[1]
    units = 2 * half
    spots, first = [], 0
    for array, (groups, rows) in enumerate(pieces):
        for group in range(groups):
            spots.append((array, group, pl.ds(first, rows)))
            first += rows

    def inward(k):
        part = pl.ds(pl.multiple_of(k * tile, tile), tile)
        copies = []
        for j, (array, group, spot) in enumerate(spots):
            source = inputs[array].at[group, k]
            copies.append(pltpu.make_async_copy(source, rows_in.at[k, spot], in_sems.at[k, j]))
        for j, weight in enumerate((gate_a, gate_b, up_a, up_b)):
            columns = into.at[k, :, pl.ds(j * half, half)]
            copies.append(pltpu.make_async_copy(weight.at[part, :], columns, into_sems.at[k, j]))
        return copies

    def outward(k):
        part = pl.ds(pl.multiple_of(k * tile, tile), tile)
        return [
            pltpu.make_async_copy(
                weight.at[:, part], out_of.at[k, pl.ds(j * half, half), :], out_of_sems.at[k, j]
            )
            for j, weight in enumerate((down_a, down_b))
        ]

    def results(k):
        return [
            pltpu.make_async_copy(
                rows_out.at[k, spot], outputs[array].at[group, k], done_sems.at[k, j]
            )
            for j, (array, group, spot) in enumerate(spots)
        ]

    for k in range(tiles):
        for copy in inward(k):
            copy.start()
    for k in range(tiles):
        for copy in outward(k):
            copy.start()
    sums[...] = jnp.zeros_like(sums)

    @pl.loop(0, tiles)
    def _(k):
        for copy in inward(k):
            copy.wait()
        sums[...] += jnp.dot(rows_in[k], into[k], preferred_element_type=jnp.float32)

    gate = sums[:, :units]
    hidden[...] = (gate / (1.0 + jnp.exp(-gate)) * sums[:, units:]).astype(jnp.bfloat16)

    @pl.loop(0, tiles)
    def _(k):
        for copy in outward(k):
            copy.wait()
        product = jnp.dot(hidden[...], out_of[k], preferred_element_type=jnp.float32)
        rows_out[k] = product.astype(jnp.bfloat16)
        for copy in results(k):
            copy.start()

    for k in range(tiles):
        for copy in results(k):
            copy.wait()


def run_expert(arrays, gates, ups, downs):
    tiles, tile = arrays[0].shape[1], arrays[0].shape[3]
    pieces = [(array.shape[0], array.shape[2]) for array in arrays]
    rows = sum(groups * held for groups, held in pieces)
    spots = sum(groups for groups, held in pieces)
    half = gates[0].shape[1]
    return pl.pallas_call(
        functools.partial(expert_kernel, pieces),
        in_specs=[pl.BlockSpec(memory_space=pl.ANY)] * (len(arrays) + 6),
        out_specs=[pl.BlockSpec(memory_space=pl.ANY)] * len(arrays),
        out_shape=[jax.ShapeDtypeStruct(array.shape, jnp.bfloat16) for array in arrays],
        scratch_shapes=[
            pltpu.VMEM((tiles, rows, tile), jnp.bfloat16),
            pltpu.VMEM((tiles, tile, 4 * half), jnp.bfloat16),
            pltpu.VMEM((tiles, 2 * half, tile), jnp.bfloat16),
            pltpu.VMEM((tiles, rows, tile), jnp.bfloat16),
            pltpu.VMEM((rows, 4 * half), jnp.float32),
            pltpu.VMEM((rows, 2 * half), jnp.bfloat16),
            pltpu.SemaphoreType.DMA((tiles, spots)),
            pltpu.SemaphoreType.DMA((tiles, 4)),
            pltpu.SemaphoreType.DMA((tiles, 2)),
            pltpu.SemaphoreType.DMA((tiles, spots)),
        ],
        compiler_params=pltpu.CompilerParams(vmem_limit_bytes=60 * 1024 * 1024),
    )(*arrays, *gates, *ups, *downs)


def tied(array, *after):
    return lax.optimization_barrier((array, *after))[0] if after else array


def exchange(array):
    return lax.all_to_all(array, ("y", "x"), split_axis=0, concat_axis=0, tiled=True)


def on_device(tokens, expert_ids, gate_levels, gate_weight, up_weight, down_weight):
    planes = lax.axis_size("z")
    plane_experts = lax.axis_size("y") * lax.axis_size("x")
    core = lax.axis_index("tp")
    tok_count, top_count = expert_ids.shape
    half_width = tokens.shape[1]
    tile = 2 * half_width // TILES
    capacity = 3 * tok_count * top_count // (2 * planes * plane_experts)
    far = planes // 2
    slots = [capacity // 2 if k in (0, far) else capacity for k in range(far + 1)]
    group = plane_experts // 2
    tall = TILES * tok_count

    routes = jnp.concatenate([expert_ids, gate_levels], axis=1).T.astype(jnp.bfloat16)
    routes = jnp.pad(routes, ((0, 0), (0, tile - tok_count)))
    received = swap(tokens)
    low = jnp.where(core == 0, tokens, received)
    high = jnp.where(core == 0, received, tokens)
    parts = [
        array[:, first : first + tile]
        for array in (low, high)
        for first in range(0, half_width, tile)
    ]
    blocks = [jnp.concatenate([*parts, routes], axis=0)]

    first = lax.axis_index("z") * plane_experts
    plane_ids = first + jnp.arange(plane_experts, dtype=jnp.int32)
    order = jnp.arange(tok_count)
    before = (order[:, None] < order[None, :]).astype(jnp.bfloat16)

    def places(k):
        table = blocks[k][tall:, :tok_count]
        ids = table[:top_count].astype(jnp.int32)
        levels = table[top_count:].astype(jnp.float32)
        weights = levels / jnp.sum(levels, axis=0, keepdims=True)
        hits = ids[None, :, :] == plane_ids[:, None, None]
        named = jnp.any(hits, axis=1)
        scale = jnp.sum(jnp.where(hits, weights[None, :, :], 0.0), axis=1)
        rank = jnp.dot(
            named.astype(jnp.bfloat16), before, preferred_element_type=jnp.float32
        ).astype(jnp.int32)
        if k in (0, far):
            rank = rank - core * slots[k]
            named = named & (rank >= 0) & (rank < slots[k])
        return jnp.where(named, rank, -TILES * planes * capacity), scale

    placed = []

    def fits(k, chunk):
        held = sum(slots[j] for j in chunk)
        skipped = sum(slots[j] for j in chunk if j < k)
        starts = skipped + held * jnp.arange(TILES, dtype=jnp.int32)
        wanted = placed[k][0][:, None, :] + starts[None, :, None]
        rows = jnp.arange(TILES * held, dtype=jnp.int32)
        return rows[None, :, None, None] == wanted[:, None, :, :]

    def pair(weight):
        return weight, swap(weight)

    gates, ups, downs = pair(gate_weight[0]), pair(up_weight[0]), pair(down_weight[0])

    def selected(chunk):
        outgoing = 0.0
        for k in chunk:
            select = fits(k, chunk).astype(jnp.bfloat16).reshape(-1, tall)
            outgoing += jnp.dot(select, blocks[k][:tall], preferred_element_type=jnp.float32)
        return outgoing.astype(jnp.bfloat16).reshape(plane_experts, -1, tile)

    def turn(chunk):
        held = sum(slots[j] for j in chunk)
        row = jnp.arange(TILES * group * held, dtype=jnp.int32)
        source, rest = row // (TILES * held), row % (TILES * held)
        goal = (rest // held) * (group * held) + source * held + rest % held
        return (row[:, None] == goal[None, :]).astype(jnp.bfloat16)

    def grouped(array, chunk):
        array = array.reshape(plane_experts // group, -1, tile)
        array = jnp.einsum(
            "rc,gcd->grd", turn(chunk), array, preferred_element_type=jnp.float32
        )
        return array.astype(jnp.bfloat16).reshape(plane_experts // group, TILES, -1, tile)

    def ungrouped(array, chunk):
        array = array.reshape(plane_experts // group, -1, tile)
        array = jnp.einsum(
            "rc,grd->gcd", turn(chunk), array, preferred_element_type=jnp.float32
        )
        return array.astype(jnp.bfloat16).reshape(plane_experts, -1, tile)

    outgoing, arrived = [], []
    for index, chunk in enumerate(CHUNKS):
        for k in chunk:
            if k > 0:
                after = [outgoing[AFTER_SELECTED[k]]] if k in AFTER_SELECTED else []
                coming = around(tied(blocks[-1], *after), 1)
                if k in WITH_ARRIVED:
                    there = WITH_ARRIVED[k]
                    coming, arrived[there] = lax.optimization_barrier((coming, arrived[there]))
                blocks.append(coming)
            placed.append(places(k))
        outgoing.append(selected(chunk))
        arrived.append(exchange(outgoing[index]))

    last = len(CHUNKS) - 1
    early = [grouped(tied(arrived[i], *arrived[i + 1 : last]), CHUNKS[i]) for i in range(last)]
    produced = list(run_expert(early, gates, ups, downs))
    produced = [ungrouped(array, chunk) for array, chunk in zip(produced, CHUNKS)]
    late = run_expert([grouped(arrived[last], CHUNKS[last])], gates, ups, downs)
    produced.append(ungrouped(late[0], CHUNKS[last]))

    total = 0.0
    before_it = tuple(produced[:-1])
    for index in reversed(range(len(CHUNKS))):
        chunk = CHUNKS[index]
        returned = exchange(tied(produced[index], *before_it))
        before_it = (returned,)
        returned = returned.reshape(-1, tile)
        for k in reversed(chunk):
            mix = jnp.where(fits(k, chunk), placed[k][1][:, None, None, :], 0.0)
            total += lax.dot_general(
                mix.astype(jnp.bfloat16).reshape(-1, tall),
                returned,
                (((0,), (0,)), ((), ())),
                preferred_element_type=jnp.float32,
            )
            if k > 0:
                total = around(total.astype(jnp.bfloat16), -1).astype(jnp.float32)
    low, high = total[: tall // 2], total[tall // 2 :]
    own = jnp.where(core == 0, low, high)
    other = jnp.where(core == 0, high, low).astype(jnp.bfloat16)
    mixed = (own + swap(other).astype(jnp.float32)).astype(jnp.bfloat16)
    return jnp.concatenate(jnp.split(mixed, TILES // 2, axis=0), axis=1)


def solution(mesh):
    n_ep, n_tp = mesh.shape["ep"], mesh.shape["tp"]
    n_y, n_x = PLANE
    torus = Mesh(
        mesh.devices.reshape(n_ep // (n_y * n_x), n_y, n_x, n_tp), ("z", "y", "x", "tp")
    )
    ep = ("z", "y", "x")
    in_specs = (
        P(ep, "tp"),
        P(ep, None),
        P(ep, None),
        P(ep, None, "tp"),
        P(ep, None, "tp"),
        P(ep, "tp", None),
    )
    return jax.shard_map(
        on_device, mesh=torus, in_specs=in_specs, out_specs=P(ep, "tp"), check_vma=False
    )
```

time: 291 us -> 309 us (1.062)
  waiting for transfers between devices: 162 us -> 119 us
  starting transfers between devices: 51.1 us -> 75.3 us
  matrix products: 28.1 us -> 50 us
  other arithmetic: 11.3 us -> 18.8 us
  local copies, waits for them, and re-layouts: 0.28 us -> 5.4 us
    ppermute x8, waiting for transfers between devices: 80.8 us -> 20.6 us  [around(): return lax.ppermute(array, ('z', 'tp'), pairs)]
    dot_general x14 -> x18, matrix products: 27.4 us -> 49.3 us  [the longest x5 14 us: selected(): jnp.dot(select, blocks[k][:tall], preferred_element_type=jnp.float32)]
    all_to_all x6 -> x8, waiting for transfers between devices: 79.3 us -> 96.4 us  [exchange(): lax.all_to_all(array, ('y', 'x'), split_axis=0, concat_axis=0, tiled=True)]
    ppermute x8, starting transfers between devices: 10.4 us -> 26.2 us  [around(): return lax.ppermute(array, ('z', 'tp'), pairs)]
    all_to_all x6 -> x8, starting transfers between devices: 30.1 us -> 40.9 us  [exchange(): lax.all_to_all(array, ('y', 'x'), split_axis=0, concat_axis=0, tiled=True)]
    convert_element_type x1 -> x8, other arithmetic: 0.97 us -> 6.23 us  [the longest x2 3.24 us: on_device(): total = around(total.astype(jnp.bfloat16), -1).astype(jnp.float32)]
    unnamed x8 -> x38, local copies, waits for them, and re-layouts: 0.02 us -> 3.82 us
    pallas_call x3 -> x2, Pallas kernels: 34.2 us -> 36.3 us  [run_expert(): pl.pallas_call(functools.partial(expert_kernel, pieces), in_specs=[pl.Blo...]
  transfers between devices with their start and end apart: 19 -> 21, of which waited for: 14 -> 12; matrix products, arithmetic and copies ran while one was open for 11% -> 16% of each run, Pallas kernels for 7% -> 5%
where the time goes in v4:
time: 309 us; the launch traced here: 305 us
  waiting for transfers between devices  119 us (39%)
  starting transfers between devices  75.3 us (24%)
  matrix products  50 us (16%)
  Pallas kernels  36.3 us (12%)
  other arithmetic  18.8 us (6%)
  local copies, waits for them, and re-layouts  5.4 us (2%)
    all_to_all x8, waiting for transfers between devices, exchange(): lax.all_to_all(array, ('y', 'x'), split_axis=0, concat_axis=0, tiled=True)  96.4 us
    all_to_all x8, starting transfers between devices, exchange(): lax.all_to_all(array, ('y', 'x'), split_axis=0, concat_axis=0, tiled=True)  40.9 us
    pallas_call x2, Pallas kernels, run_expert(): pl.pallas_call(functools.partial(expert_kernel, pieces), in_specs=[pl.Blo...  36.3 us
    ppermute x8, starting transfers between devices, around(): return lax.ppermute(array, ('z', 'tp'), pairs)  26.2 us
    ppermute x8, waiting for transfers between devices, around(): return lax.ppermute(array, ('z', 'tp'), pairs)  20.6 us
    dot_general x5, matrix products, selected(): jnp.dot(select, blocks[k][:tall], preferred_element_type=jnp.float32)  14 us
    dot_general x4, matrix products, grouped(): jnp.einsum('rc,gcd->grd', turn(chunk), array, preferred_element_type=jnp....  13.9 us
    dot_general x4, matrix products, ungrouped(): jnp.einsum('rc,grd->gcd', turn(chunk), array, preferred_element_type=jnp....  12 us
  transfers between devices with their start and end apart: 21, of which 12 were waited for; matrix products, arithmetic and copies ran while one was open for 16% of the time, Pallas kernels for 5%

profile of v4, /device:TPU:1, one launch (start us, length us, event | category | flops | bytes accessed | tf_op | source)
XLA Modules:
  0.0 305.1 jit_solution(15783595667340487853)
XLA Ops:
  6.4 3.9 %collective-permute-start.1 = (bf16[528,1024]{1,0:T(8,128)(2,1)S(1)}, bf16[528,1024]{1,0:T(8,128)(2,1)}, u32[]{:S(2)}, u32[]{:S(2)}) collective-permute-start(bf16[528,1024]{1,0:T(8,128)(2,1)S(1)} %pad_dynamic-update-slice_fusion), channel_id=1, source_target_pairs={{0,32},{1,225},{32,64},{33,1},{64,96},{65,33},{96,128},{97,65},{12... | collective-permute-start | bytes 3244040 | tf_op jit(solution)/shard_map/ppermute | solution.py:27
  12.1 6.8 %all-to-all-start = ((bf16[16,24,1024]{2,1,0:T(8,128)(2,1)}), bf16[16,24,1024]{2,1,0:T(8,128)(2,1)S(1)}, u32[]{:S(2)}, u32[]{:S(2)}) async-start(bf16[16,24,1024]{2,1,0:T(8,128)(2,1)} %bitcast.1), calls=%async_computation | async-start | bytes 1572864 | tf_op jit(solution)/shard_map/all_to_all | solution.py:136
  18.9 12.0 %all-to-all-done = bf16[16,24,1024]{2,1,0:T(8,128)(2,1)S(1)} async-done(((bf16[16,24,1024]{2,1,0:T(8,128)(2,1)}), bf16[16,24,1024]{2,1,0:T(8,128)(2,1)S(1)}, u32[]{:S(2)}, u32[]{:S(2)}) %all-to-all-start) | async-done | bytes 786464 | tf_op jit(solution)/shard_map/all_to_all | solution.py:136
  31.6 3.8 %collective-permute-start.2 = (bf16[528,1024]{1,0:T(8,128)(2,1)}, bf16[528,1024]{1,0:T(8,128)(2,1)}, u32[]{:S(2)}, u32[]{:S(2)}) collective-permute-start(bf16[528,1024]{1,0:T(8,128)(2,1)} %collective-permute-done.1), channel_id=1, source_target_pairs={{0,32},{1,225},{32,64},{33,1},{64,96},{65,33},{96,128},{97,65},{12... | collective-permute-start | bytes 3244040 | tf_op jit(solution)/shard_map/ppermute | solution.py:27
  40.0 3.7 %all-to-all-start.1 = ((bf16[16,48,1024]{2,1,0:T(8,128)(2,1)}), bf16[16,48,1024]{2,1,0:T(8,128)(2,1)S(1)}, u32[]{:S(2)}, u32[]{:S(2)}) async-start(bf16[16,48,1024]{2,1,0:T(8,128)(2,1)} %bitcast.2), calls=%async_computation.1 | async-start | bytes 3145728 | tf_op jit(solution)/shard_map/all_to_all | solution.py:136
  43.7 4.1 %collective-permute-done.2 = bf16[528,1024]{1,0:T(8,128)(2,1)} collective-permute-done((bf16[528,1024]{1,0:T(8,128)(2,1)}, bf16[528,1024]{1,0:T(8,128)(2,1)}, u32[]{:S(2)}, u32[]{:S(2)}) %collective-permute-start.2) | collective-permute-done | bytes 1081376 | tf_op jit(solution)/shard_map/ppermute | solution.py:27
  51.9 12.3 %all-to-all-done.1 = bf16[16,48,1024]{2,1,0:T(8,128)(2,1)S(1)} async-done(((bf16[16,48,1024]{2,1,0:T(8,128)(2,1)}), bf16[16,48,1024]{2,1,0:T(8,128)(2,1)S(1)}, u32[]{:S(2)}, u32[]{:S(2)}) %all-to-all-start.1) | async-done | bytes 1572896 | tf_op jit(solution)/shard_map/all_to_all | solution.py:136
  69.1 4.7 %all-to-all-start.2 = ((bf16[16,48,1024]{2,1,0:T(8,128)(2,1)}), bf16[16,48,1024]{2,1,0:T(8,128)(2,1)}, u32[]{:S(2)}, u32[]{:S(2)}) async-start(bf16[16,48,1024]{2,1,0:T(8,128)(2,1)} %bitcast.160), calls=%async_computation.2 | async-start | bytes 3145728 | tf_op jit(solution)/shard_map/all_to_all | solution.py:136
  79.9 11.1 %collective-permute-done.4 = bf16[528,1024]{1,0:T(8,128)(2,1)} collective-permute-done((bf16[528,1024]{1,0:T(8,128)(2,1)}, bf16[528,1024]{1,0:T(8,128)(2,1)}, u32[]{:S(2)}, u32[]{:S(2)}) %collective-permute-start.4) | collective-permute-done | bytes 1081376 | tf_op jit(solution)/shard_map/ppermute | solution.py:27
  102.9 5.6 %all-to-all-start.3 = ((bf16[16,72,1024]{2,1,0:T(8,128)(2,1)}), bf16[16,72,1024]{2,1,0:T(8,128)(2,1)}, u32[]{:S(2)}, u32[]{:S(2)}) async-start(bf16[16,72,1024]{2,1,0:T(8,128)(2,1)} %bitcast.145), calls=%async_computation.3 | async-start | bytes 4718592 | tf_op jit(solution)/shard_map/all_to_all | solution.py:136
  113.6 3.7 %convolution_convert_fusion.4 = bf16[2,1024,384]{1,2,0:T(8,128)(2,1)} fusion(bf16[2,384,1024]{2,1,0:T(8,128)(2,1)} %bitcast.24, s32[384]{0:T(512)S(1)} %fusion.88), kind=kOutput, calls=%fused_computation.17 | convolution fusion | flops 604913664 | bytes 3147264 | tf_op jit(solution)/shard_map/rc,gcd->grd/dot_general | solution.py:216
  117.3 15.0 %shard_map.65 = (bf16[2,4,48,1024]{3,2,1,0:T(8,128)(2,1)}, bf16[2,4,96,1024]{3,2,1,0:T(8,128)(2,1)}, bf16[2,4,96,1024]{3,2,1,0:T(8,128)(2,1)}) custom-call(bf16[2,4,48,1024]{3,2,1,0:T(8,128)(2,1)} %bitcast.151, bf16[2,4,96,1024]{3,2,1,0:T(8,128)(2,1)} %bitcast.157, bf16[2,4,96,1024]{3,2,1,0:T(8,128)(2,1)} %bitcast.158, bf16[4096,384]{1,0:T(8,128)(2,1)} %bitcast.136, ...), custom_call_target="tpu_custom_call" | custom-call | tf_op jit(solution)/shard_map/pallas_call | solution.py:110
  139.2 5.3 %convolution_convert_fusion.1 = bf16[2,1024,576]{1,2,0:T(8,128)(2,1)} fusion(bf16[2,576,1024]{2,1,0:T(8,128)(2,1)} %bitcast.5, s32[576]{0:T(1024)S(1)} %fusion.71), kind=kOutput, calls=%fused_computation.14 | convolution fusion | flops 1360465920 | bytes 4720896 | tf_op jit(solution)/shard_map/rc,gcd->grd/dot_general | solution.py:216
  144.5 21.3 %shard_map.64 = bf16[2,4,144,1024]{3,2,1,0:T(8,128)(2,1)} custom-call(bf16[2,4,144,1024]{3,2,1,0:T(8,128)(2,1)} %bitcast.155, bf16[4096,384]{1,0:T(8,128)(2,1)} %bitcast.137, bf16[4096,384]{1,0:T(8,128)(2,1)} %collective-permute-done.5.refs_2_.refs_4_, bf16[4096,384]{1,0:T(8,128)(2,1)} %bitcast.141, ...), custom_call_target="tpu_custom_call" | custom-call | tf_op jit(solution)/shard_map/pallas_call | solution.py:110
  165.8 5.1 %convolution_convert_fusion = bf16[2,1024,576]{1,2,0:T(8,128)(2,1)} fusion(bf16[2,576,1024]{2,1,0:T(8,128)(2,1)} %bitcast.154, s32[576]{0:T(1024)S(1)} %fusion.71), kind=kOutput, calls=%fused_computation.13 | convolution fusion | flops 1360465920 | bytes 4720896 | tf_op jit(solution)/shard_map/rc,grd->gcd/dot_general | solution.py:223
  170.9 6.6 %all-to-all-start.4 = ((bf16[16,72,1024]{2,1,0:T(8,128)(2,1)}), bf16[16,72,1024]{2,1,0:T(8,128)(2,1)S(1)}, u32[]{:S(2)}, u32[]{:S(2)}) async-start(bf16[16,72,1024]{2,1,0:T(8,128)(2,1)} %bitcast.156), calls=%async_computation.4 | async-start | bytes 4718592 | tf_op jit(solution)/shard_map/all_to_all | solution.py:136
  184.5 20.8 %all-to-all-done.4 = bf16[16,72,1024]{2,1,0:T(8,128)(2,1)S(1)} async-done(((bf16[16,72,1024]{2,1,0:T(8,128)(2,1)}), bf16[16,72,1024]{2,1,0:T(8,128)(2,1)S(1)}, u32[]{:S(2)}, u32[]{:S(2)}) %all-to-all-start.4) | async-done | bytes 2359328 | tf_op jit(solution)/shard_map/all_to_all | solution.py:136
  207.8 9.4 %collective-permute-start.8 = (bf16[512,1024]{1,0:T(8,128)(2,1)}, bf16[512,1024]{1,0:T(8,128)(2,1)S(1)}, u32[]{:S(2)}, u32[]{:S(2)}) collective-permute-start(bf16[512,1024]{1,0:T(8,128)(2,1)} %convolution_convert_fusion.8), channel_id=1, source_target_pairs={{0,224},{1,33},{32,0},{33,65},{64,32},{65,97},{96,64},{97,129},{12... | collective-permute-start | bytes 3145736 | tf_op jit(solution)/shard_map/ppermute | solution.py:27
  217.1 6.2 %all-to-all-start.5 = ((bf16[16,48,1024]{2,1,0:T(8,128)(2,1)}), bf16[16,48,1024]{2,1,0:T(8,128)(2,1)}, u32[]{:S(2)}, u32[]{:S(2)}) async-start(bf16[16,48,1024]{2,1,0:T(8,128)(2,1)} %bitcast.148), calls=%async_computation.5 | async-start | bytes 3145728 | tf_op jit(solution)/shard_map/all_to_all | solution.py:136
  223.9 5.3 %collective-permute-done.8 = bf16[512,1024]{1,0:T(8,128)(2,1)S(1)} collective-permute-done((bf16[512,1024]{1,0:T(8,128)(2,1)}, bf16[512,1024]{1,0:T(8,128)(2,1)S(1)}, u32[]{:S(2)}, u32[]{:S(2)}) %collective-permute-start.8) | collective-permute-done | bytes 1048608 | tf_op jit(solution)/shard_map/ppermute | solution.py:27
  235.2 15.2 %all-to-all-done.5 = bf16[16,48,1024]{2,1,0:T(8,128)(2,1)} async-done(((bf16[16,48,1024]{2,1,0:T(8,128)(2,1)}), bf16[16,48,1024]{2,1,0:T(8,128)(2,1)}, u32[]{:S(2)}, u32[]{:S(2)}) %all-to-all-start.5) | async-done | bytes 1572896 | tf_op jit(solution)/shard_map/all_to_all | solution.py:136
  250.4 3.7 %all-to-all-start.6 = ((bf16[16,48,1024]{2,1,0:T(8,128)(2,1)}), bf16[16,48,1024]{2,1,0:T(8,128)(2,1)S(1)}, u32[]{:S(2)}, u32[]{:S(2)}) async-start(bf16[16,48,1024]{2,1,0:T(8,128)(2,1)} %bitcast.147), calls=%async_computation.6 | async-start | bytes 3145728 | tf_op jit(solution)/shard_map/all_to_all | solution.py:136
  259.1 20.1 %all-to-all-done.6 = bf16[16,48,1024]{2,1,0:T(8,128)(2,1)S(1)} async-done(((bf16[16,48,1024]{2,1,0:T(8,128)(2,1)}), bf16[16,48,1024]{2,1,0:T(8,128)(2,1)S(1)}, u32[]{:S(2)}, u32[]{:S(2)}) %all-to-all-start.6) | async-done | bytes 1572896 | tf_op jit(solution)/shard_map/all_to_all | solution.py:136
  285.7 12.7 %all-to-all-done.7 = bf16[16,24,1024]{2,1,0:T(8,128)(2,1)S(1)} async-done(((bf16[16,24,1024]{2,1,0:T(8,128)(2,1)}), bf16[16,24,1024]{2,1,0:T(8,128)(2,1)S(1)}, u32[]{:S(2)}, u32[]{:S(2)}) %all-to-all-start.7) | async-done | bytes 786464 | tf_op jit(solution)/shard_map/all_to_all | solution.py:136
  (144 shorter events, 86.0 us)
Async XLA Ops:
  0.0 5.0 %collective-permute-start = (bf16[128,2048]{1,0:T(8,128)(2,1)}, bf16[128,2048]{1,0:T(8,128)(2,1)S(1)}, u32[]{:S(2)}, u32[]{:S(2)}) collective-permute-start(bf16[128,2048]{1,0:T(8,128)(2,1)} %param.6), channel_id=1, source_target_pairs={{0,1},{1,0},{2,3},{3,2},{4,5},{5,4},{6,7},{7,6},{8,9},{9,8},{10,11... | collective-permute-start | bytes 1572872 | tf_op jit(solution)/shard_map/ppermute | solution.py:18
  6.4 24.6 %collective-permute-start.1 = (bf16[528,1024]{1,0:T(8,128)(2,1)S(1)}, bf16[528,1024]{1,0:T(8,128)(2,1)}, u32[]{:S(2)}, u32[]{:S(2)}) collective-permute-start(bf16[528,1024]{1,0:T(8,128)(2,1)S(1)} %pad_dynamic-update-slice_fusion), channel_id=1, source_target_pairs={{0,32},{1,225},{32,64},{33,1},{64,96},{65,33},{96,128},{97,65},{12... | collective-permute-start | bytes 3244040 | tf_op jit(solution)/shard_map/ppermute | solution.py:27
  12.1 18.9 %all-to-all-start = ((bf16[16,24,1024]{2,1,0:T(8,128)(2,1)}), bf16[16,24,1024]{2,1,0:T(8,128)(2,1)S(1)}, u32[]{:S(2)}, u32[]{:S(2)}) async-start(bf16[16,24,1024]{2,1,0:T(8,128)(2,1)} %bitcast.1), calls=%async_computation | async-start | bytes 1572864 | tf_op jit(solution)/shard_map/all_to_all | solution.py:136
  31.6 16.3 %collective-permute-start.2 = (bf16[528,1024]{1,0:T(8,128)(2,1)}, bf16[528,1024]{1,0:T(8,128)(2,1)}, u32[]{:S(2)}, u32[]{:S(2)}) collective-permute-start(bf16[528,1024]{1,0:T(8,128)(2,1)} %collective-permute-done.1), channel_id=1, source_target_pairs={{0,32},{1,225},{32,64},{33,1},{64,96},{65,33},{96,128},{97,65},{12... | collective-permute-start | bytes 3244040 | tf_op jit(solution)/shard_map/ppermute | solution.py:27
  40.0 24.2 %all-to-all-start.1 = ((bf16[16,48,1024]{2,1,0:T(8,128)(2,1)}), bf16[16,48,1024]{2,1,0:T(8,128)(2,1)S(1)}, u32[]{:S(2)}, u32[]{:S(2)}) async-start(bf16[16,48,1024]{2,1,0:T(8,128)(2,1)} %bitcast.2), calls=%async_computation.1 | async-start | bytes 3145728 | tf_op jit(solution)/shard_map/all_to_all | solution.py:136
  47.9 16.3 %collective-permute-start.3 = (bf16[528,1024]{1,0:T(8,128)(2,1)}, bf16[528,1024]{1,0:T(8,128)(2,1)S(1)}, u32[]{:S(2)}, u32[]{:S(2)}) collective-permute-start(bf16[528,1024]{1,0:T(8,128)(2,1)} %collective-permute-done.2), channel_id=1, source_target_pairs={{0,32},{1,225},{32,64},{33,1},{64,96},{65,33},{96,128},{97,65},{12... | collective-permute-start | bytes 3244040 | tf_op jit(solution)/shard_map/ppermute | solution.py:27
  69.1 25.2 %all-to-all-start.2 = ((bf16[16,48,1024]{2,1,0:T(8,128)(2,1)}), bf16[16,48,1024]{2,1,0:T(8,128)(2,1)}, u32[]{:S(2)}, u32[]{:S(2)}) async-start(bf16[16,48,1024]{2,1,0:T(8,128)(2,1)} %bitcast.160), calls=%async_computation.2 | async-start | bytes 3145728 | tf_op jit(solution)/shard_map/all_to_all | solution.py:136
  73.8 17.2 %collective-permute-start.4 = (bf16[528,1024]{1,0:T(8,128)(2,1)}, bf16[528,1024]{1,0:T(8,128)(2,1)}, u32[]{:S(2)}, u32[]{:S(2)}) collective-permute-start(bf16[528,1024]{1,0:T(8,128)(2,1)} %copy-done.7), channel_id=1, source_target_pairs={{0,32},{1,225},{32,64},{33,1},{64,96},{65,33},{96,128},{97,65},{12... | collective-permute-start | bytes 3244040 | tf_op jit(solution)/shard_map/ppermute | solution.py:27
  77.1 40.1 %collective-permute-start.5 = (bf16[4096,384]{1,0:T(8,128)(2,1)S(1)}, bf16[4096,384]{1,0:T(8,128)(2,1)}, u32[]{:S(2)}, u32[]{:S(2)}) collective-permute-start(bf16[4096,384]{1,0:T(8,128)(2,1)S(1)} %bitcast.138), channel_id=1, source_target_pairs={{0,1},{1,0},{2,3},{3,2},{4,5},{5,4},{6,7},{7,6},{8,9},{9,8},{10,11... | collective-permute-start | bytes 9437192 | tf_op jit(solution)/shard_map/ppermute | solution.py:18
  78.8 38.5 %collective-permute-start.6 = (bf16[4096,384]{1,0:T(8,128)(2,1)}, bf16[4096,384]{1,0:T(8,128)(2,1)}, u32[]{:S(2)}, u32[]{:S(2)}) collective-permute-start(bf16[4096,384]{1,0:T(8,128)(2,1)} %bitcast.139), channel_id=1, source_target_pairs={{0,1},{1,0},{2,3},{3,2},{4,5},{5,4},{6,7},{7,6},{8,9},{9,8},{10,11... | collective-permute-start | bytes 9437192 | tf_op jit(solution)/shard_map/ppermute | solution.py:18
  78.8 38.4 %collective-permute-start.7 = (bf16[384,4096]{1,0:T(8,128)(2,1)}, bf16[384,4096]{1,0:T(8,128)(2,1)}, u32[]{:S(2)}, u32[]{:S(2)}) collective-permute-start(bf16[384,4096]{1,0:T(8,128)(2,1)} %bitcast.142), channel_id=1, source_target_pairs={{0,1},{1,0},{2,3},{3,2},{4,5},{5,4},{6,7},{7,6},{8,9},{9,8},{10,11... | collective-permute-start | bytes 9437192 | tf_op jit(solution)/shard_map/ppermute | solution.py:18
  79.9 18.8 %copy-start.9 = (s32[16,4,128]{2,1,0:T(4,128)}, s32[16,4,128]{2,1,0:T(4,128)S(1)}, u32[]{:S(2)}) copy-start(s32[16,4,128]{2,1,0:T(4,128)S(1)} %broadcast_add_fusion) | copy-start | bytes 98308
  102.9 36.3 %all-to-all-start.3 = ((bf16[16,72,1024]{2,1,0:T(8,128)(2,1)}), bf16[16,72,1024]{2,1,0:T(8,128)(2,1)}, u32[]{:S(2)}, u32[]{:S(2)}) async-start(bf16[16,72,1024]{2,1,0:T(8,128)(2,1)} %bitcast.145), calls=%async_computation.3 | async-start | bytes 4718592 | tf_op jit(solution)/shard_map/all_to_all | solution.py:136
  170.9 34.3 %all-to-all-start.4 = ((bf16[16,72,1024]{2,1,0:T(8,128)(2,1)}), bf16[16,72,1024]{2,1,0:T(8,128)(2,1)S(1)}, u32[]{:S(2)}, u32[]{:S(2)}) async-start(bf16[16,72,1024]{2,1,0:T(8,128)(2,1)} %bitcast.156), calls=%async_computation.4 | async-start | bytes 4718592 | tf_op jit(solution)/shard_map/all_to_all | solution.py:136
  207.8 15.6 %copy-start.10 = (s32[16,4,128]{2,1,0:T(4,128)S(1)}, s32[16,4,128]{2,1,0:T(4,128)}, u32[]{:S(2)}) copy-start(s32[16,4,128]{2,1,0:T(4,128)} %copy-done.9) | copy-start | bytes 98308
  207.8 21.4 %collective-permute-start.8 = (bf16[512,1024]{1,0:T(8,128)(2,1)}, bf16[512,1024]{1,0:T(8,128)(2,1)S(1)}, u32[]{:S(2)}, u32[]{:S(2)}) collective-permute-start(bf16[512,1024]{1,0:T(8,128)(2,1)} %convolution_convert_fusion.8), channel_id=1, source_target_pairs={{0,224},{1,33},{32,0},{33,65},{64,32},{65,97},{96,64},{97,129},{12... | collective-permute-start | bytes 3145736 | tf_op jit(solution)/shard_map/ppermute | solution.py:27
  217.1 33.3 %all-to-all-start.5 = ((bf16[16,48,1024]{2,1,0:T(8,128)(2,1)}), bf16[16,48,1024]{2,1,0:T(8,128)(2,1)}, u32[]{:S(2)}, u32[]{:S(2)}) async-start(bf16[16,48,1024]{2,1,0:T(8,128)(2,1)} %bitcast.148), calls=%async_computation.5 | async-start | bytes 3145728 | tf_op jit(solution)/shard_map/all_to_all | solution.py:136
  232.9 21.2 %copy-start.15 = (s32[16,4,128]{2,1,0:T(4,128)S(1)}, s32[16,4,128]{2,1,0:T(4,128)}, u32[]{:S(2)}) copy-start(s32[16,4,128]{2,1,0:T(4,128)} %copy-done.14) | copy-start | bytes 98308
  233.0 24.0 %collective-permute-start.9 = (bf16[512,1024]{1,0:T(8,128)(2,1)S(1)}, bf16[512,1024]{1,0:T(8,128)(2,1)}, u32[]{:S(2)}, u32[]{:S(2)}) collective-permute-start(bf16[512,1024]{1,0:T(8,128)(2,1)S(1)} %add_convert_fusion.2), channel_id=1, source_target_pairs={{0,224},{1,33},{32,0},{33,65},{64,32},{65,97},{96,64},{97,129},{12... | collective-permute-start | bytes 3145736 | tf_op jit(solution)/shard_map/ppermute | solution.py:27
  250.4 28.7 %all-to-all-start.6 = ((bf16[16,48,1024]{2,1,0:T(8,128)(2,1)}), bf16[16,48,1024]{2,1,0:T(8,128)(2,1)S(1)}, u32[]{:S(2)}, u32[]{:S(2)}) async-start(bf16[16,48,1024]{2,1,0:T(8,128)(2,1)} %bitcast.147), calls=%async_computation.6 | async-start | bytes 3145728 | tf_op jit(solution)/shard_map/all_to_all | solution.py:136
  258.6 21.5 %collective-permute-start.10 = (bf16[512,1024]{1,0:T(8,128)(2,1)S(1)}, bf16[512,1024]{1,0:T(8,128)(2,1)}, u32[]{:S(2)}, u32[]{:S(2)}) collective-permute-start(bf16[512,1024]{1,0:T(8,128)(2,1)S(1)} %add_convert_fusion.1), channel_id=1, source_target_pairs={{0,224},{1,33},{32,0},{33,65},{64,32},{65,97},{96,64},{97,129},{12... | collective-permute-start | bytes 3145736 | tf_op jit(solution)/shard_map/ppermute | solution.py:27
  281.8 17.3 %collective-permute-start.11 = (bf16[512,1024]{1,0:T(8,128)(2,1)S(1)}, bf16[512,1024]{1,0:T(8,128)(2,1)S(1)}, u32[]{:S(2)}, u32[]{:S(2)}) collective-permute-start(bf16[512,1024]{1,0:T(8,128)(2,1)S(1)} %add_convert_fusion), channel_id=1, source_target_pairs={{0,224},{1,33},{32,0},{33,65},{64,32},{65,97},{96,64},{97,129},{12... | collective-permute-start | bytes 3145736 | tf_op jit(solution)/shard_map/ppermute | solution.py:27
  281.9 16.5 %all-to-all-start.7 = ((bf16[16,24,1024]{2,1,0:T(8,128)(2,1)}), bf16[16,24,1024]{2,1,0:T(8,128)(2,1)S(1)}, u32[]{:S(2)}, u32[]{:S(2)}) async-start(bf16[16,24,1024]{2,1,0:T(8,128)(2,1)} %bitcast.31), calls=%async_computation.7 | async-start | bytes 1572864 | tf_op jit(solution)/shard_map/all_to_all | solution.py:136
  299.7 4.1 %collective-permute-start.12 = (bf16[256,1024]{1,0:T(8,128)(2,1)S(1)}, bf16[256,1024]{1,0:T(8,128)(2,1)S(1)}, u32[]{:S(2)}, u32[]{:S(2)}) collective-permute-start(bf16[256,1024]{1,0:T(8,128)(2,1)S(1)} %select_convert_fusion.4), channel_id=1, source_target_pairs={{0,1},{1,0},{2,3},{3,2},{4,5},{5,4},{6,7},{7,6},{8,9},{9,8},{10,11... | collective-permute-start | bytes 1572872 | tf_op jit(solution)/shard_map/ppermute | solution.py:18
  (15 other events, 45.9 us)

commit v5 on v3

--- a/solution.py
+++ b/solution.py
@@ -210,28 +210,31 @@
         produced.append(expert(here))
 
     returns = [None] * len(chunks)
-    before_it = tuple(produced[:-1])
-    for index in reversed(range(len(chunks))):
+    before_it = (*produced[:-1], arrived[-1])
+    for index in (1, 2, 0):
         returns[index] = exchange(tied(produced[index], *before_it))
         before_it = (returns[index],)
     returns = [one.reshape(-1, model_width) for one in returns]
 
-    total = 0.0
+    totals = [0.0, 0.0]
     for k in reversed(range(far + 1)):
         for index in reversed(range(len(chunks))):
             chunk = chunks[index]
             if within(k, chunk):
                 mix = jnp.where(fits(k, chunk), placed[k][1][:, None, :], 0.0)
                 mix = mix.astype(jnp.bfloat16).reshape(-1, tok_count)
-                total += lax.dot_general(
-                    mix,
-                    returns[index],
-                    (((0,), (0,)), ((), ())),
-                    preferred_element_type=jnp.float32,
-                )
+                for half in range(2):
+                    totals[half] += lax.dot_general(
+                        mix,
+                        returns[index][:, half * half_width : (half + 1) * half_width],
+                        (((0,), (0,)), ((), ())),
+                        preferred_element_type=jnp.float32,
+                    )
         if k > 0:
-            total = around(total.astype(jnp.bfloat16), -1).astype(jnp.float32)
-    low, high = total[:, :half_width], total[:, half_width:]
+            totals = [
+                around(total.astype(jnp.bfloat16), -1).astype(jnp.float32) for total in totals
+            ]
+    low, high = totals
     own = jnp.where(core == 0, low, high)
     other = jnp.where(core == 0, high, low).astype(jnp.bfloat16)
     return (own + swap(other).astype(jnp.float32)).astype(jnp.bfloat16)

time: 291 us -> 275 us (0.945)
  waiting for transfers between devices: 162 us -> 147 us
    all_to_all x6, waiting for transfers between devices: 79.3 us -> 71.6 us  [exchange(): lax.all_to_all(array, ('y', 'x'), split_axis=0, concat_axis=0, tiled=True)]
    ppermute x8 -> x12, waiting for transfers between devices: 80.8 us -> 73.4 us  [around(): return lax.ppermute(array, ('z', 'tp'), pairs)]
    dot_general x7 -> x14, matrix products: 14.1 us -> 12.6 us  [on_device(): lax.dot_general(mix, returns[index][:, half * half_width:(half + 1) * hal...]
    ppermute x8 -> x12, starting transfers between devices: 10.4 us -> 11 us  [around(): return lax.ppermute(array, ('z', 'tp'), pairs)]
  transfers between devices with their start and end apart: 19 -> 23, of which waited for: 14 -> 18; matrix products, arithmetic and copies ran while one was open for 11% -> 12% of each run, Pallas kernels for 7% -> 13%
where the time goes in v5:
time: 275 us; the launch traced here: 273 us
  waiting for transfers between devices  147 us (53%)
  starting transfers between devices  51.8 us (19%)
  Pallas kernels  34.2 us (12%)
  matrix products  26.6 us (10%)
  other arithmetic  12.2 us (4%)
    ppermute x12, waiting for transfers between devices, around(): return lax.ppermute(array, ('z', 'tp'), pairs)  73.4 us
    all_to_all x6, waiting for transfers between devices, exchange(): lax.all_to_all(array, ('y', 'x'), split_axis=0, concat_axis=0, tiled=True)  71.6 us
    pallas_call x3, Pallas kernels, run_expert(): pl.pallas_call(expert_kernel, in_specs=[pl.BlockSpec(memory_space=pl.ANY)...  34.2 us
    all_to_all x6, starting transfers between devices, exchange(): lax.all_to_all(array, ('y', 'x'), split_axis=0, concat_axis=0, tiled=True)  30.9 us
    dot_general x7, matrix products, selected(): jnp.dot(select, blocks[k][:, :model_width], preferred_element_type=jnp.fl...  13.2 us
    dot_general x14, matrix products, on_device(): lax.dot_general(mix, returns[index][:, half * half_width:(half + 1) * hal...  12.6 us
    ppermute x12, starting transfers between devices, around(): return lax.ppermute(array, ('z', 'tp'), pairs)  11 us
    ppermute x5, starting transfers between devices, swap(): return lax.ppermute(array, 'tp', [(0, 1), (1, 0)])  9.84 us
  transfers between devices with their start and end apart: 23, of which 18 were waited for; matrix products, arithmetic and copies ran while one was open for 12% of the time, Pallas kernels for 13%

profile of v5, /device:TPU:1, one launch (start us, length us, event | category | flops | bytes accessed | tf_op | source)
XLA Modules:
  0.0 273.5 jit_solution(3978102920037890727)
XLA Ops:
  6.2 3.9 %collective-permute-start.1 = (bf16[128,4224]{1,0:T(8,128)(2,1)S(1)}, bf16[128,4224]{1,0:T(8,128)(2,1)S(1)}, u32[]{:S(2)}, u32[]{:S(2)}) collective-permute-start(bf16[128,4224]{1,0:T(8,128)(2,1)S(1)} %fusion.22), channel_id=1, source_target_pairs={{0,32},{1,225},{32,64},{33,1},{64,96},{65,33},{96,128},{97,65},{12... | collective-permute-start | bytes 3244040 | tf_op jit(solution)/shard_map/ppermute | solution.py:23
  10.2 12.0 %collective-permute-done.1 = bf16[128,4224]{1,0:T(8,128)(2,1)S(1)} collective-permute-done((bf16[128,4224]{1,0:T(8,128)(2,1)S(1)}, bf16[128,4224]{1,0:T(8,128)(2,1)S(1)}, u32[]{:S(2)}, u32[]{:S(2)}) %collective-permute-start.1) | collective-permute-done | bytes 1081376 | tf_op jit(solution)/shard_map/ppermute | solution.py:23
  28.7 6.8 %all-to-all-start = ((bf16[16,16,4096]{2,1,0:T(8,128)(2,1)}), bf16[16,16,4096]{2,1,0:T(8,128)(2,1)}, u32[]{:S(2)}, u32[]{:S(2)}) async-start(bf16[16,16,4096]{2,1,0:T(8,128)(2,1)} %bitcast.3), calls=%async_computation | async-start | bytes 4194304 | tf_op jit(solution)/shard_map/all_to_all | solution.py:114
  41.3 11.5 %collective-permute-done.3 = bf16[128,4224]{1,0:T(8,128)(2,1)} collective-permute-done((bf16[128,4224]{1,0:T(8,128)(2,1)S(1)}, bf16[128,4224]{1,0:T(8,128)(2,1)}, u32[]{:S(2)}, u32[]{:S(2)}) %collective-permute-start.3) | collective-permute-done | bytes 1081376 | tf_op jit(solution)/shard_map/ppermute | solution.py:23
  56.7 12.1 %all-to-all-done = bf16[16,16,4096]{2,1,0:T(8,128)(2,1)} async-done(((bf16[16,16,4096]{2,1,0:T(8,128)(2,1)}), bf16[16,16,4096]{2,1,0:T(8,128)(2,1)}, u32[]{:S(2)}, u32[]{:S(2)}) %all-to-all-start) | async-done | bytes 2097184 | tf_op jit(solution)/shard_map/all_to_all | solution.py:114
  69.5 4.3 %all-to-all-start.2 = ((bf16[16,8,4096]{2,1,0:T(8,128)(2,1)}), bf16[16,8,4096]{2,1,0:T(8,128)(2,1)}, u32[]{:S(2)}, u32[]{:S(2)}) async-start(bf16[16,8,4096]{2,1,0:T(8,128)(2,1)} %fusion.2), calls=%async_computation.2 | async-start | bytes 2097152 | tf_op jit(solution)/shard_map/all_to_all | solution.py:114
  74.0 9.4 %collective-permute-done.4 = bf16[128,4224]{1,0:T(8,128)(2,1)} collective-permute-done((bf16[128,4224]{1,0:T(8,128)(2,1)}, bf16[128,4224]{1,0:T(8,128)(2,1)}, u32[]{:S(2)}, u32[]{:S(2)}) %collective-permute-start.4) | collective-permute-done | bytes 1081376 | tf_op jit(solution)/shard_map/ppermute | solution.py:23
  91.6 4.7 %all-to-all-start.1 = ((bf16[16,24,4096]{2,1,0:T(8,128)(2,1)}), bf16[16,24,4096]{2,1,0:T(8,128)(2,1)}, u32[]{:S(2)}, u32[]{:S(2)}) async-start(bf16[16,24,4096]{2,1,0:T(8,128)(2,1)} %bitcast.139), calls=%async_computation.1 | async-start | bytes 6291456 | tf_op jit(solution)/shard_map/all_to_all | solution.py:114
  96.3 11.4 %shard_map.66 = bf16[256,4096]{1,0:T(8,128)(2,1)} custom-call(bf16[256,4096]{1,0:T(8,128)(2,1)} %bitcast.19.x, bf16[4096,384]{1,0:T(8,128)(2,1)} %bitcast.126, bf16[4096,384]{1,0:T(8,128)(2,1)} %collective-permute-done.5.gate_b, bf16[4096,384]{1,0:T(8,128)(2,1)} %bitcast.131, bf16[4096,384]{1,0:T(8,128)(2,1)} %collective-permute-done.6.up_b, ...), custom_call_target="tpu_custom_call" | custom-call | tf_op jit(solution)/shard_map/pallas_call | solution.py:89
  107.7 9.7 %shard_map.65 = bf16[128,4096]{1,0:T(8,128)(2,1)} custom-call(bf16[128,4096]{1,0:T(8,128)(2,1)} %bitcast.17.x, bf16[4096,384]{1,0:T(8,128)(2,1)} %bitcast.127, bf16[4096,384]{1,0:T(8,128)(2,1)} %collective-permute-done.5.gate_b, bf16[4096,384]{1,0:T(8,128)(2,1)} %bitcast.132, bf16[4096,384]{1,0:T(8,128)(2,1)} %collective-permute-done.6.up_b, ...), custom_call_target="tpu_custom_call" | custom-call | tf_op jit(solution)/shard_map/pallas_call | solution.py:89
  117.4 21.5 %all-to-all-done.1 = bf16[16,24,4096]{2,1,0:T(8,128)(2,1)} async-done(((bf16[16,24,4096]{2,1,0:T(8,128)(2,1)}), bf16[16,24,4096]{2,1,0:T(8,128)(2,1)}, u32[]{:S(2)}, u32[]{:S(2)}) %all-to-all-start.1) | async-done | bytes 3145760 | tf_op jit(solution)/shard_map/all_to_all | solution.py:114
  138.9 5.0 %all-to-all-start.3 = ((bf16[16,8,4096]{2,1,0:T(8,128)(2,1)}), bf16[16,8,4096]{2,1,0:T(8,128)(2,1)S(1)}, u32[]{:S(2)}, u32[]{:S(2)}) async-start(bf16[16,8,4096]{2,1,0:T(8,128)(2,1)} %bitcast.145), calls=%async_computation.3 | async-start | bytes 2097152 | tf_op jit(solution)/shard_map/all_to_all | solution.py:114
  143.8 13.1 %shard_map.64 = bf16[384,4096]{1,0:T(8,128)(2,1)} custom-call(bf16[384,4096]{1,0:T(8,128)(2,1)} %bitcast.12.x, bf16[4096,384]{1,0:T(8,128)(2,1)} %bitcast.128, bf16[4096,384]{1,0:T(8,128)(2,1)} %collective-permute-done.5.gate_b, bf16[4096,384]{1,0:T(8,128)(2,1)} %bitcast.133, bf16[4096,384]{1,0:T(8,128)(2,1)} %collective-permute-done.6.up_b, ...), custom_call_target="tpu_custom_call" | custom-call | tf_op jit(solution)/shard_map/pallas_call | solution.py:89
  160.0 5.0 %all-to-all-start.4 = ((bf16[16,24,4096]{2,1,0:T(8,128)(2,1)}), bf16[16,24,4096]{2,1,0:T(8,128)(2,1)S(1)}, u32[]{:S(2)}, u32[]{:S(2)}) async-start(bf16[16,24,4096]{2,1,0:T(8,128)(2,1)} %bitcast.138), calls=%async_computation.4 | async-start | bytes 6291456 | tf_op jit(solution)/shard_map/all_to_all | solution.py:114
  171.5 36.0 %all-to-all-done.4 = bf16[16,24,4096]{2,1,0:T(8,128)(2,1)S(1)} async-done(((bf16[16,24,4096]{2,1,0:T(8,128)(2,1)}), bf16[16,24,4096]{2,1,0:T(8,128)(2,1)S(1)}, u32[]{:S(2)}, u32[]{:S(2)}) %all-to-all-start.4) | async-done | bytes 3145760 | tf_op jit(solution)/shard_map/all_to_all | solution.py:114
  208.8 5.2 %all-to-all-start.5 = ((bf16[16,16,4096]{2,1,0:T(8,128)(2,1)}), bf16[16,16,4096]{2,1,0:T(8,128)(2,1)}, u32[]{:S(2)}, u32[]{:S(2)}) async-start(bf16[16,16,4096]{2,1,0:T(8,128)(2,1)} %bitcast.144), calls=%async_computation.5 | async-start | bytes 4194304 | tf_op jit(solution)/shard_map/all_to_all | solution.py:114
  215.1 8.7 %collective-permute-done.12 = bf16[128,2048]{1,0:T(8,128)(2,1)} collective-permute-done((bf16[128,2048]{1,0:T(8,128)(2,1)}, bf16[128,2048]{1,0:T(8,128)(2,1)}, u32[]{:S(2)}, u32[]{:S(2)}) %collective-permute-start.12) | collective-permute-done | bytes 524320 | tf_op jit(solution)/shard_map/ppermute | solution.py:23
  225.5 4.3 %collective-permute-done.8 = bf16[128,2048]{1,0:T(8,128)(2,1)S(1)} collective-permute-done((bf16[128,2048]{1,0:T(8,128)(2,1)S(1)}, bf16[128,2048]{1,0:T(8,128)(2,1)S(1)}, u32[]{:S(2)}, u32[]{:S(2)}) %collective-permute-start.8) | collective-permute-done | bytes 524320 | tf_op jit(solution)/shard_map/ppermute | solution.py:23
  230.8 4.6 %collective-permute-done.13 = bf16[128,2048]{1,0:T(8,128)(2,1)S(1)} collective-permute-done((bf16[128,2048]{1,0:T(8,128)(2,1)S(1)}, bf16[128,2048]{1,0:T(8,128)(2,1)S(1)}, u32[]{:S(2)}, u32[]{:S(2)}) %collective-permute-start.13) | collective-permute-done | bytes 524320 | tf_op jit(solution)/shard_map/ppermute | solution.py:23
  235.9 5.1 %collective-permute-done.9 = bf16[128,2048]{1,0:T(8,128)(2,1)S(1)} collective-permute-done((bf16[128,2048]{1,0:T(8,128)(2,1)S(1)}, bf16[128,2048]{1,0:T(8,128)(2,1)S(1)}, u32[]{:S(2)}, u32[]{:S(2)}) %collective-permute-start.9) | collective-permute-done | bytes 524320 | tf_op jit(solution)/shard_map/ppermute | solution.py:23
  243.3 3.3 %collective-permute-done.14 = bf16[128,2048]{1,0:T(8,128)(2,1)S(1)} collective-permute-done((bf16[128,2048]{1,0:T(8,128)(2,1)S(1)}, bf16[128,2048]{1,0:T(8,128)(2,1)S(1)}, u32[]{:S(2)}, u32[]{:S(2)}) %collective-permute-start.14) | collective-permute-done | bytes 524320 | tf_op jit(solution)/shard_map/ppermute | solution.py:23
  253.9 3.6 %collective-permute-done.15 = bf16[128,2048]{1,0:T(8,128)(2,1)S(1)} collective-permute-done((bf16[128,2048]{1,0:T(8,128)(2,1)S(1)}, bf16[128,2048]{1,0:T(8,128)(2,1)S(1)}, u32[]{:S(2)}, u32[]{:S(2)}) %collective-permute-start.15) | collective-permute-done | bytes 524320 | tf_op jit(solution)/shard_map/ppermute | solution.py:23
  257.4 5.6 %collective-permute-done.11 = bf16[128,2048]{1,0:T(8,128)(2,1)S(1)} collective-permute-done((bf16[128,2048]{1,0:T(8,128)(2,1)S(1)}, bf16[128,2048]{1,0:T(8,128)(2,1)S(1)}, u32[]{:S(2)}, u32[]{:S(2)}) %collective-permute-start.11) | collective-permute-done | bytes 524320 | tf_op jit(solution)/shard_map/ppermute | solution.py:23
  264.8 6.0 %collective-permute-start.16 = (bf16[128,2048]{1,0:T(8,128)(2,1)S(1)}, bf16[128,2048]{1,0:T(8,128)(2,1)S(1)}, u32[]{:S(2)}, u32[]{:S(2)}) collective-permute-start(bf16[128,2048]{1,0:T(8,128)(2,1)S(1)} %get-tuple-element.38), channel_id=1, source_target_pairs={{0,1},{1,0},{2,3},{3,2},{4,5},{5,4},{6,7},{7,6},{8,9},{9,8},{10,11... | collective-permute-start | bytes 1572872 | tf_op jit(solution)/shard_map/ppermute | solution.py:14
  (105 shorter events, 60.3 us)
Async XLA Ops:
  0.0 5.0 %collective-permute-start = (bf16[128,2048]{1,0:T(8,128)(2,1)}, bf16[128,2048]{1,0:T(8,128)(2,1)S(1)}, u32[]{:S(2)}, u32[]{:S(2)}) collective-permute-start(bf16[128,2048]{1,0:T(8,128)(2,1)} %param.6), channel_id=1, source_target_pairs={{0,1},{1,0},{2,3},{3,2},{4,5},{5,4},{6,7},{7,6},{8,9},{9,8},{10,11... | collective-permute-start | bytes 1572872 | tf_op jit(solution)/shard_map/ppermute | solution.py:14
  6.2 16.0 %collective-permute-start.1 = (bf16[128,4224]{1,0:T(8,128)(2,1)S(1)}, bf16[128,4224]{1,0:T(8,128)(2,1)S(1)}, u32[]{:S(2)}, u32[]{:S(2)}) collective-permute-start(bf16[128,4224]{1,0:T(8,128)(2,1)S(1)} %fusion.22), channel_id=1, source_target_pairs={{0,32},{1,225},{32,64},{33,1},{64,96},{65,33},{96,128},{97,65},{12... | collective-permute-start | bytes 3244040 | tf_op jit(solution)/shard_map/ppermute | solution.py:23
  22.2 18.6 %copy-start.6 = (bf16[128,4224]{1,0:T(8,128)(2,1)}, bf16[128,4224]{1,0:T(8,128)(2,1)S(1)}, u32[]{:S(2)}) copy-start(bf16[128,4224]{1,0:T(8,128)(2,1)S(1)} %collective-permute-done.1) | copy-start | bytes 3244036
  22.3 15.3 %collective-permute-start.2 = (bf16[128,4224]{1,0:T(8,128)(2,1)S(1)}, bf16[128,4224]{1,0:T(8,128)(2,1)S(1)}, u32[]{:S(2)}, u32[]{:S(2)}) collective-permute-start(bf16[128,4224]{1,0:T(8,128)(2,1)S(1)} %collective-permute-done.1), channel_id=1, source_target_pairs={{0,32},{1,225},{32,64},{33,1},{64,96},{65,33},{96,128},{97,65},{12... | collective-permute-start | bytes 3244040 | tf_op jit(solution)/shard_map/ppermute | solution.py:23
  28.7 40.1 %all-to-all-start = ((bf16[16,16,4096]{2,1,0:T(8,128)(2,1)}), bf16[16,16,4096]{2,1,0:T(8,128)(2,1)}, u32[]{:S(2)}, u32[]{:S(2)}) async-start(bf16[16,16,4096]{2,1,0:T(8,128)(2,1)} %bitcast.3), calls=%async_computation | async-start | bytes 4194304 | tf_op jit(solution)/shard_map/all_to_all | solution.py:114
  37.6 15.2 %collective-permute-start.3 = (bf16[128,4224]{1,0:T(8,128)(2,1)S(1)}, bf16[128,4224]{1,0:T(8,128)(2,1)}, u32[]{:S(2)}, u32[]{:S(2)}) collective-permute-start(bf16[128,4224]{1,0:T(8,128)(2,1)S(1)} %collective-permute-done.2), channel_id=1, source_target_pairs={{0,32},{1,225},{32,64},{33,1},{64,96},{65,33},{96,128},{97,65},{12... | collective-permute-start | bytes 3244040 | tf_op jit(solution)/shard_map/ppermute | solution.py:23
  68.8 14.6 %collective-permute-start.4 = (bf16[128,4224]{1,0:T(8,128)(2,1)}, bf16[128,4224]{1,0:T(8,128)(2,1)}, u32[]{:S(2)}, u32[]{:S(2)}) collective-permute-start(bf16[128,4224]{1,0:T(8,128)(2,1)} %collective-permute-done.3), channel_id=1, source_target_pairs={{0,32},{1,225},{32,64},{33,1},{64,96},{65,33},{96,128},{97,65},{12... | collective-permute-start | bytes 3244040 | tf_op jit(solution)/shard_map/ppermute | solution.py:23
  68.8 27.5 %collective-permute-start.5 = (bf16[4096,384]{1,0:T(8,128)(2,1)S(1)}, bf16[4096,384]{1,0:T(8,128)(2,1)}, u32[]{:S(2)}, u32[]{:S(2)}) collective-permute-start(bf16[4096,384]{1,0:T(8,128)(2,1)S(1)} %bitcast.129), channel_id=1, source_target_pairs={{0,1},{1,0},{2,3},{3,2},{4,5},{5,4},{6,7},{7,6},{8,9},{9,8},{10,11... | collective-permute-start | bytes 9437192 | tf_op jit(solution)/shard_map/ppermute | solution.py:14
  68.8 27.4 %collective-permute-start.6 = (bf16[4096,384]{1,0:T(8,128)(2,1)}, bf16[4096,384]{1,0:T(8,128)(2,1)}, u32[]{:S(2)}, u32[]{:S(2)}) collective-permute-start(bf16[4096,384]{1,0:T(8,128)(2,1)} %bitcast.130), channel_id=1, source_target_pairs={{0,1},{1,0},{2,3},{3,2},{4,5},{5,4},{6,7},{7,6},{8,9},{9,8},{10,11... | collective-permute-start | bytes 9437192 | tf_op jit(solution)/shard_map/ppermute | solution.py:14
  69.3 27.0 %collective-permute-start.7 = (bf16[384,4096]{1,0:T(8,128)(2,1)}, bf16[384,4096]{1,0:T(8,128)(2,1)}, u32[]{:S(2)}, u32[]{:S(2)}) collective-permute-start(bf16[384,4096]{1,0:T(8,128)(2,1)} %bitcast.134), channel_id=1, source_target_pairs={{0,1},{1,0},{2,3},{3,2},{4,5},{5,4},{6,7},{7,6},{8,9},{9,8},{10,11... | collective-permute-start | bytes 9437192 | tf_op jit(solution)/shard_map/ppermute | solution.py:14
  69.5 22.1 %all-to-all-start.2 = ((bf16[16,8,4096]{2,1,0:T(8,128)(2,1)}), bf16[16,8,4096]{2,1,0:T(8,128)(2,1)}, u32[]{:S(2)}, u32[]{:S(2)}) async-start(bf16[16,8,4096]{2,1,0:T(8,128)(2,1)} %fusion.2), calls=%async_computation.2 | async-start | bytes 2097152 | tf_op jit(solution)/shard_map/all_to_all | solution.py:114
  91.6 47.3 %all-to-all-start.1 = ((bf16[16,24,4096]{2,1,0:T(8,128)(2,1)}), bf16[16,24,4096]{2,1,0:T(8,128)(2,1)}, u32[]{:S(2)}, u32[]{:S(2)}) async-start(bf16[16,24,4096]{2,1,0:T(8,128)(2,1)} %bitcast.139), calls=%async_computation.1 | async-start | bytes 6291456 | tf_op jit(solution)/shard_map/all_to_all | solution.py:114
  138.9 20.1 %all-to-all-start.3 = ((bf16[16,8,4096]{2,1,0:T(8,128)(2,1)}), bf16[16,8,4096]{2,1,0:T(8,128)(2,1)S(1)}, u32[]{:S(2)}, u32[]{:S(2)}) async-start(bf16[16,8,4096]{2,1,0:T(8,128)(2,1)} %bitcast.145), calls=%async_computation.3 | async-start | bytes 2097152 | tf_op jit(solution)/shard_map/all_to_all | solution.py:114
  160.0 47.5 %all-to-all-start.4 = ((bf16[16,24,4096]{2,1,0:T(8,128)(2,1)}), bf16[16,24,4096]{2,1,0:T(8,128)(2,1)S(1)}, u32[]{:S(2)}, u32[]{:S(2)}) async-start(bf16[16,24,4096]{2,1,0:T(8,128)(2,1)} %bitcast.138), calls=%async_computation.4 | async-start | bytes 6291456 | tf_op jit(solution)/shard_map/all_to_all | solution.py:114
  208.8 15.0 %collective-permute-start.12 = (bf16[128,2048]{1,0:T(8,128)(2,1)}, bf16[128,2048]{1,0:T(8,128)(2,1)}, u32[]{:S(2)}, u32[]{:S(2)}) collective-permute-start(bf16[128,2048]{1,0:T(8,128)(2,1)} %convolution_convert_fusion), channel_id=1, source_target_pairs={{0,224},{1,33},{32,0},{33,65},{64,32},{65,97},{96,64},{97,129},{12... | collective-permute-start | bytes 1572872 | tf_op jit(solution)/shard_map/ppermute | solution.py:23
  208.8 32.9 %all-to-all-start.5 = ((bf16[16,16,4096]{2,1,0:T(8,128)(2,1)}), bf16[16,16,4096]{2,1,0:T(8,128)(2,1)}, u32[]{:S(2)}, u32[]{:S(2)}) async-start(bf16[16,16,4096]{2,1,0:T(8,128)(2,1)} %bitcast.144), calls=%async_computation.5 | async-start | bytes 4194304 | tf_op jit(solution)/shard_map/all_to_all | solution.py:114
  214.5 15.2 %collective-permute-start.8 = (bf16[128,2048]{1,0:T(8,128)(2,1)S(1)}, bf16[128,2048]{1,0:T(8,128)(2,1)S(1)}, u32[]{:S(2)}, u32[]{:S(2)}) collective-permute-start(bf16[128,2048]{1,0:T(8,128)(2,1)S(1)} %convolution_convert_fusion.1), channel_id=1, source_target_pairs={{0,224},{1,33},{32,0},{33,65},{64,32},{65,97},{96,64},{97,129},{12... | collective-permute-start | bytes 1572872 | tf_op jit(solution)/shard_map/ppermute | solution.py:23
  225.4 10.0 %collective-permute-start.13 = (bf16[128,2048]{1,0:T(8,128)(2,1)S(1)}, bf16[128,2048]{1,0:T(8,128)(2,1)S(1)}, u32[]{:S(2)}, u32[]{:S(2)}) collective-permute-start(bf16[128,2048]{1,0:T(8,128)(2,1)S(1)} %add_convert_fusion.4), channel_id=1, source_target_pairs={{0,224},{1,33},{32,0},{33,65},{64,32},{65,97},{96,64},{97,129},{12... | collective-permute-start | bytes 1572872 | tf_op jit(solution)/shard_map/ppermute | solution.py:23
  230.2 10.8 %collective-permute-start.9 = (bf16[128,2048]{1,0:T(8,128)(2,1)S(1)}, bf16[128,2048]{1,0:T(8,128)(2,1)S(1)}, u32[]{:S(2)}, u32[]{:S(2)}) collective-permute-start(bf16[128,2048]{1,0:T(8,128)(2,1)S(1)} %add_convert_fusion.7), channel_id=1, source_target_pairs={{0,224},{1,33},{32,0},{33,65},{64,32},{65,97},{96,64},{97,129},{12... | collective-permute-start | bytes 1572872 | tf_op jit(solution)/shard_map/ppermute | solution.py:23
  235.8 10.8 %collective-permute-start.14 = (bf16[128,2048]{1,0:T(8,128)(2,1)S(1)}, bf16[128,2048]{1,0:T(8,128)(2,1)S(1)}, u32[]{:S(2)}, u32[]{:S(2)}) collective-permute-start(bf16[128,2048]{1,0:T(8,128)(2,1)S(1)} %add_convert_fusion.3), channel_id=1, source_target_pairs={{0,224},{1,33},{32,0},{33,65},{64,32},{65,97},{96,64},{97,129},{12... | collective-permute-start | bytes 1572872 | tf_op jit(solution)/shard_map/ppermute | solution.py:23
  241.4 10.4 %collective-permute-start.10 = (bf16[128,2048]{1,0:T(8,128)(2,1)S(1)}, bf16[128,2048]{1,0:T(8,128)(2,1)S(1)}, u32[]{:S(2)}, u32[]{:S(2)}) collective-permute-start(bf16[128,2048]{1,0:T(8,128)(2,1)S(1)} %add_convert_fusion.6), channel_id=1, source_target_pairs={{0,224},{1,33},{32,0},{33,65},{64,32},{65,97},{96,64},{97,129},{12... | collective-permute-start | bytes 1572872 | tf_op jit(solution)/shard_map/ppermute | solution.py:23
  247.0 10.4 %collective-permute-start.15 = (bf16[128,2048]{1,0:T(8,128)(2,1)S(1)}, bf16[128,2048]{1,0:T(8,128)(2,1)S(1)}, u32[]{:S(2)}, u32[]{:S(2)}) collective-permute-start(bf16[128,2048]{1,0:T(8,128)(2,1)S(1)} %add_convert_fusion.2), channel_id=1, source_target_pairs={{0,224},{1,33},{32,0},{33,65},{64,32},{65,97},{96,64},{97,129},{12... | collective-permute-start | bytes 1572872 | tf_op jit(solution)/shard_map/ppermute | solution.py:23
  252.2 10.8 %collective-permute-start.11 = (bf16[128,2048]{1,0:T(8,128)(2,1)S(1)}, bf16[128,2048]{1,0:T(8,128)(2,1)S(1)}, u32[]{:S(2)}, u32[]{:S(2)}) collective-permute-start(bf16[128,2048]{1,0:T(8,128)(2,1)S(1)} %add_convert_fusion.5), channel_id=1, source_target_pairs={{0,224},{1,33},{32,0},{33,65},{64,32},{65,97},{96,64},{97,129},{12... | collective-permute-start | bytes 1572872 | tf_op jit(solution)/shard_map/ppermute | solution.py:23
  264.8 7.5 %collective-permute-start.16 = (bf16[128,2048]{1,0:T(8,128)(2,1)S(1)}, bf16[128,2048]{1,0:T(8,128)(2,1)S(1)}, u32[]{:S(2)}, u32[]{:S(2)}) collective-permute-start(bf16[128,2048]{1,0:T(8,128)(2,1)S(1)} %get-tuple-element.38), channel_id=1, source_target_pairs={{0,1},{1,0},{2,3},{3,2},{4,5},{5,4},{6,7},{7,6},{8,9},{9,8},{10,11... | collective-permute-start | bytes 1572872 | tf_op jit(solution)/shard_map/ppermute | solution.py:14
  (7 other events, 61.5 us)

commit v6 on v5

--- a/solution.py
+++ b/solution.py
@@ -40,7 +40,8 @@
         return copies
 
     def outward(k):
-        part = pl.ds(pl.multiple_of(k * tile, tile), tile)
+        column = lax.rem(k + lax.axis_index("tp") * (tiles // 2), tiles)
+        part = pl.ds(pl.multiple_of(column * tile, tile), tile)
         return [
             pltpu.make_async_copy(
                 weight.at[:, part], out_of.at[k, pl.ds(j * half, half), :], out_of_sems.at[k, j]
@@ -231,13 +232,14 @@
                         preferred_element_type=jnp.float32,
                     )
         if k > 0:
-            totals = [
-                around(total.astype(jnp.bfloat16), -1).astype(jnp.float32) for total in totals
-            ]
-    low, high = totals
-    own = jnp.where(core == 0, low, high)
-    other = jnp.where(core == 0, high, low).astype(jnp.bfloat16)
-    return (own + swap(other).astype(jnp.float32)).astype(jnp.bfloat16)
+            kept, given = [total.astype(jnp.bfloat16) for total in totals]
+            kept = tied(kept, given)
+            given = around(given, -1).astype(jnp.float32)
+            kept = around(kept, -1).astype(jnp.float32)
+            totals = [kept, given]
+    kept, given = totals
+    given = swap(given.astype(jnp.bfloat16)).astype(jnp.float32)
+    return (kept + given).astype(jnp.bfloat16)
 
 
 def solution(mesh):

time: 275 us -> 269 us (0.978)
  waiting for transfers between devices: 147 us -> 140 us
    ppermute x12, waiting for transfers between devices: 73.4 us -> 67.7 us  [around(): return lax.ppermute(array, ('z', 'tp'), pairs)]
  transfers between devices with their start and end apart: 23 -> 23, of which waited for: 18 -> 16; matrix products, arithmetic and copies ran while one was open for 12% -> 13% of each run, Pallas kernels for 13% -> 13%
where the time goes in v6:
time: 269 us; the launch traced here: 267 us
  waiting for transfers between devices  140 us (52%)
  starting transfers between devices  52.4 us (19%)
  Pallas kernels  34.3 us (13%)
  matrix products  26.4 us (10%)
  other arithmetic  12.2 us (5%)
    all_to_all x6, waiting for transfers between devices, exchange(): lax.all_to_all(array, ('y', 'x'), split_axis=0, concat_axis=0, tiled=True)  71.5 us
    ppermute x12, waiting for transfers between devices, around(): return lax.ppermute(array, ('z', 'tp'), pairs)  67.7 us
    pallas_call x3, Pallas kernels, run_expert(): pl.pallas_call(expert_kernel, in_specs=[pl.BlockSpec(memory_space=pl.ANY)...  34.3 us
    all_to_all x6, starting transfers between devices, exchange(): lax.all_to_all(array, ('y', 'x'), split_axis=0, concat_axis=0, tiled=True)  31 us
    dot_general x7, matrix products, selected(): jnp.dot(select, blocks[k][:, :model_width], preferred_element_type=jnp.fl...  13.3 us
    dot_general x14, matrix products, on_device(): lax.dot_general(mix, returns[index][:, half * half_width:(half + 1) * hal...  12.5 us
    ppermute x12, starting transfers between devices, around(): return lax.ppermute(array, ('z', 'tp'), pairs)  11 us
    ppermute x5, starting transfers between devices, swap(): return lax.ppermute(array, 'tp', [(0, 1), (1, 0)])  10.4 us
  transfers between devices with their start and end apart: 23, of which 16 were waited for; matrix products, arithmetic and copies ran while one was open for 13% of the time, Pallas kernels for 13%

profile of v6, /device:TPU:1, one launch (start us, length us, event | category | flops | bytes accessed | tf_op | source)
XLA Modules:
  0.0 266.6 jit_solution(17370633193678023615)
XLA Ops:
  0.0 3.2 %collective-permute-start = (bf16[128,2048]{1,0:T(8,128)(2,1)}, bf16[128,2048]{1,0:T(8,128)(2,1)S(1)}, u32[]{:S(2)}, u32[]{:S(2)}) collective-permute-start(bf16[128,2048]{1,0:T(8,128)(2,1)} %param.6), channel_id=1, source_target_pairs={{0,1},{1,0},{2,3},{3,2},{4,5},{5,4},{6,7},{7,6},{8,9},{9,8},{10,11... | collective-permute-start | bytes 1572872 | tf_op jit(solution)/shard_map/ppermute | solution.py:14
  6.2 3.9 %collective-permute-start.1 = (bf16[128,4224]{1,0:T(8,128)(2,1)S(1)}, bf16[128,4224]{1,0:T(8,128)(2,1)S(1)}, u32[]{:S(2)}, u32[]{:S(2)}) collective-permute-start(bf16[128,4224]{1,0:T(8,128)(2,1)S(1)} %fusion.22), channel_id=1, source_target_pairs={{0,32},{1,225},{32,64},{33,1},{64,96},{65,33},{96,128},{97,65},{12... | collective-permute-start | bytes 3244040 | tf_op jit(solution)/shard_map/ppermute | solution.py:23
  10.2 12.0 %collective-permute-done.1 = bf16[128,4224]{1,0:T(8,128)(2,1)S(1)} collective-permute-done((bf16[128,4224]{1,0:T(8,128)(2,1)S(1)}, bf16[128,4224]{1,0:T(8,128)(2,1)S(1)}, u32[]{:S(2)}, u32[]{:S(2)}) %collective-permute-start.1) | collective-permute-done | bytes 1081376 | tf_op jit(solution)/shard_map/ppermute | solution.py:23
  28.7 6.8 %all-to-all-start = ((bf16[16,16,4096]{2,1,0:T(8,128)(2,1)}), bf16[16,16,4096]{2,1,0:T(8,128)(2,1)}, u32[]{:S(2)}, u32[]{:S(2)}) async-start(bf16[16,16,4096]{2,1,0:T(8,128)(2,1)} %bitcast.3), calls=%async_computation | async-start | bytes 4194304 | tf_op jit(solution)/shard_map/all_to_all | solution.py:115
  41.3 11.5 %collective-permute-done.3 = bf16[128,4224]{1,0:T(8,128)(2,1)} collective-permute-done((bf16[128,4224]{1,0:T(8,128)(2,1)S(1)}, bf16[128,4224]{1,0:T(8,128)(2,1)}, u32[]{:S(2)}, u32[]{:S(2)}) %collective-permute-start.3) | collective-permute-done | bytes 1081376 | tf_op jit(solution)/shard_map/ppermute | solution.py:23
  56.7 12.1 %all-to-all-done = bf16[16,16,4096]{2,1,0:T(8,128)(2,1)} async-done(((bf16[16,16,4096]{2,1,0:T(8,128)(2,1)}), bf16[16,16,4096]{2,1,0:T(8,128)(2,1)}, u32[]{:S(2)}, u32[]{:S(2)}) %all-to-all-start) | async-done | bytes 2097184 | tf_op jit(solution)/shard_map/all_to_all | solution.py:115
  69.5 4.4 %all-to-all-start.2 = ((bf16[16,8,4096]{2,1,0:T(8,128)(2,1)}), bf16[16,8,4096]{2,1,0:T(8,128)(2,1)}, u32[]{:S(2)}, u32[]{:S(2)}) async-start(bf16[16,8,4096]{2,1,0:T(8,128)(2,1)} %fusion.2), calls=%async_computation.2 | async-start | bytes 2097152 | tf_op jit(solution)/shard_map/all_to_all | solution.py:115
  74.0 9.4 %collective-permute-done.4 = bf16[128,4224]{1,0:T(8,128)(2,1)} collective-permute-done((bf16[128,4224]{1,0:T(8,128)(2,1)}, bf16[128,4224]{1,0:T(8,128)(2,1)}, u32[]{:S(2)}, u32[]{:S(2)}) %collective-permute-start.4) | collective-permute-done | bytes 1081376 | tf_op jit(solution)/shard_map/ppermute | solution.py:23
  91.6 4.7 %all-to-all-start.1 = ((bf16[16,24,4096]{2,1,0:T(8,128)(2,1)}), bf16[16,24,4096]{2,1,0:T(8,128)(2,1)}, u32[]{:S(2)}, u32[]{:S(2)}) async-start(bf16[16,24,4096]{2,1,0:T(8,128)(2,1)} %bitcast.139), calls=%async_computation.1 | async-start | bytes 6291456 | tf_op jit(solution)/shard_map/all_to_all | solution.py:115
  96.3 11.4 %shard_map.66 = bf16[256,4096]{1,0:T(8,128)(2,1)} custom-call(bf16[256,4096]{1,0:T(8,128)(2,1)} %bitcast.19.x, bf16[4096,384]{1,0:T(8,128)(2,1)} %bitcast.126, bf16[4096,384]{1,0:T(8,128)(2,1)} %collective-permute-done.5.gate_b, bf16[4096,384]{1,0:T(8,128)(2,1)} %bitcast.131, bf16[4096,384]{1,0:T(8,128)(2,1)} %collective-permute-done.6.up_b, ...), custom_call_target="tpu_custom_call" | custom-call | tf_op jit(solution)/shard_map/pallas_call | solution.py:90
  107.7 9.8 %shard_map.65 = bf16[128,4096]{1,0:T(8,128)(2,1)} custom-call(bf16[128,4096]{1,0:T(8,128)(2,1)} %bitcast.17.x, bf16[4096,384]{1,0:T(8,128)(2,1)} %bitcast.127, bf16[4096,384]{1,0:T(8,128)(2,1)} %collective-permute-done.5.gate_b, bf16[4096,384]{1,0:T(8,128)(2,1)} %bitcast.132, bf16[4096,384]{1,0:T(8,128)(2,1)} %collective-permute-done.6.up_b, ...), custom_call_target="tpu_custom_call" | custom-call | tf_op jit(solution)/shard_map/pallas_call | solution.py:90
  117.5 21.4 %all-to-all-done.1 = bf16[16,24,4096]{2,1,0:T(8,128)(2,1)} async-done(((bf16[16,24,4096]{2,1,0:T(8,128)(2,1)}), bf16[16,24,4096]{2,1,0:T(8,128)(2,1)}, u32[]{:S(2)}, u32[]{:S(2)}) %all-to-all-start.1) | async-done | bytes 3145760 | tf_op jit(solution)/shard_map/all_to_all | solution.py:115
  138.9 5.0 %all-to-all-start.3 = ((bf16[16,8,4096]{2,1,0:T(8,128)(2,1)}), bf16[16,8,4096]{2,1,0:T(8,128)(2,1)S(1)}, u32[]{:S(2)}, u32[]{:S(2)}) async-start(bf16[16,8,4096]{2,1,0:T(8,128)(2,1)} %bitcast.145), calls=%async_computation.3 | async-start | bytes 2097152 | tf_op jit(solution)/shard_map/all_to_all | solution.py:115
  143.9 13.2 %shard_map.64 = bf16[384,4096]{1,0:T(8,128)(2,1)} custom-call(bf16[384,4096]{1,0:T(8,128)(2,1)} %bitcast.12.x, bf16[4096,384]{1,0:T(8,128)(2,1)} %bitcast.128, bf16[4096,384]{1,0:T(8,128)(2,1)} %collective-permute-done.5.gate_b, bf16[4096,384]{1,0:T(8,128)(2,1)} %bitcast.133, bf16[4096,384]{1,0:T(8,128)(2,1)} %collective-permute-done.6.up_b, ...), custom_call_target="tpu_custom_call" | custom-call | tf_op jit(solution)/shard_map/pallas_call | solution.py:90
  160.1 5.0 %all-to-all-start.4 = ((bf16[16,24,4096]{2,1,0:T(8,128)(2,1)}), bf16[16,24,4096]{2,1,0:T(8,128)(2,1)S(1)}, u32[]{:S(2)}, u32[]{:S(2)}) async-start(bf16[16,24,4096]{2,1,0:T(8,128)(2,1)} %bitcast.138), calls=%async_computation.4 | async-start | bytes 6291456 | tf_op jit(solution)/shard_map/all_to_all | solution.py:115
  171.6 36.0 %all-to-all-done.4 = bf16[16,24,4096]{2,1,0:T(8,128)(2,1)S(1)} async-done(((bf16[16,24,4096]{2,1,0:T(8,128)(2,1)}), bf16[16,24,4096]{2,1,0:T(8,128)(2,1)S(1)}, u32[]{:S(2)}, u32[]{:S(2)}) %all-to-all-start.4) | async-done | bytes 3145760 | tf_op jit(solution)/shard_map/all_to_all | solution.py:115
  208.9 5.2 %all-to-all-start.5 = ((bf16[16,16,4096]{2,1,0:T(8,128)(2,1)}), bf16[16,16,4096]{2,1,0:T(8,128)(2,1)}, u32[]{:S(2)}, u32[]{:S(2)}) async-start(bf16[16,16,4096]{2,1,0:T(8,128)(2,1)} %bitcast.144), calls=%async_computation.5 | async-start | bytes 4194304 | tf_op jit(solution)/shard_map/all_to_all | solution.py:115
  215.1 8.7 %collective-permute-done.9 = bf16[128,2048]{1,0:T(8,128)(2,1)} collective-permute-done((bf16[128,2048]{1,0:T(8,128)(2,1)}, bf16[128,2048]{1,0:T(8,128)(2,1)}, u32[]{:S(2)}, u32[]{:S(2)}) %collective-permute-start.9) | collective-permute-done | bytes 524320 | tf_op jit(solution)/shard_map/ppermute | solution.py:23
  225.4 4.3 %collective-permute-done.8 = bf16[128,2048]{1,0:T(8,128)(2,1)S(1)} collective-permute-done((bf16[128,2048]{1,0:T(8,128)(2,1)S(1)}, bf16[128,2048]{1,0:T(8,128)(2,1)S(1)}, u32[]{:S(2)}, u32[]{:S(2)}) %collective-permute-start.8) | collective-permute-done | bytes 524320 | tf_op jit(solution)/shard_map/ppermute | solution.py:23
  230.7 4.6 %collective-permute-done.11 = bf16[128,2048]{1,0:T(8,128)(2,1)S(1)} collective-permute-done((bf16[128,2048]{1,0:T(8,128)(2,1)S(1)}, bf16[128,2048]{1,0:T(8,128)(2,1)S(1)}, u32[]{:S(2)}, u32[]{:S(2)}) %collective-permute-start.11) | collective-permute-done | bytes 524320 | tf_op jit(solution)/shard_map/ppermute | solution.py:23
  235.8 5.1 %collective-permute-done.10 = bf16[128,2048]{1,0:T(8,128)(2,1)S(1)} collective-permute-done((bf16[128,2048]{1,0:T(8,128)(2,1)S(1)}, bf16[128,2048]{1,0:T(8,128)(2,1)S(1)}, u32[]{:S(2)}, u32[]{:S(2)}) %collective-permute-start.10) | collective-permute-done | bytes 524320 | tf_op jit(solution)/shard_map/ppermute | solution.py:23
  243.2 3.3 %collective-permute-done.13 = bf16[128,2048]{1,0:T(8,128)(2,1)S(1)} collective-permute-done((bf16[128,2048]{1,0:T(8,128)(2,1)S(1)}, bf16[128,2048]{1,0:T(8,128)(2,1)S(1)}, u32[]{:S(2)}, u32[]{:S(2)}) %collective-permute-start.13) | collective-permute-done | bytes 524320 | tf_op jit(solution)/shard_map/ppermute | solution.py:23
  253.8 3.6 %collective-permute-done.15 = bf16[128,2048]{1,0:T(8,128)(2,1)S(1)} collective-permute-done((bf16[128,2048]{1,0:T(8,128)(2,1)S(1)}, bf16[128,2048]{1,0:T(8,128)(2,1)S(1)}, u32[]{:S(2)}, u32[]{:S(2)}) %collective-permute-start.15) | collective-permute-done | bytes 524320 | tf_op jit(solution)/shard_map/ppermute | solution.py:23
  257.5 6.5 %collective-permute-start.16 = (bf16[128,2048]{1,0:T(8,128)(2,1)S(1)}, bf16[128,2048]{1,0:T(8,128)(2,1)S(1)}, u32[]{:S(2)}, u32[]{:S(2)}) collective-permute-start(bf16[128,2048]{1,0:T(8,128)(2,1)S(1)} %add_convert_fusion.2), channel_id=1, source_target_pairs={{0,1},{1,0},{2,3},{3,2},{4,5},{5,4},{6,7},{7,6},{8,9},{9,8},{10,11... | collective-permute-start | bytes 1572872 | tf_op jit(solution)/shard_map/ppermute | solution.py:14
  (106 shorter events, 55.3 us)
Async XLA Ops:
  0.0 5.0 %collective-permute-start = (bf16[128,2048]{1,0:T(8,128)(2,1)}, bf16[128,2048]{1,0:T(8,128)(2,1)S(1)}, u32[]{:S(2)}, u32[]{:S(2)}) collective-permute-start(bf16[128,2048]{1,0:T(8,128)(2,1)} %param.6), channel_id=1, source_target_pairs={{0,1},{1,0},{2,3},{3,2},{4,5},{5,4},{6,7},{7,6},{8,9},{9,8},{10,11... | collective-permute-start | bytes 1572872 | tf_op jit(solution)/shard_map/ppermute | solution.py:14
  6.2 16.0 %collective-permute-start.1 = (bf16[128,4224]{1,0:T(8,128)(2,1)S(1)}, bf16[128,4224]{1,0:T(8,128)(2,1)S(1)}, u32[]{:S(2)}, u32[]{:S(2)}) collective-permute-start(bf16[128,4224]{1,0:T(8,128)(2,1)S(1)} %fusion.22), channel_id=1, source_target_pairs={{0,32},{1,225},{32,64},{33,1},{64,96},{65,33},{96,128},{97,65},{12... | collective-permute-start | bytes 3244040 | tf_op jit(solution)/shard_map/ppermute | solution.py:23
  22.2 18.6 %copy-start.6 = (bf16[128,4224]{1,0:T(8,128)(2,1)}, bf16[128,4224]{1,0:T(8,128)(2,1)S(1)}, u32[]{:S(2)}) copy-start(bf16[128,4224]{1,0:T(8,128)(2,1)S(1)} %collective-permute-done.1) | copy-start | bytes 3244036
  22.3 15.3 %collective-permute-start.2 = (bf16[128,4224]{1,0:T(8,128)(2,1)S(1)}, bf16[128,4224]{1,0:T(8,128)(2,1)S(1)}, u32[]{:S(2)}, u32[]{:S(2)}) collective-permute-start(bf16[128,4224]{1,0:T(8,128)(2,1)S(1)} %collective-permute-done.1), channel_id=1, source_target_pairs={{0,32},{1,225},{32,64},{33,1},{64,96},{65,33},{96,128},{97,65},{12... | collective-permute-start | bytes 3244040 | tf_op jit(solution)/shard_map/ppermute | solution.py:23
  28.7 40.1 %all-to-all-start = ((bf16[16,16,4096]{2,1,0:T(8,128)(2,1)}), bf16[16,16,4096]{2,1,0:T(8,128)(2,1)}, u32[]{:S(2)}, u32[]{:S(2)}) async-start(bf16[16,16,4096]{2,1,0:T(8,128)(2,1)} %bitcast.3), calls=%async_computation | async-start | bytes 4194304 | tf_op jit(solution)/shard_map/all_to_all | solution.py:115
  37.6 15.2 %collective-permute-start.3 = (bf16[128,4224]{1,0:T(8,128)(2,1)S(1)}, bf16[128,4224]{1,0:T(8,128)(2,1)}, u32[]{:S(2)}, u32[]{:S(2)}) collective-permute-start(bf16[128,4224]{1,0:T(8,128)(2,1)S(1)} %collective-permute-done.2), channel_id=1, source_target_pairs={{0,32},{1,225},{32,64},{33,1},{64,96},{65,33},{96,128},{97,65},{12... | collective-permute-start | bytes 3244040 | tf_op jit(solution)/shard_map/ppermute | solution.py:23
  68.8 14.6 %collective-permute-start.4 = (bf16[128,4224]{1,0:T(8,128)(2,1)}, bf16[128,4224]{1,0:T(8,128)(2,1)}, u32[]{:S(2)}, u32[]{:S(2)}) collective-permute-start(bf16[128,4224]{1,0:T(8,128)(2,1)} %collective-permute-done.3), channel_id=1, source_target_pairs={{0,32},{1,225},{32,64},{33,1},{64,96},{65,33},{96,128},{97,65},{12... | collective-permute-start | bytes 3244040 | tf_op jit(solution)/shard_map/ppermute | solution.py:23
  68.8 27.5 %collective-permute-start.5 = (bf16[4096,384]{1,0:T(8,128)(2,1)S(1)}, bf16[4096,384]{1,0:T(8,128)(2,1)}, u32[]{:S(2)}, u32[]{:S(2)}) collective-permute-start(bf16[4096,384]{1,0:T(8,128)(2,1)S(1)} %bitcast.129), channel_id=1, source_target_pairs={{0,1},{1,0},{2,3},{3,2},{4,5},{5,4},{6,7},{7,6},{8,9},{9,8},{10,11... | collective-permute-start | bytes 9437192 | tf_op jit(solution)/shard_map/ppermute | solution.py:14
  68.8 27.4 %collective-permute-start.6 = (bf16[4096,384]{1,0:T(8,128)(2,1)}, bf16[4096,384]{1,0:T(8,128)(2,1)}, u32[]{:S(2)}, u32[]{:S(2)}) collective-permute-start(bf16[4096,384]{1,0:T(8,128)(2,1)} %bitcast.130), channel_id=1, source_target_pairs={{0,1},{1,0},{2,3},{3,2},{4,5},{5,4},{6,7},{7,6},{8,9},{9,8},{10,11... | collective-permute-start | bytes 9437192 | tf_op jit(solution)/shard_map/ppermute | solution.py:14
  69.3 27.0 %collective-permute-start.7 = (bf16[384,4096]{1,0:T(8,128)(2,1)}, bf16[384,4096]{1,0:T(8,128)(2,1)}, u32[]{:S(2)}, u32[]{:S(2)}) collective-permute-start(bf16[384,4096]{1,0:T(8,128)(2,1)} %bitcast.134), channel_id=1, source_target_pairs={{0,1},{1,0},{2,3},{3,2},{4,5},{5,4},{6,7},{7,6},{8,9},{9,8},{10,11... | collective-permute-start | bytes 9437192 | tf_op jit(solution)/shard_map/ppermute | solution.py:14
  69.5 22.1 %all-to-all-start.2 = ((bf16[16,8,4096]{2,1,0:T(8,128)(2,1)}), bf16[16,8,4096]{2,1,0:T(8,128)(2,1)}, u32[]{:S(2)}, u32[]{:S(2)}) async-start(bf16[16,8,4096]{2,1,0:T(8,128)(2,1)} %fusion.2), calls=%async_computation.2 | async-start | bytes 2097152 | tf_op jit(solution)/shard_map/all_to_all | solution.py:115
  91.6 47.3 %all-to-all-start.1 = ((bf16[16,24,4096]{2,1,0:T(8,128)(2,1)}), bf16[16,24,4096]{2,1,0:T(8,128)(2,1)}, u32[]{:S(2)}, u32[]{:S(2)}) async-start(bf16[16,24,4096]{2,1,0:T(8,128)(2,1)} %bitcast.139), calls=%async_computation.1 | async-start | bytes 6291456 | tf_op jit(solution)/shard_map/all_to_all | solution.py:115
  138.9 20.1 %all-to-all-start.3 = ((bf16[16,8,4096]{2,1,0:T(8,128)(2,1)}), bf16[16,8,4096]{2,1,0:T(8,128)(2,1)S(1)}, u32[]{:S(2)}, u32[]{:S(2)}) async-start(bf16[16,8,4096]{2,1,0:T(8,128)(2,1)} %bitcast.145), calls=%async_computation.3 | async-start | bytes 2097152 | tf_op jit(solution)/shard_map/all_to_all | solution.py:115
  160.1 47.6 %all-to-all-start.4 = ((bf16[16,24,4096]{2,1,0:T(8,128)(2,1)}), bf16[16,24,4096]{2,1,0:T(8,128)(2,1)S(1)}, u32[]{:S(2)}, u32[]{:S(2)}) async-start(bf16[16,24,4096]{2,1,0:T(8,128)(2,1)} %bitcast.138), calls=%async_computation.4 | async-start | bytes 6291456 | tf_op jit(solution)/shard_map/all_to_all | solution.py:115
  208.9 14.9 %collective-permute-start.9 = (bf16[128,2048]{1,0:T(8,128)(2,1)}, bf16[128,2048]{1,0:T(8,128)(2,1)}, u32[]{:S(2)}, u32[]{:S(2)}) collective-permute-start(bf16[128,2048]{1,0:T(8,128)(2,1)} %convolution_convert_fusion), channel_id=1, source_target_pairs={{0,224},{1,33},{32,0},{33,65},{64,32},{65,97},{96,64},{97,129},{12... | collective-permute-start | bytes 1572872 | tf_op jit(solution)/shard_map/ppermute | solution.py:23
  208.9 32.8 %all-to-all-start.5 = ((bf16[16,16,4096]{2,1,0:T(8,128)(2,1)}), bf16[16,16,4096]{2,1,0:T(8,128)(2,1)}, u32[]{:S(2)}, u32[]{:S(2)}) async-start(bf16[16,16,4096]{2,1,0:T(8,128)(2,1)} %bitcast.144), calls=%async_computation.5 | async-start | bytes 4194304 | tf_op jit(solution)/shard_map/all_to_all | solution.py:115
  214.5 15.2 %collective-permute-start.8 = (bf16[128,2048]{1,0:T(8,128)(2,1)S(1)}, bf16[128,2048]{1,0:T(8,128)(2,1)S(1)}, u32[]{:S(2)}, u32[]{:S(2)}) collective-permute-start(bf16[128,2048]{1,0:T(8,128)(2,1)S(1)} %convolution_convert_fusion.1), channel_id=1, source_target_pairs={{0,224},{1,33},{32,0},{33,65},{64,32},{65,97},{96,64},{97,129},{12... | collective-permute-start | bytes 1572872 | tf_op jit(solution)/shard_map/ppermute | solution.py:23
  225.3 10.0 %collective-permute-start.11 = (bf16[128,2048]{1,0:T(8,128)(2,1)S(1)}, bf16[128,2048]{1,0:T(8,128)(2,1)S(1)}, u32[]{:S(2)}, u32[]{:S(2)}) collective-permute-start(bf16[128,2048]{1,0:T(8,128)(2,1)S(1)} %add_convert_fusion.7), channel_id=1, source_target_pairs={{0,224},{1,33},{32,0},{33,65},{64,32},{65,97},{96,64},{97,129},{12... | collective-permute-start | bytes 1572872 | tf_op jit(solution)/shard_map/ppermute | solution.py:23
  230.2 10.8 %collective-permute-start.10 = (bf16[128,2048]{1,0:T(8,128)(2,1)S(1)}, bf16[128,2048]{1,0:T(8,128)(2,1)S(1)}, u32[]{:S(2)}, u32[]{:S(2)}) collective-permute-start(bf16[128,2048]{1,0:T(8,128)(2,1)S(1)} %add_convert_fusion.8), channel_id=1, source_target_pairs={{0,224},{1,33},{32,0},{33,65},{64,32},{65,97},{96,64},{97,129},{12... | collective-permute-start | bytes 1572872 | tf_op jit(solution)/shard_map/ppermute | solution.py:23
  235.7 10.8 %collective-permute-start.13 = (bf16[128,2048]{1,0:T(8,128)(2,1)S(1)}, bf16[128,2048]{1,0:T(8,128)(2,1)S(1)}, u32[]{:S(2)}, u32[]{:S(2)}) collective-permute-start(bf16[128,2048]{1,0:T(8,128)(2,1)S(1)} %add_convert_fusion.5), channel_id=1, source_target_pairs={{0,224},{1,33},{32,0},{33,65},{64,32},{65,97},{96,64},{97,129},{12... | collective-permute-start | bytes 1572872 | tf_op jit(solution)/shard_map/ppermute | solution.py:23
  241.3 10.4 %collective-permute-start.12 = (bf16[128,2048]{1,0:T(8,128)(2,1)S(1)}, bf16[128,2048]{1,0:T(8,128)(2,1)S(1)}, u32[]{:S(2)}, u32[]{:S(2)}) collective-permute-start(bf16[128,2048]{1,0:T(8,128)(2,1)S(1)} %add_convert_fusion.6), channel_id=1, source_target_pairs={{0,224},{1,33},{32,0},{33,65},{64,32},{65,97},{96,64},{97,129},{12... | collective-permute-start | bytes 1572872 | tf_op jit(solution)/shard_map/ppermute | solution.py:23
  247.0 10.4 %collective-permute-start.15 = (bf16[128,2048]{1,0:T(8,128)(2,1)S(1)}, bf16[128,2048]{1,0:T(8,128)(2,1)S(1)}, u32[]{:S(2)}, u32[]{:S(2)}) collective-permute-start(bf16[128,2048]{1,0:T(8,128)(2,1)S(1)} %add_convert_fusion.3), channel_id=1, source_target_pairs={{0,224},{1,33},{32,0},{33,65},{64,32},{65,97},{96,64},{97,129},{12... | collective-permute-start | bytes 1572872 | tf_op jit(solution)/shard_map/ppermute | solution.py:23
  252.2 13.4 %collective-permute-start.14 = (bf16[128,2048]{1,0:T(8,128)(2,1)S(1)}, bf16[128,2048]{1,0:T(8,128)(2,1)S(1)}, u32[]{:S(2)}, u32[]{:S(2)}) collective-permute-start(bf16[128,2048]{1,0:T(8,128)(2,1)S(1)} %add_convert_fusion.4), channel_id=1, source_target_pairs={{0,224},{1,33},{32,0},{33,65},{64,32},{65,97},{96,64},{97,129},{12... | collective-permute-start | bytes 1572872 | tf_op jit(solution)/shard_map/ppermute | solution.py:23
  257.5 8.1 %collective-permute-start.16 = (bf16[128,2048]{1,0:T(8,128)(2,1)S(1)}, bf16[128,2048]{1,0:T(8,128)(2,1)S(1)}, u32[]{:S(2)}, u32[]{:S(2)}) collective-permute-start(bf16[128,2048]{1,0:T(8,128)(2,1)S(1)} %add_convert_fusion.2), channel_id=1, source_target_pairs={{0,1},{1,0},{2,3},{3,2},{4,5},{5,4},{6,7},{7,6},{8,9},{9,8},{10,11... | collective-permute-start | bytes 1572872 | tf_op jit(solution)/shard_map/ppermute | solution.py:14
  (7 other events, 61.5 us)

commit v7 on v6

--- a/solution.py
+++ b/solution.py
@@ -31,17 +31,21 @@
     half = gate_a.shape[1]
     units = 2 * half
 
+    def turned(k):
+        column = lax.rem(k + lax.axis_index("tp") * (tiles // 2), tiles)
+        return pl.ds(pl.multiple_of(column * tile, tile), tile)
+
     def inward(k):
         part = pl.ds(pl.multiple_of(k * tile, tile), tile)
+        rows = turned(k)
         copies = [pltpu.make_async_copy(x.at[:, part], rows_in.at[k], into_sems.at[k, 4])]
         for j, weight in enumerate((gate_a, gate_b, up_a, up_b)):
             columns = into.at[k, :, pl.ds(j * half, half)]
-            copies.append(pltpu.make_async_copy(weight.at[part, :], columns, into_sems.at[k, j]))
+            copies.append(pltpu.make_async_copy(weight.at[rows, :], columns, into_sems.at[k, j]))
         return copies
 
     def outward(k):
-        column = lax.rem(k + lax.axis_index("tp") * (tiles // 2), tiles)
-        part = pl.ds(pl.multiple_of(column * tile, tile), tile)
+        part = turned(k)
         return [
             pltpu.make_async_copy(
                 weight.at[:, part], out_of.at[k, pl.ds(j * half, half), :], out_of_sems.at[k, j]
@@ -131,10 +135,7 @@
 
     routes = jnp.concatenate([expert_ids, gate_levels], axis=1).T.astype(jnp.bfloat16)
     routes = jnp.pad(routes, ((0, tok_count - 2 * top_count), (0, 128 - tok_count)))
-    received = swap(tokens)
-    low = jnp.where(core == 0, tokens, received)
-    high = jnp.where(core == 0, received, tokens)
-    blocks = [jnp.concatenate([low, high, routes], axis=1)]
+    blocks = [jnp.concatenate([tokens, swap(tokens), routes], axis=1)]
 
     first = lax.axis_index("z") * plane_experts
     plane_ids = first + jnp.arange(plane_experts, dtype=jnp.int32)

time: 269 us -> 270 us (level)
  no operation moved by 1% of the time
where the time goes in v7:
time: 270 us; the launch traced here: 267 us
  waiting for transfers between devices  140 us (52%)
  starting transfers between devices  52.3 us (19%)
  Pallas kernels  34.2 us (13%)
  matrix products  26.4 us (10%)
  other arithmetic  11.4 us (4%)
    all_to_all x6, waiting for transfers between devices, exchange(): lax.all_to_all(array, ('y', 'x'), split_axis=0, concat_axis=0, tiled=True)  71.8 us
    ppermute x12, waiting for transfers between devices, around(): return lax.ppermute(array, ('z', 'tp'), pairs)  67.4 us
    pallas_call x3, Pallas kernels, run_expert(): pl.pallas_call(expert_kernel, in_specs=[pl.BlockSpec(memory_space=pl.ANY)...  34.2 us
    all_to_all x6, starting transfers between devices, exchange(): lax.all_to_all(array, ('y', 'x'), split_axis=0, concat_axis=0, tiled=True)  30.9 us
    dot_general x7, matrix products, selected(): jnp.dot(select, blocks[k][:, :model_width], preferred_element_type=jnp.fl...  13.2 us
    dot_general x14, matrix products, on_device(): lax.dot_general(mix, returns[index][:, half * half_width:(half + 1) * hal...  12.5 us
    ppermute x12, starting transfers between devices, around(): return lax.ppermute(array, ('z', 'tp'), pairs)  11 us
    ppermute x5, starting transfers between devices, swap(): return lax.ppermute(array, 'tp', [(0, 1), (1, 0)])  10.3 us
  transfers between devices with their start and end apart: 23, of which 16 were waited for; matrix products, arithmetic and copies ran while one was open for 13% of the time, Pallas kernels for 13%

profile of v7, /device:TPU:1, one launch (start us, length us, event | category | flops | bytes accessed | tf_op | source)
XLA Modules:
  0.0 266.9 jit_solution(17259421992965011311)
XLA Ops:
  0.0 3.2 %collective-permute-start = (bf16[128,2048]{1,0:T(8,128)(2,1)}, bf16[128,2048]{1,0:T(8,128)(2,1)S(1)}, u32[]{:S(2)}, u32[]{:S(2)}) collective-permute-start(bf16[128,2048]{1,0:T(8,128)(2,1)} %param.6), channel_id=1, source_target_pairs={{0,1},{1,0},{2,3},{3,2},{4,5},{5,4},{6,7},{7,6},{8,9},{9,8},{10,11... | collective-permute-start | bytes 1572872 | tf_op jit(solution)/shard_map/ppermute | solution.py:14
  6.1 3.9 %collective-permute-start.1 = (bf16[128,4224]{1,0:T(8,128)(2,1)S(1)}, bf16[128,4224]{1,0:T(8,128)(2,1)S(1)}, u32[]{:S(2)}, u32[]{:S(2)}) collective-permute-start(bf16[128,4224]{1,0:T(8,128)(2,1)S(1)} %fusion.22), channel_id=1, source_target_pairs={{0,32},{1,225},{32,64},{33,1},{64,96},{65,33},{96,128},{97,65},{12... | collective-permute-start | bytes 3244040 | tf_op jit(solution)/shard_map/ppermute | solution.py:23
  10.1 12.0 %collective-permute-done.1 = bf16[128,4224]{1,0:T(8,128)(2,1)S(1)} collective-permute-done((bf16[128,4224]{1,0:T(8,128)(2,1)S(1)}, bf16[128,4224]{1,0:T(8,128)(2,1)S(1)}, u32[]{:S(2)}, u32[]{:S(2)}) %collective-permute-start.1) | collective-permute-done | bytes 1081376 | tf_op jit(solution)/shard_map/ppermute | solution.py:23
  29.0 6.8 %all-to-all-start = ((bf16[16,16,4096]{2,1,0:T(8,128)(2,1)}), bf16[16,16,4096]{2,1,0:T(8,128)(2,1)}, u32[]{:S(2)}, u32[]{:S(2)}) async-start(bf16[16,16,4096]{2,1,0:T(8,128)(2,1)} %bitcast.3), calls=%async_computation | async-start | bytes 4194304 | tf_op jit(solution)/shard_map/all_to_all | solution.py:119
  41.3 11.5 %collective-permute-done.3 = bf16[128,4224]{1,0:T(8,128)(2,1)S(1)} collective-permute-done((bf16[128,4224]{1,0:T(8,128)(2,1)S(1)}, bf16[128,4224]{1,0:T(8,128)(2,1)S(1)}, u32[]{:S(2)}, u32[]{:S(2)}) %collective-permute-start.3) | collective-permute-done | bytes 1081376 | tf_op jit(solution)/shard_map/ppermute | solution.py:23
  56.8 12.2 %all-to-all-done = bf16[16,16,4096]{2,1,0:T(8,128)(2,1)} async-done(((bf16[16,16,4096]{2,1,0:T(8,128)(2,1)}), bf16[16,16,4096]{2,1,0:T(8,128)(2,1)}, u32[]{:S(2)}, u32[]{:S(2)}) %all-to-all-start) | async-done | bytes 2097184 | tf_op jit(solution)/shard_map/all_to_all | solution.py:119
  69.7 4.3 %all-to-all-start.2 = ((bf16[16,8,4096]{2,1,0:T(8,128)(2,1)}), bf16[16,8,4096]{2,1,0:T(8,128)(2,1)}, u32[]{:S(2)}, u32[]{:S(2)}) async-start(bf16[16,8,4096]{2,1,0:T(8,128)(2,1)} %fusion.2), calls=%async_computation.2 | async-start | bytes 2097152 | tf_op jit(solution)/shard_map/all_to_all | solution.py:119
  74.2 9.4 %collective-permute-done.4 = bf16[128,4224]{1,0:T(8,128)(2,1)} collective-permute-done((bf16[128,4224]{1,0:T(8,128)(2,1)}, bf16[128,4224]{1,0:T(8,128)(2,1)}, u32[]{:S(2)}, u32[]{:S(2)}) %collective-permute-start.4) | collective-permute-done | bytes 1081376 | tf_op jit(solution)/shard_map/ppermute | solution.py:23
  91.8 4.7 %all-to-all-start.1 = ((bf16[16,24,4096]{2,1,0:T(8,128)(2,1)}), bf16[16,24,4096]{2,1,0:T(8,128)(2,1)}, u32[]{:S(2)}, u32[]{:S(2)}) async-start(bf16[16,24,4096]{2,1,0:T(8,128)(2,1)} %bitcast.139), calls=%async_computation.1 | async-start | bytes 6291456 | tf_op jit(solution)/shard_map/all_to_all | solution.py:119
  96.5 11.4 %shard_map.66 = bf16[256,4096]{1,0:T(8,128)(2,1)} custom-call(bf16[256,4096]{1,0:T(8,128)(2,1)} %bitcast.19.x, bf16[4096,384]{1,0:T(8,128)(2,1)} %bitcast.126, bf16[4096,384]{1,0:T(8,128)(2,1)} %collective-permute-done.5.gate_b, bf16[4096,384]{1,0:T(8,128)(2,1)} %bitcast.131, bf16[4096,384]{1,0:T(8,128)(2,1)} %collective-permute-done.6.up_b, ...), custom_call_target="tpu_custom_call" | custom-call | tf_op jit(solution)/shard_map/pallas_call | solution.py:94
  107.9 9.7 %shard_map.65 = bf16[128,4096]{1,0:T(8,128)(2,1)} custom-call(bf16[128,4096]{1,0:T(8,128)(2,1)} %bitcast.17.x, bf16[4096,384]{1,0:T(8,128)(2,1)} %bitcast.127, bf16[4096,384]{1,0:T(8,128)(2,1)} %collective-permute-done.5.gate_b, bf16[4096,384]{1,0:T(8,128)(2,1)} %bitcast.132, bf16[4096,384]{1,0:T(8,128)(2,1)} %collective-permute-done.6.up_b, ...), custom_call_target="tpu_custom_call" | custom-call | tf_op jit(solution)/shard_map/pallas_call | solution.py:94
  117.7 21.4 %all-to-all-done.1 = bf16[16,24,4096]{2,1,0:T(8,128)(2,1)} async-done(((bf16[16,24,4096]{2,1,0:T(8,128)(2,1)}), bf16[16,24,4096]{2,1,0:T(8,128)(2,1)}, u32[]{:S(2)}, u32[]{:S(2)}) %all-to-all-start.1) | async-done | bytes 3145760 | tf_op jit(solution)/shard_map/all_to_all | solution.py:119
  139.1 5.0 %all-to-all-start.3 = ((bf16[16,8,4096]{2,1,0:T(8,128)(2,1)}), bf16[16,8,4096]{2,1,0:T(8,128)(2,1)S(1)}, u32[]{:S(2)}, u32[]{:S(2)}) async-start(bf16[16,8,4096]{2,1,0:T(8,128)(2,1)} %bitcast.145), calls=%async_computation.3 | async-start | bytes 2097152 | tf_op jit(solution)/shard_map/all_to_all | solution.py:119
  144.1 13.1 %shard_map.64 = bf16[384,4096]{1,0:T(8,128)(2,1)} custom-call(bf16[384,4096]{1,0:T(8,128)(2,1)} %bitcast.12.x, bf16[4096,384]{1,0:T(8,128)(2,1)} %bitcast.128, bf16[4096,384]{1,0:T(8,128)(2,1)} %collective-permute-done.5.gate_b, bf16[4096,384]{1,0:T(8,128)(2,1)} %bitcast.133, bf16[4096,384]{1,0:T(8,128)(2,1)} %collective-permute-done.6.up_b, ...), custom_call_target="tpu_custom_call" | custom-call | tf_op jit(solution)/shard_map/pallas_call | solution.py:94
  160.3 5.0 %all-to-all-start.4 = ((bf16[16,24,4096]{2,1,0:T(8,128)(2,1)}), bf16[16,24,4096]{2,1,0:T(8,128)(2,1)S(1)}, u32[]{:S(2)}, u32[]{:S(2)}) async-start(bf16[16,24,4096]{2,1,0:T(8,128)(2,1)} %bitcast.138), calls=%async_computation.4 | async-start | bytes 6291456 | tf_op jit(solution)/shard_map/all_to_all | solution.py:119
  171.8 36.1 %all-to-all-done.4 = bf16[16,24,4096]{2,1,0:T(8,128)(2,1)S(1)} async-done(((bf16[16,24,4096]{2,1,0:T(8,128)(2,1)}), bf16[16,24,4096]{2,1,0:T(8,128)(2,1)S(1)}, u32[]{:S(2)}, u32[]{:S(2)}) %all-to-all-start.4) | async-done | bytes 3145760 | tf_op jit(solution)/shard_map/all_to_all | solution.py:119
  209.2 5.1 %all-to-all-start.5 = ((bf16[16,16,4096]{2,1,0:T(8,128)(2,1)}), bf16[16,16,4096]{2,1,0:T(8,128)(2,1)}, u32[]{:S(2)}, u32[]{:S(2)}) async-start(bf16[16,16,4096]{2,1,0:T(8,128)(2,1)} %bitcast.144), calls=%async_computation.5 | async-start | bytes 4194304 | tf_op jit(solution)/shard_map/all_to_all | solution.py:119
  215.4 8.7 %collective-permute-done.9 = bf16[128,2048]{1,0:T(8,128)(2,1)} collective-permute-done((bf16[128,2048]{1,0:T(8,128)(2,1)}, bf16[128,2048]{1,0:T(8,128)(2,1)}, u32[]{:S(2)}, u32[]{:S(2)}) %collective-permute-start.9) | collective-permute-done | bytes 524320 | tf_op jit(solution)/shard_map/ppermute | solution.py:23
  225.7 4.3 %collective-permute-done.8 = bf16[128,2048]{1,0:T(8,128)(2,1)S(1)} collective-permute-done((bf16[128,2048]{1,0:T(8,128)(2,1)S(1)}, bf16[128,2048]{1,0:T(8,128)(2,1)S(1)}, u32[]{:S(2)}, u32[]{:S(2)}) %collective-permute-start.8) | collective-permute-done | bytes 524320 | tf_op jit(solution)/shard_map/ppermute | solution.py:23
  231.1 4.6 %collective-permute-done.11 = bf16[128,2048]{1,0:T(8,128)(2,1)S(1)} collective-permute-done((bf16[128,2048]{1,0:T(8,128)(2,1)S(1)}, bf16[128,2048]{1,0:T(8,128)(2,1)S(1)}, u32[]{:S(2)}, u32[]{:S(2)}) %collective-permute-start.11) | collective-permute-done | bytes 524320 | tf_op jit(solution)/shard_map/ppermute | solution.py:23
  236.1 5.1 %collective-permute-done.10 = bf16[128,2048]{1,0:T(8,128)(2,1)S(1)} collective-permute-done((bf16[128,2048]{1,0:T(8,128)(2,1)S(1)}, bf16[128,2048]{1,0:T(8,128)(2,1)S(1)}, u32[]{:S(2)}, u32[]{:S(2)}) %collective-permute-start.10) | collective-permute-done | bytes 524320 | tf_op jit(solution)/shard_map/ppermute | solution.py:23
  243.5 3.3 %collective-permute-done.13 = bf16[128,2048]{1,0:T(8,128)(2,1)S(1)} collective-permute-done((bf16[128,2048]{1,0:T(8,128)(2,1)S(1)}, bf16[128,2048]{1,0:T(8,128)(2,1)S(1)}, u32[]{:S(2)}, u32[]{:S(2)}) %collective-permute-start.13) | collective-permute-done | bytes 524320 | tf_op jit(solution)/shard_map/ppermute | solution.py:23
  254.1 3.6 %collective-permute-done.15 = bf16[128,2048]{1,0:T(8,128)(2,1)S(1)} collective-permute-done((bf16[128,2048]{1,0:T(8,128)(2,1)S(1)}, bf16[128,2048]{1,0:T(8,128)(2,1)S(1)}, u32[]{:S(2)}, u32[]{:S(2)}) %collective-permute-start.15) | collective-permute-done | bytes 524320 | tf_op jit(solution)/shard_map/ppermute | solution.py:23
  257.8 6.5 %collective-permute-start.16 = (bf16[128,2048]{1,0:T(8,128)(2,1)S(1)}, bf16[128,2048]{1,0:T(8,128)(2,1)S(1)}, u32[]{:S(2)}, u32[]{:S(2)}) collective-permute-start(bf16[128,2048]{1,0:T(8,128)(2,1)S(1)} %add_convert_fusion.2), channel_id=1, source_target_pairs={{0,1},{1,0},{2,3},{3,2},{4,5},{5,4},{6,7},{7,6},{8,9},{9,8},{10,11... | collective-permute-start | bytes 1572872 | tf_op jit(solution)/shard_map/ppermute | solution.py:14
  (109 shorter events, 55.4 us)
Async XLA Ops:
  0.0 5.0 %collective-permute-start = (bf16[128,2048]{1,0:T(8,128)(2,1)}, bf16[128,2048]{1,0:T(8,128)(2,1)S(1)}, u32[]{:S(2)}, u32[]{:S(2)}) collective-permute-start(bf16[128,2048]{1,0:T(8,128)(2,1)} %param.6), channel_id=1, source_target_pairs={{0,1},{1,0},{2,3},{3,2},{4,5},{5,4},{6,7},{7,6},{8,9},{9,8},{10,11... | collective-permute-start | bytes 1572872 | tf_op jit(solution)/shard_map/ppermute | solution.py:14
  6.1 16.0 %collective-permute-start.1 = (bf16[128,4224]{1,0:T(8,128)(2,1)S(1)}, bf16[128,4224]{1,0:T(8,128)(2,1)S(1)}, u32[]{:S(2)}, u32[]{:S(2)}) collective-permute-start(bf16[128,4224]{1,0:T(8,128)(2,1)S(1)} %fusion.22), channel_id=1, source_target_pairs={{0,32},{1,225},{32,64},{33,1},{64,96},{65,33},{96,128},{97,65},{12... | collective-permute-start | bytes 3244040 | tf_op jit(solution)/shard_map/ppermute | solution.py:23
  22.1 18.6 %copy-start.6 = (bf16[128,4224]{1,0:T(8,128)(2,1)}, bf16[128,4224]{1,0:T(8,128)(2,1)S(1)}, u32[]{:S(2)}) copy-start(bf16[128,4224]{1,0:T(8,128)(2,1)S(1)} %collective-permute-done.1) | copy-start | bytes 3244036
  22.3 15.3 %collective-permute-start.2 = (bf16[128,4224]{1,0:T(8,128)(2,1)S(1)}, bf16[128,4224]{1,0:T(8,128)(2,1)S(1)}, u32[]{:S(2)}, u32[]{:S(2)}) collective-permute-start(bf16[128,4224]{1,0:T(8,128)(2,1)S(1)} %collective-permute-done.1), channel_id=1, source_target_pairs={{0,32},{1,225},{32,64},{33,1},{64,96},{65,33},{96,128},{97,65},{12... | collective-permute-start | bytes 3244040 | tf_op jit(solution)/shard_map/ppermute | solution.py:23
  29.0 40.1 %all-to-all-start = ((bf16[16,16,4096]{2,1,0:T(8,128)(2,1)}), bf16[16,16,4096]{2,1,0:T(8,128)(2,1)}, u32[]{:S(2)}, u32[]{:S(2)}) async-start(bf16[16,16,4096]{2,1,0:T(8,128)(2,1)} %bitcast.3), calls=%async_computation | async-start | bytes 4194304 | tf_op jit(solution)/shard_map/all_to_all | solution.py:119
  37.5 15.2 %collective-permute-start.3 = (bf16[128,4224]{1,0:T(8,128)(2,1)S(1)}, bf16[128,4224]{1,0:T(8,128)(2,1)S(1)}, u32[]{:S(2)}, u32[]{:S(2)}) collective-permute-start(bf16[128,4224]{1,0:T(8,128)(2,1)S(1)} %collective-permute-done.2), channel_id=1, source_target_pairs={{0,32},{1,225},{32,64},{33,1},{64,96},{65,33},{96,128},{97,65},{12... | collective-permute-start | bytes 3244040 | tf_op jit(solution)/shard_map/ppermute | solution.py:23
  69.0 14.6 %collective-permute-start.4 = (bf16[128,4224]{1,0:T(8,128)(2,1)}, bf16[128,4224]{1,0:T(8,128)(2,1)}, u32[]{:S(2)}, u32[]{:S(2)}) collective-permute-start(bf16[128,4224]{1,0:T(8,128)(2,1)} %copy-done.8), channel_id=1, source_target_pairs={{0,32},{1,225},{32,64},{33,1},{64,96},{65,33},{96,128},{97,65},{12... | collective-permute-start | bytes 3244040 | tf_op jit(solution)/shard_map/ppermute | solution.py:23
  69.0 27.5 %collective-permute-start.5 = (bf16[4096,384]{1,0:T(8,128)(2,1)S(1)}, bf16[4096,384]{1,0:T(8,128)(2,1)}, u32[]{:S(2)}, u32[]{:S(2)}) collective-permute-start(bf16[4096,384]{1,0:T(8,128)(2,1)S(1)} %bitcast.129), channel_id=1, source_target_pairs={{0,1},{1,0},{2,3},{3,2},{4,5},{5,4},{6,7},{7,6},{8,9},{9,8},{10,11... | collective-permute-start | bytes 9437192 | tf_op jit(solution)/shard_map/ppermute | solution.py:14
  69.1 27.4 %collective-permute-start.6 = (bf16[4096,384]{1,0:T(8,128)(2,1)}, bf16[4096,384]{1,0:T(8,128)(2,1)}, u32[]{:S(2)}, u32[]{:S(2)}) collective-permute-start(bf16[4096,384]{1,0:T(8,128)(2,1)} %bitcast.130), channel_id=1, source_target_pairs={{0,1},{1,0},{2,3},{3,2},{4,5},{5,4},{6,7},{7,6},{8,9},{9,8},{10,11... | collective-permute-start | bytes 9437192 | tf_op jit(solution)/shard_map/ppermute | solution.py:14
  69.6 27.0 %collective-permute-start.7 = (bf16[384,4096]{1,0:T(8,128)(2,1)}, bf16[384,4096]{1,0:T(8,128)(2,1)}, u32[]{:S(2)}, u32[]{:S(2)}) collective-permute-start(bf16[384,4096]{1,0:T(8,128)(2,1)} %bitcast.134), channel_id=1, source_target_pairs={{0,1},{1,0},{2,3},{3,2},{4,5},{5,4},{6,7},{7,6},{8,9},{9,8},{10,11... | collective-permute-start | bytes 9437192 | tf_op jit(solution)/shard_map/ppermute | solution.py:14
  69.7 22.1 %all-to-all-start.2 = ((bf16[16,8,4096]{2,1,0:T(8,128)(2,1)}), bf16[16,8,4096]{2,1,0:T(8,128)(2,1)}, u32[]{:S(2)}, u32[]{:S(2)}) async-start(bf16[16,8,4096]{2,1,0:T(8,128)(2,1)} %fusion.2), calls=%async_computation.2 | async-start | bytes 2097152 | tf_op jit(solution)/shard_map/all_to_all | solution.py:119
  91.8 47.2 %all-to-all-start.1 = ((bf16[16,24,4096]{2,1,0:T(8,128)(2,1)}), bf16[16,24,4096]{2,1,0:T(8,128)(2,1)}, u32[]{:S(2)}, u32[]{:S(2)}) async-start(bf16[16,24,4096]{2,1,0:T(8,128)(2,1)} %bitcast.139), calls=%async_computation.1 | async-start | bytes 6291456 | tf_op jit(solution)/shard_map/all_to_all | solution.py:119
  139.1 20.2 %all-to-all-start.3 = ((bf16[16,8,4096]{2,1,0:T(8,128)(2,1)}), bf16[16,8,4096]{2,1,0:T(8,128)(2,1)S(1)}, u32[]{:S(2)}, u32[]{:S(2)}) async-start(bf16[16,8,4096]{2,1,0:T(8,128)(2,1)} %bitcast.145), calls=%async_computation.3 | async-start | bytes 2097152 | tf_op jit(solution)/shard_map/all_to_all | solution.py:119
  160.3 47.7 %all-to-all-start.4 = ((bf16[16,24,4096]{2,1,0:T(8,128)(2,1)}), bf16[16,24,4096]{2,1,0:T(8,128)(2,1)S(1)}, u32[]{:S(2)}, u32[]{:S(2)}) async-start(bf16[16,24,4096]{2,1,0:T(8,128)(2,1)} %bitcast.138), calls=%async_computation.4 | async-start | bytes 6291456 | tf_op jit(solution)/shard_map/all_to_all | solution.py:119
  209.2 14.9 %collective-permute-start.9 = (bf16[128,2048]{1,0:T(8,128)(2,1)}, bf16[128,2048]{1,0:T(8,128)(2,1)}, u32[]{:S(2)}, u32[]{:S(2)}) collective-permute-start(bf16[128,2048]{1,0:T(8,128)(2,1)} %convolution_convert_fusion), channel_id=1, source_target_pairs={{0,224},{1,33},{32,0},{33,65},{64,32},{65,97},{96,64},{97,129},{12... | collective-permute-start | bytes 1572872 | tf_op jit(solution)/shard_map/ppermute | solution.py:23
  209.2 32.8 %all-to-all-start.5 = ((bf16[16,16,4096]{2,1,0:T(8,128)(2,1)}), bf16[16,16,4096]{2,1,0:T(8,128)(2,1)}, u32[]{:S(2)}, u32[]{:S(2)}) async-start(bf16[16,16,4096]{2,1,0:T(8,128)(2,1)} %bitcast.144), calls=%async_computation.5 | async-start | bytes 4194304 | tf_op jit(solution)/shard_map/all_to_all | solution.py:119
  214.8 15.2 %collective-permute-start.8 = (bf16[128,2048]{1,0:T(8,128)(2,1)S(1)}, bf16[128,2048]{1,0:T(8,128)(2,1)S(1)}, u32[]{:S(2)}, u32[]{:S(2)}) collective-permute-start(bf16[128,2048]{1,0:T(8,128)(2,1)S(1)} %convolution_convert_fusion.1), channel_id=1, source_target_pairs={{0,224},{1,33},{32,0},{33,65},{64,32},{65,97},{96,64},{97,129},{12... | collective-permute-start | bytes 1572872 | tf_op jit(solution)/shard_map/ppermute | solution.py:23
  225.6 10.0 %collective-permute-start.11 = (bf16[128,2048]{1,0:T(8,128)(2,1)S(1)}, bf16[128,2048]{1,0:T(8,128)(2,1)S(1)}, u32[]{:S(2)}, u32[]{:S(2)}) collective-permute-start(bf16[128,2048]{1,0:T(8,128)(2,1)S(1)} %add_convert_fusion.7), channel_id=1, source_target_pairs={{0,224},{1,33},{32,0},{33,65},{64,32},{65,97},{96,64},{97,129},{12... | collective-permute-start | bytes 1572872 | tf_op jit(solution)/shard_map/ppermute | solution.py:23
  230.5 10.8 %collective-permute-start.10 = (bf16[128,2048]{1,0:T(8,128)(2,1)S(1)}, bf16[128,2048]{1,0:T(8,128)(2,1)S(1)}, u32[]{:S(2)}, u32[]{:S(2)}) collective-permute-start(bf16[128,2048]{1,0:T(8,128)(2,1)S(1)} %add_convert_fusion.8), channel_id=1, source_target_pairs={{0,224},{1,33},{32,0},{33,65},{64,32},{65,97},{96,64},{97,129},{12... | collective-permute-start | bytes 1572872 | tf_op jit(solution)/shard_map/ppermute | solution.py:23
  236.0 10.8 %collective-permute-start.13 = (bf16[128,2048]{1,0:T(8,128)(2,1)S(1)}, bf16[128,2048]{1,0:T(8,128)(2,1)S(1)}, u32[]{:S(2)}, u32[]{:S(2)}) collective-permute-start(bf16[128,2048]{1,0:T(8,128)(2,1)S(1)} %add_convert_fusion.5), channel_id=1, source_target_pairs={{0,224},{1,33},{32,0},{33,65},{64,32},{65,97},{96,64},{97,129},{12... | collective-permute-start | bytes 1572872 | tf_op jit(solution)/shard_map/ppermute | solution.py:23
  241.7 10.4 %collective-permute-start.12 = (bf16[128,2048]{1,0:T(8,128)(2,1)S(1)}, bf16[128,2048]{1,0:T(8,128)(2,1)S(1)}, u32[]{:S(2)}, u32[]{:S(2)}) collective-permute-start(bf16[128,2048]{1,0:T(8,128)(2,1)S(1)} %add_convert_fusion.6), channel_id=1, source_target_pairs={{0,224},{1,33},{32,0},{33,65},{64,32},{65,97},{96,64},{97,129},{12... | collective-permute-start | bytes 1572872 | tf_op jit(solution)/shard_map/ppermute | solution.py:23
  247.3 10.4 %collective-permute-start.15 = (bf16[128,2048]{1,0:T(8,128)(2,1)S(1)}, bf16[128,2048]{1,0:T(8,128)(2,1)S(1)}, u32[]{:S(2)}, u32[]{:S(2)}) collective-permute-start(bf16[128,2048]{1,0:T(8,128)(2,1)S(1)} %add_convert_fusion.3), channel_id=1, source_target_pairs={{0,224},{1,33},{32,0},{33,65},{64,32},{65,97},{96,64},{97,129},{12... | collective-permute-start | bytes 1572872 | tf_op jit(solution)/shard_map/ppermute | solution.py:23
  252.5 13.4 %collective-permute-start.14 = (bf16[128,2048]{1,0:T(8,128)(2,1)S(1)}, bf16[128,2048]{1,0:T(8,128)(2,1)S(1)}, u32[]{:S(2)}, u32[]{:S(2)}) collective-permute-start(bf16[128,2048]{1,0:T(8,128)(2,1)S(1)} %add_convert_fusion.4), channel_id=1, source_target_pairs={{0,224},{1,33},{32,0},{33,65},{64,32},{65,97},{96,64},{97,129},{12... | collective-permute-start | bytes 1572872 | tf_op jit(solution)/shard_map/ppermute | solution.py:23
  257.8 8.1 %collective-permute-start.16 = (bf16[128,2048]{1,0:T(8,128)(2,1)S(1)}, bf16[128,2048]{1,0:T(8,128)(2,1)S(1)}, u32[]{:S(2)}, u32[]{:S(2)}) collective-permute-start(bf16[128,2048]{1,0:T(8,128)(2,1)S(1)} %add_convert_fusion.2), channel_id=1, source_target_pairs={{0,1},{1,0},{2,3},{3,2},{4,5},{5,4},{6,7},{7,6},{8,9},{9,8},{10,11... | collective-permute-start | bytes 1572872 | tf_op jit(solution)/shard_map/ppermute | solution.py:14
  (9 other events, 63.0 us)
